TPU v7x, 32 devices: a whole 2x2x4 slice. The times are simulated.
32 devices in a mesh: groups: 2 (over x), space: 16 (over z, y, core).
Axes of the slice: x: 2, y: 2, z: 4, core: 2. Of those that a mesh axis runs over, the one named last changes fastest.
Arguments:
- counts: int32 [1024, 65536], P('space', 'groups'), parts along dimension 1, may hold values from 0 to 7
- latent: float32 [32, 65536], P(None, ('groups', 'space')), parts along dimension 1, may hold values from -4 to 4
- loading: bfloat16 [32, 2048], P(None, ('groups', 'space')), parts along dimension 1, may hold values from 0.019897461 to 0.5
- background: float32 [2048], P(('groups', 'space')), parts along dimension 0, may hold values from 0.05 to 0.5
- coupling: float32 [64], P('groups'), parts along dimension 0, may hold values from 0.05 to 0.3
- tissue: int32 [65536], P('groups'), parts along dimension 0, may hold values 0 or 1
Outputs:
- grad_latent: float32 [32, 65536], P(None, ('groups', 'space')), parts along dimension 1
- grad_loading: float32 [32, 2048], P(None, ('groups', 'space')), parts along dimension 1
There are 2 independent parts, one for each index of `groups`. A program takes and returns all parts, laid end to end along the dimension named above; each array names one. Nothing has to cross between parts.
All inputs are finite; a program needn't handle non-finite values.
Results may differ from a plain program's by a relative error of at most 0.0018.
Values may be sent and summed in bfloat16 or wider, within the bound.
No kernel may reach another device: no remote copies, remote signals or barrier semaphores. Data moves between devices by JAX's collectives and lax.ppermute only.
A program may use at most 128 MiB of HBM per device.

v0:
```python
import jax
import jax.numpy as jnp
from jax import lax
from jax.sharding import PartitionSpec as P

GENES = 1024
ROW_SPOTS = 2048


def extended(cells, sides, width):
    for axis, dim in sides:
        count = lax.axis_size(axis)
        ends = count - 1
        head = lax.slice_in_dim(cells, 0, width, axis=dim)
        tail = lax.slice_in_dim(cells, cells.shape[dim] - width, cells.shape[dim], axis=dim)
        cells = jnp.concatenate(
            [
                lax.ppermute(tail, axis, [(i, (i + 1) % count) for i in range(ends)]),
                cells,
                lax.ppermute(head, axis, [((i + 1) % count, i) for i in range(ends)]),
            ],
            axis=dim,
        )
    return cells


def neighbours(values_in, padded):
    columns = values_in.shape[1]
    upper_row = padded[:, :columns]
    lower_row = padded[:, 2 * ROW_SPOTS :]
    column = lax.broadcasted_iota(jnp.int32, (1, columns), 1) % ROW_SPOTS
    zero_col = jnp.zeros((values_in.shape[0], 1), values_in.dtype)
    left_cell = jnp.where(column > 0, jnp.concatenate([zero_col, values_in[:, :-1]], axis=1), 0.0)
    right_cell = jnp.where(
        column < ROW_SPOTS - 1, jnp.concatenate([values_in[:, 1:], zero_col], axis=1), 0.0
    )
    return upper_row + lower_row + left_cell + right_cell


def local(counts, latent, loading, background, coupling, tissue):
    factor_count = latent.shape[0]
    spot_dev = latent.shape[1]
    total_spots = counts.shape[1]
    latent_pad = extended(latent, (("space", 1),), ROW_SPOTS)
    smoothed = latent + coupling[:, None] * (neighbours(latent, latent_pad) - 4.0 * latent)
    factors = jax.nn.softplus(smoothed).astype(jnp.bfloat16)
    weight_of = tissue.astype(jnp.float32)
    gathered = lax.all_gather(factors, "space", axis=1, tiled=True)
    expected = (
        lax.dot_general(
            loading, gathered, (((0,), (0,)), ((), ())), preferred_element_type=jnp.float32
        )
        + background[:, None]
    )
    observed = counts.astype(jnp.float32)
    residual = (weight_of[None, :] * (1.0 - observed / expected)).astype(jnp.bfloat16)
    load_sum = lax.dot_general(
        gathered, residual, (((1,), (1,)), ((), ())), preferred_element_type=jnp.float32
    )
    spot_sums = jnp.dot(loading, residual, preferred_element_type=jnp.float32)
    received = lax.all_to_all(
        spot_sums.astype(jnp.bfloat16), "space", split_axis=1, concat_axis=0, tiled=True
    ).astype(spot_sums.dtype)
    own_sum = jnp.sum(received.reshape(-1, factor_count, spot_dev), axis=0)
    grad_smooth = own_sum * jax.nn.sigmoid(smoothed) / GENES
    adjoint_pad = extended(grad_smooth, (("space", 1),), ROW_SPOTS)
    grad_latent = grad_smooth + coupling[:, None] * (
        neighbours(grad_smooth, adjoint_pad) - 4.0 * grad_smooth
    )
    grad_loading = load_sum / total_spots
    return (grad_latent, grad_loading)


def solution(mesh):
    placed = (
        P("space", "groups"),
        P(None, ("groups", "space")),
        P(None, ("groups", "space")),
        P(("groups", "space")),
        P("groups"),
        P("groups"),
    )
    return jax.shard_map(
        local,
        mesh=mesh,
        in_specs=placed,
        out_specs=(P(None, ("groups", "space")), P(None, ("groups", "space"))),
        check_vma=False,
    )
```

profile of v0, /device:TPU:12, one launch (start us, length us, event | category | flops | bytes accessed | tf_op | source)
XLA Modules:
  0.0 143.2 jit_solution(12022771995010914601)
XLA Ops:
  7.2 0.0 copy-start
  7.2 0.0 all-gather.2.cloned.1.call-start
  7.2 1.9 %collective-permute-start.1 = (f32[32,2048]{1,0:T(8,128)}, f32[32,2048]{1,0:T(8,128)S(1)}, u32[]{:S(2)}, u32[]{:S(2)}) collective-permute-start(f32[32,2048]{1,0:T(8,128)} %param.7), channel_id=1, source_target_pairs={{1,0},{2,1},{3,2},{4,3},{5,4},{6,5},{7,6},{8,7},{9,8},{10,9},{11,1... | collective-permute-start | bytes 786440 | tf_op jit(solution)/shard_map/ppermute | solution.py:20
  9.2 2.4 %collective-permute-start = (f32[32,2048]{1,0:T(8,128)}, f32[32,2048]{1,0:T(8,128)S(1)}, u32[]{:S(2)}, u32[]{:S(2)}) collective-permute-start(f32[32,2048]{1,0:T(8,128)} %param.7), channel_id=1, source_target_pairs={{0,1},{1,2},{2,3},{3,4},{4,5},{5,6},{6,7},{7,8},{8,9},{9,10},{10,1... | collective-permute-start | bytes 786440 | tf_op jit(solution)/shard_map/ppermute | solution.py:18
  11.6 1.2 fusion.12
  12.8 0.6 collective-permute-done.1
  13.3 5.5 %collective-permute-done = f32[32,2048]{1,0:T(8,128)S(1)} collective-permute-done((f32[32,2048]{1,0:T(8,128)}, f32[32,2048]{1,0:T(8,128)S(1)}, u32[]{:S(2)}, u32[]{:S(2)}) %collective-permute-start) | collective-permute-done | bytes 262176 | tf_op jit(solution)/shard_map/ppermute | solution.py:18
  18.8 1.9 %fusion.5 = (bf16[32,2048]{1,0:T(8,128)(2,1)}, f32[32,2048]{1,0:T(8,128)S(1)}) fusion(f32[32,2048]{1,0:T(8,128)} %param.7, f32[32,2047]{1,0:T(8,128)S(1)} %get-tuple-element.7, pred[2048]{0:T(1024)(128)(4,1)S(1)} %get-tuple-element.8, f32[32,2047]{1,0:T(8,128)S(1)} %get-tuple-element.6, pred[2048]{0:T(1024)(128)(4,1)S(1)} %get-tuple-element.9, ...), kind=kLoop, calls=%fused_computation.11 | loop fusion | flops 1048576 | bytes 1707904 | tf_op jit(solution)/shard_map/convert_element_type | solution.py:46
  20.8 0.0 all-gather.2.cloned.1.call-update
  20.8 0.9 convert_element_type.23
  21.7 38.9 %all-gather.2.cloned.1.call-done = bf16[32,32768]{1,0:T(8,128)(2,1)} async-done(((bf16[32,2048]{1,0:T(8,128)(2,1)}), bf16[32,32768]{1,0:T(8,128)(2,1)}) %all-gather.2.cloned.1.call-update) | async-done | bytes 2097168 | tf_op jit(solution)/shard_map/all_gather | solution.py:48
  60.6 0.0 copy-done
  60.6 6.7 %fusion.4 = bf16[64,32768]{1,0:T(8,128)(2,1)S(1)} fusion(bf16[32,32768]{1,0:T(8,128)(2,1)} %all-gather.2.cloned.1.call-done, bf16[32,64]{1,0:T(8,128)(2,1)S(1)} %copy-done, s32[64,32768]{1,0:T(8,128)} %param.6, f32[64]{0:T(128)} %param.9, f32[32768]{0:T(1024)S(1)} %convert_element_type.23), kind=kOutput, calls=%fused_computation.6 | convolution fusion | flops 146800640 | bytes 14815488 | tf_op jit(solution)/shard_map/dot_general | solution.py:50
  67.3 0.0 copy-start.1
  67.3 0.7 convolution_convert_fusion
  68.0 1.9 %copy.11 = bf16[4,16,8,2048]{3,2,0,1:T(8,128)(2,1)} copy(bf16[4,16,8,2048]{3,2,1,0:T(8,128)(2,1)S(1)} %bitcast.22) | data formatting | bytes 4194304 | tf_op jit(solution)/shard_map/all_to_all | solution.py:61
  69.9 0.0 copy-done.1
  69.9 6.0 %all-to-all-start = ((bf16[32,16,2048]{2,0,1:T(8,128)(2,1)}), bf16[32,16,2048]{2,0,1:T(8,128)(2,1)S(1)}, u32[]{:S(2)}, u32[]{:S(2)}) async-start(bf16[32,16,2048]{2,0,1:T(8,128)(2,1)} %bitcast.21), calls=%async_computation | async-start | bytes 4194304 | tf_op jit(solution)/shard_map/all_to_all | solution.py:61
  75.8 0.0 copy-start.2
  75.8 4.7 %convolution_multiply_fusion = f32[32,64]{1,0:T(8,128)} fusion(bf16[32,32768]{1,0:T(8,128)(2,1)} %all-gather.2.cloned.1.call-done, bf16[64,32768]{1,0:T(8,128)(2,1)} %copy-done.1), kind=kOutput, calls=%fused_computation.9 | convolution fusion | flops 134219776 | bytes 6299648 | tf_op jit(solution)/shard_map/dot_general | solution.py:57
  80.5 42.6 %all-to-all-done = bf16[32,16,2048]{2,0,1:T(8,128)(2,1)S(1)} async-done(((bf16[32,16,2048]{2,0,1:T(8,128)(2,1)}), bf16[32,16,2048]{2,0,1:T(8,128)(2,1)S(1)}, u32[]{:S(2)}, u32[]{:S(2)}) %all-to-all-start) | async-done | bytes 2097184 | tf_op jit(solution)/shard_map/all_to_all | solution.py:61
  123.1 0.4 convert_reduce_fusion
  123.5 0.1 broadcast_multiply_fusion
  123.6 1.9 %collective-permute-start.3 = (f32[32,2048]{1,0:T(8,128)S(1)}, f32[32,2048]{1,0:T(8,128)S(1)}, u32[]{:S(2)}, u32[]{:S(2)}) collective-permute-start(f32[32,2048]{1,0:T(8,128)S(1)} %broadcast_multiply_fusion), channel_id=1, source_target_pairs={{1,0},{2,1},{3,2},{4,3},{5,4},{6,5},{7,6},{8,7},{9,8},{10,9},{11,1... | collective-permute-start | bytes 786440 | tf_op jit(solution)/shard_map/ppermute | solution.py:20
  125.5 2.4 %collective-permute-start.2 = (f32[32,2048]{1,0:T(8,128)S(1)}, f32[32,2048]{1,0:T(8,128)S(1)}, u32[]{:S(2)}, u32[]{:S(2)}) collective-permute-start(f32[32,2048]{1,0:T(8,128)S(1)} %broadcast_multiply_fusion), channel_id=1, source_target_pairs={{0,1},{1,2},{2,3},{3,4},{4,5},{5,6},{6,7},{7,8},{8,9},{9,10},{10,1... | collective-permute-start | bytes 786440 | tf_op jit(solution)/shard_map/ppermute | solution.py:18
  127.9 0.1 fusion.11
  128.1 4.1 %collective-permute-done.3 = f32[32,2048]{1,0:T(8,128)S(1)} collective-permute-done((f32[32,2048]{1,0:T(8,128)S(1)}, f32[32,2048]{1,0:T(8,128)S(1)}, u32[]{:S(2)}, u32[]{:S(2)}) %collective-permute-start.3) | collective-permute-done | bytes 262176 | tf_op jit(solution)/shard_map/ppermute | solution.py:20
  132.2 3.3 %collective-permute-done.2 = f32[32,2048]{1,0:T(8,128)S(1)} collective-permute-done((f32[32,2048]{1,0:T(8,128)S(1)}, f32[32,2048]{1,0:T(8,128)S(1)}, u32[]{:S(2)}, u32[]{:S(2)}) %collective-permute-start.2) | collective-permute-done | bytes 262176 | tf_op jit(solution)/shard_map/ppermute | solution.py:18
  135.5 0.0 copy-done.2
  135.5 0.9 multiply_add_fusion
  (1 shorter events, 0.0 us)
Async XLA Ops:
  7.2 53.4 %copy-start = (bf16[32,64]{1,0:T(8,128)(2,1)S(1)}, bf16[32,64]{1,0:T(8,128)(2,1)}, u32[]{:S(2)}) copy-start(bf16[32,64]{1,0:T(8,128)(2,1)} %param.8) | copy-start | bytes 12292
  7.2 53.4 %all-gather.2.cloned.1.call-start = ((), (), s32[]{:S(2)}) async-start(), calls=%async_computation.1 | async-start | bytes 2228224 | tf_op jit(solution)/shard_map/all_gather | solution.py:48
  7.2 6.1 %collective-permute-start.1 = (f32[32,2048]{1,0:T(8,128)}, f32[32,2048]{1,0:T(8,128)S(1)}, u32[]{:S(2)}, u32[]{:S(2)}) collective-permute-start(f32[32,2048]{1,0:T(8,128)} %param.7), channel_id=1, source_target_pairs={{1,0},{2,1},{3,2},{4,3},{5,4},{6,5},{7,6},{8,7},{9,8},{10,9},{11,1... | collective-permute-start | bytes 786440 | tf_op jit(solution)/shard_map/ppermute | solution.py:20
  9.2 9.7 %collective-permute-start = (f32[32,2048]{1,0:T(8,128)}, f32[32,2048]{1,0:T(8,128)S(1)}, u32[]{:S(2)}, u32[]{:S(2)}) collective-permute-start(f32[32,2048]{1,0:T(8,128)} %param.7), channel_id=1, source_target_pairs={{0,1},{1,2},{2,3},{3,4},{4,5},{5,6},{6,7},{7,8},{8,9},{9,10},{10,1... | collective-permute-start | bytes 786440 | tf_op jit(solution)/shard_map/ppermute | solution.py:18
  67.3 2.6 %copy-start.1 = (bf16[64,32768]{1,0:T(8,128)(2,1)}, bf16[64,32768]{1,0:T(8,128)(2,1)S(1)}, u32[]{:S(2)}) copy-start(bf16[64,32768]{1,0:T(8,128)(2,1)S(1)} %fusion.4) | copy-start | bytes 12582916
  69.9 53.2 %all-to-all-start = ((bf16[32,16,2048]{2,0,1:T(8,128)(2,1)}), bf16[32,16,2048]{2,0,1:T(8,128)(2,1)S(1)}, u32[]{:S(2)}, u32[]{:S(2)}) async-start(bf16[32,16,2048]{2,0,1:T(8,128)(2,1)} %bitcast.21), calls=%async_computation | async-start | bytes 4194304 | tf_op jit(solution)/shard_map/all_to_all | solution.py:61
  75.8 59.6 %copy-start.2 = (f32[32]{0:T(128)S(1)}, f32[32]{0:T(128)}, u32[]{:S(2)}) copy-start(f32[32]{0:T(128)} %param.10) | copy-start | bytes 388
  123.6 8.6 %collective-permute-start.3 = (f32[32,2048]{1,0:T(8,128)S(1)}, f32[32,2048]{1,0:T(8,128)S(1)}, u32[]{:S(2)}, u32[]{:S(2)}) collective-permute-start(f32[32,2048]{1,0:T(8,128)S(1)} %broadcast_multiply_fusion), channel_id=1, source_target_pairs={{1,0},{2,1},{3,2},{4,3},{5,4},{6,5},{7,6},{8,7},{9,8},{10,9},{11,1... | collective-permute-start | bytes 786440 | tf_op jit(solution)/shard_map/ppermute | solution.py:20
  125.5 9.9 %collective-permute-start.2 = (f32[32,2048]{1,0:T(8,128)S(1)}, f32[32,2048]{1,0:T(8,128)S(1)}, u32[]{:S(2)}, u32[]{:S(2)}) collective-permute-start(f32[32,2048]{1,0:T(8,128)S(1)} %broadcast_multiply_fusion), channel_id=1, source_target_pairs={{0,1},{1,2},{2,3},{3,4},{4,5},{5,6},{6,7},{7,8},{8,9},{9,10},{10,1... | collective-permute-start | bytes 786440 | tf_op jit(solution)/shard_map/ppermute | solution.py:18
Sparse Core Ops, SparseCore 0:
  20.9 39.6 all-gather.1
where the time goes:
time: 144 us; the launch traced here: 143 us
  waiting for transfers between devices  95 us (66%)
  starting transfers between devices  14.6 us (10%)
  between operations  14.1 us (10%)
  matrix products  12 us (8%)
  other arithmetic  4.21 us (3%)
  local copies, waits for them, and re-layouts  3.23 us (2%)
    all_to_all x1, waiting for transfers between devices, local(): lax.all_to_all(spot_sums.astype(jnp.bfloat16), 'space', split_axis=1, con...  42.6 us
    all_gather x1, waiting for transfers between devices, local(): gathered = lax.all_gather(factors, 'space', axis=1, tiled=True)  38.9 us
    ppermute x2, waiting for transfers between devices, extended(): lax.ppermute(tail, axis, [(i, (i + 1) % count) for i in range(ends)])  8.78 us
    dot_general x1, matrix products, local(): lax.dot_general(loading, gathered, (((0,), (0,)), ((), ())), preferred_el...  6.66 us
    all_to_all x1, starting transfers between devices, local(): lax.all_to_all(spot_sums.astype(jnp.bfloat16), 'space', split_axis=1, con...  5.95 us
    ppermute x2, starting transfers between devices, extended(): lax.ppermute(tail, axis, [(i, (i + 1) % count) for i in range(ends)])  4.81 us
    ppermute x2, waiting for transfers between devices, extended(): lax.ppermute(head, axis, [((i + 1) % count, i) for i in range(ends)])  4.68 us
    dot_general x1, matrix products, local(): lax.dot_general(gathered, residual, (((1,), (1,)), ((), ())), preferred_e...  4.65 us
  transfers between devices with their start and end apart: 6, of which 6 were waited for; matrix products, arithmetic and copies ran while one was open for 5% of the time, Pallas kernels for 0%

commit v1 on v0

v1 whole, which is shorter than its diff:
```python
import functools

import jax
import jax.numpy as jnp
from jax import lax
from jax.experimental import pallas as pl
from jax.experimental.pallas import tpu as pltpu
from jax.sharding import PartitionSpec as P

SPACE = "space"
MIB = 1024 * 1024
VMEM = pl.BlockSpec(memory_space=pltpu.VMEM)


def params(mib):
    return pltpu.CompilerParams(vmem_limit_bytes=mib * MIB)


def cost(flops, nbytes, trans=0):
    return pl.CostEstimate(flops=flops, bytes_accessed=nbytes, transcendentals=trans)


def split_kernel(place, counts_ref, keep_ref, send_ref, *, width):
    core = place[0]
    mine = pl.multiple_of(core * width, width)
    other = pl.multiple_of((1 - core) * width, width)
    keep_ref[0, 0] = counts_ref[:, pl.ds(mine, width)].astype(jnp.float32).astype(jnp.bfloat16)
    send_ref[0, 0] = counts_ref[:, pl.ds(other, width)].astype(jnp.float32).astype(jnp.bfloat16)


def split_counts(counts, core, row, planes, width):
    genes = counts.shape[0]
    half = jax.ShapeDtypeStruct((planes, 2, genes, width), jnp.bfloat16)
    block = pl.BlockSpec((1, 1, genes, width), lambda i, j, p: (i, lax.rem(j + p[1], 2), 0, 0))
    return pl.pallas_call(
        functools.partial(split_kernel, width=width),
        grid_spec=pltpu.PrefetchScalarGridSpec(
            num_scalar_prefetch=1,
            grid=(planes, 2),
            in_specs=[pl.BlockSpec((genes, 2 * width), lambda i, j, p: (0, 2 * i + j))],
            out_specs=[block, block],
        ),
        out_shape=[half, half],
        compiler_params=params(12),
        cost_estimate=cost(counts.size, counts.size * 6),
    )(jnp.stack([core, row]), counts)


def stencil(values, upper, lower, strength):
    width = values.shape[1]
    column = lax.broadcasted_iota(jnp.int32, values.shape, 1)
    left = jnp.where(column > 0, pltpu.roll(values, 1, 1), 0.0)
    right = jnp.where(column < width - 1, pltpu.roll(values, width - 1, 1), 0.0)
    return values + strength * (upper + lower + left + right - 4.0 * values)


def factor_kernel(latent_ref, up_ref, down_ref, strength_ref, tissue_ref, factor_ref, slope_ref, *, scale):
    smoothed = stencil(latent_ref[...], up_ref[...], down_ref[...], strength_ref[...])
    small = jnp.exp(-jnp.abs(smoothed))
    inside = tissue_ref[...] > 0
    soft = jnp.maximum(smoothed, 0.0) + jnp.log1p(small)
    factor_ref[...] = jnp.where(inside, soft, 0.0).astype(jnp.bfloat16)
    sigmoid = jnp.where(smoothed >= 0.0, 1.0, small) / (1.0 + small)
    slope_ref[...] = jnp.where(inside, sigmoid * scale, 0.0)


def gene_kernel(place, own_f, other_f, keep_ref, came_ref, weight_ref, turned_ref, back_ref, own_p, other_p, load_p, *, step):
    genes = keep_ref.shape[2]
    width = own_f.shape[1]
    weights, turned = weight_ref[...], turned_ref[...]
    offset = jnp.concatenate([back_ref[...]] * (step // 128), axis=1)
    load = jnp.zeros(load_p.shape, jnp.float32)
    for half, (field, out) in enumerate(((own_f, own_p), (other_f, other_p))):
        for at in range(0, width, step):
            f = field[:, at : at + step]
            rate = jnp.dot(turned, f, preferred_element_type=jnp.float32) + offset
            seen = jnp.concatenate(
                [keep_ref[0, half, :, at : at + step], came_ref[0, half, :, at : at + step]], axis=0
            ).astype(jnp.float32)
            residual = (1.0 - seen / rate).astype(jnp.bfloat16)
            out[:, at : at + step] = jnp.dot(weights, residual, preferred_element_type=jnp.float32).astype(out.dtype)
            load += lax.dot_general(f, residual, (((1,), (1,)), ((), ())), preferred_element_type=jnp.float32)
    load_p[...] = load


def gene_sums(plane, own_f, other_f, keep, came, weights, turned, back):
    factors, width = own_f.shape
    genes = keep.shape[2]
    whole = lambda shape: pl.BlockSpec(shape, lambda i, p: (0,) * len(shape))
    part = pl.BlockSpec((1, 2, genes, width), lambda i, p: (p[0], 0, 0, 0))
    work = 2 * genes * 2 * width
    return pl.pallas_call(
        functools.partial(gene_kernel, step=512),
        grid_spec=pltpu.PrefetchScalarGridSpec(
            num_scalar_prefetch=1,
            grid=(1,),
            in_specs=[
                whole(own_f.shape), whole(own_f.shape), part, part,
                whole(weights.shape), whole(turned.shape), whole(back.shape),
            ],
            out_specs=[whole(own_f.shape), whole(own_f.shape), whole((factors, 2 * genes))],
        ),
        out_shape=[
            jax.ShapeDtypeStruct(own_f.shape, jnp.float32),
            jax.ShapeDtypeStruct(own_f.shape, jnp.bfloat16),
            jax.ShapeDtypeStruct((factors, 2 * genes), jnp.float32),
        ],
        compiler_params=params(12),
        cost_estimate=cost(6 * factors * work, 3 * work, work),
    )(plane.reshape(1), own_f, other_f, keep, came, weights, turned, back)


def last_kernel(own_ref, up_ref, down_ref, strength_ref, out_ref):
    out_ref[...] = stencil(
        own_ref[...], up_ref[...].astype(jnp.float32), down_ref[...].astype(jnp.float32), strength_ref[...]
    )


def local(counts, latent, loading, background, coupling, tissue):
    factors, width = latent.shape
    genes, total_spots = counts.shape
    count = lax.axis_size(SPACE)
    planes = count // 4
    me = lax.axis_index(SPACE)
    core, row, plane = lax.rem(me, 2), lax.rem(me // 2, 2), me // 4

    def send(x, to):
        return lax.ppermute(x, SPACE, [(i, to(i)) for i in range(count)])

    def halo(x):
        return (
            lax.ppermute(x, SPACE, [(i, i + 1) for i in range(count - 1)]),
            lax.ppermute(x, SPACE, [(i + 1, i) for i in range(count - 1)]),
        )

    over_core = lambda i: i ^ 1
    over_row = lambda i: i ^ 2
    along = lambda s: lambda i: (i + 4 * s) % count

    up, down = halo(latent)
    both = jnp.concatenate([loading.astype(jnp.float32), background[None], jnp.zeros((7, genes), jnp.float32)])
    both = jnp.concatenate([both, send(both, over_core)], axis=1)
    weights = both[:factors].astype(jnp.bfloat16)
    turned = weights.T
    back = jnp.broadcast_to(both[factors][:, None], (2 * genes, 128))

    keep, away = split_counts(counts, core, row, planes, width)
    came = send(away, over_core)

    inside = lax.dynamic_slice(tissue, (me * width,), (width,)).reshape(1, width)
    strength = coupling.reshape(factors, 1)
    field, slope = pl.pallas_call(
        functools.partial(factor_kernel, scale=1.0 / (genes * count)),
        in_specs=[VMEM] * 5,
        out_specs=[VMEM] * 2,
        out_shape=[jax.ShapeDtypeStruct(latent.shape, jnp.bfloat16), jax.ShapeDtypeStruct(latent.shape, jnp.float32)],
        compiler_params=params(8),
        cost_estimate=cost(latent.size * 20, latent.size * 18, latent.size * 3),
    )(latent, up, down, strength, inside)

    order = sorted(range(planes), key=lambda s: min(s, planes - s))
    fields = {s: field if s == 0 else send(field, along(s)) for s in order}
    others = {s: send(fields[s], over_row) for s in order}
    total = None
    loads = None
    returned = []
    for s in order:
        source = lax.rem(plane - s + planes, planes)
        own_p, other_p, load = gene_sums(source, fields[s], others[s], keep, came, weights, turned, back)
        summed = own_p + send(other_p, over_row).astype(jnp.float32)
        loads = load if loads is None else loads + load
        if s == 0:
            total = summed
        else:
            returned.append(send(summed.astype(jnp.bfloat16), along(-s)))
    for r in returned:
        total = total + r.astype(jnp.float32)
    grad_smooth = total * slope
    up2, down2 = halo(grad_smooth.astype(jnp.bfloat16))
    grad_latent = pl.pallas_call(
        last_kernel,
        in_specs=[VMEM] * 4,
        out_specs=VMEM,
        out_shape=jax.ShapeDtypeStruct(latent.shape, jnp.float32),
        compiler_params=params(8),
        cost_estimate=cost(latent.size * 10, latent.size * 12),
    )(grad_smooth, up2, down2, strength)
    swapped = send(loads[:, genes:], over_core)
    grad_loading = (loads[:, :genes] + swapped) / total_spots
    return grad_latent, grad_loading


def solution(mesh):
    split = P(None, ("groups", SPACE))
    return jax.shard_map(
        local,
        mesh=mesh,
        in_specs=(P(SPACE, "groups"), split, split, P(("groups", SPACE)), P("groups"), P("groups")),
        out_specs=(split, split),
        check_vma=False,
    )
```

time: 144 us -> 82.4 us (0.57)
  the two profiles are of different devices: /device:TPU:12 before, /device:TPU:1 now
where the time goes in v1:
time: 82.4 us; the launch traced here: 81.9 us
  starting transfers between devices  30.4 us (37%)
  waiting for transfers between devices  23.8 us (29%)
  Pallas kernels  17.4 us (21%)
  local copies, waits for them, and re-layouts  7.57 us (9%)
  other arithmetic  1.96 us (2%)
    ppermute x17, starting transfers between devices, send(): return lax.ppermute(x, SPACE, [(i, to(i)) for i in range(count)])  18.2 us
    ppermute x17, waiting for transfers between devices, send(): return lax.ppermute(x, SPACE, [(i, to(i)) for i in range(count)])  15.1 us
    pallas_call x4, Pallas kernels, gene_sums(): pl.pallas_call(functools.partial(gene_kernel, step=512), grid_spec=pltpu....  11.9 us
    ppermute x2, starting transfers between devices, halo(): lax.ppermute(x, SPACE, [(i, i + 1) for i in range(count - 1)])  8.36 us
    ppermute x2, waiting for transfers between devices, halo(): lax.ppermute(x, SPACE, [(i + 1, i) for i in range(count - 1)])  8.13 us
    unnamed x19, local copies, waits for them, and re-layouts  6.63 us
    pallas_call x1, Pallas kernels, split_counts(): pl.pallas_call(functools.partial(split_kernel, width=width), grid_spec=pl...  4.06 us
    ppermute x2, starting transfers between devices, halo(): lax.ppermute(x, SPACE, [(i + 1, i) for i in range(count - 1)])  3.84 us
  transfers between devices with their start and end apart: 21, of which 8 were waited for; matrix products, arithmetic and copies ran while one was open for 4% of the time, Pallas kernels for 15%

profile of v1, /device:TPU:1, one launch (start us, length us, event | category | flops | bytes accessed | tf_op | source)
XLA Modules:
  0.0 81.9 jit_solution(5138616618948749772)
XLA Ops:
  0.6 0.1 pad_add_fusion.place
  0.7 3.4 %copy-done = s32[64,32768]{1,0:T(8,128)S(1)} copy-done((s32[64,32768]{1,0:T(8,128)S(1)}, s32[64,32768]{1,0:T(8,128)}, u32[]{:S(2)}) %copy-start) | copy-done | bytes 8388632
  4.1 4.1 %shard_map.78 = (bf16[4,2,64,2048]{3,2,1,0:T(8,128)(2,1)S(1)}, bf16[4,2,64,2048]{3,2,1,0:T(8,128)(2,1)}) custom-call(s32[2]{0:T(128)S(1)} %pad_add_fusion.place, s32[64,32768]{1,0:T(8,128)S(1)} %copy-done), custom_call_target="tpu_custom_call" | custom-call | flops 2097152 | bytes 12582912 | tf_op jit(solution)/shard_map/pallas_call | solution.py:35
  8.2 0.1 collective-permute-start.3
  8.2 4.5 %collective-permute-start = (f32[32,2048]{1,0:T(8,128)S(1)}, f32[32,2048]{1,0:T(8,128)S(1)}, u32[]{:S(2)}, u32[]{:S(2)}) collective-permute-start(f32[32,2048]{1,0:T(8,128)S(1)} %copy-done.1), channel_id=1, source_target_pairs={{0,1},{1,2},{2,3},{3,4},{4,5},{5,6},{6,7},{7,8},{8,9},{9,10},{10,1... | collective-permute-start | bytes 786440 | tf_op jit(solution)/shard_map/ppermute | solution.py:132
  12.7 1.9 %collective-permute-start.1 = (f32[32,2048]{1,0:T(8,128)S(1)}, f32[32,2048]{1,0:T(8,128)S(1)}, u32[]{:S(2)}, u32[]{:S(2)}) collective-permute-start(f32[32,2048]{1,0:T(8,128)S(1)} %copy-done.1), channel_id=1, source_target_pairs={{1,0},{2,1},{3,2},{4,3},{5,4},{6,5},{7,6},{8,7},{9,8},{10,9},{11,1... | collective-permute-start | bytes 786440 | tf_op jit(solution)/shard_map/ppermute | solution.py:133
  14.7 0.1 copy.31.strength_ref
  14.8 0.7 dynamic_slice.3
  15.5 0.6 collective-permute-done.up_ref
  16.0 4.4 %collective-permute-done.1.down_ref = f32[32,2048]{1,0:T(8,128)S(1)} collective-permute-done((f32[32,2048]{1,0:T(8,128)S(1)}, f32[32,2048]{1,0:T(8,128)S(1)}, u32[]{:S(2)}, u32[]{:S(2)}) %collective-permute-start.1) | collective-permute-done | bytes 262176 | tf_op jit(solution)/shard_map/ppermute | solution.py:133
  20.4 0.5 shard_map.77
  20.9 1.3 %collective-permute-start.6 = (bf16[32,2048]{1,0:T(8,128)(2,1)S(1)}, bf16[32,2048]{1,0:T(8,128)(2,1)S(1)}, u32[]{:S(2)}, u32[]{:S(2)}) collective-permute-start(bf16[32,2048]{1,0:T(8,128)(2,1)S(1)} %get-tuple-element.18.own_f), channel_id=1, source_target_pairs={{0,4},{1,5},{2,6},{3,7},{4,8},{5,9},{6,10},{7,11},{8,12},{9,13},{1... | collective-permute-start | bytes 393224 | tf_op jit(solution)/shard_map/ppermute | solution.py:128
  22.3 2.1 %collective-permute-start.10 = (bf16[32,2048]{1,0:T(8,128)(2,1)S(1)}, bf16[32,2048]{1,0:T(8,128)(2,1)S(1)}, u32[]{:S(2)}, u32[]{:S(2)}) collective-permute-start(bf16[32,2048]{1,0:T(8,128)(2,1)S(1)} %get-tuple-element.18.own_f), channel_id=1, source_target_pairs={{0,12},{1,13},{2,14},{3,15},{4,0},{5,1},{6,2},{7,3},{8,4},{9,5},{1... | collective-permute-start | bytes 393224 | tf_op jit(solution)/shard_map/ppermute | solution.py:128
  24.4 0.1 collective-permute-start.4
  24.5 0.5 collective-permute-start.14
  25.0 3.1 %collective-permute-done.6.own_f = bf16[32,2048]{1,0:T(8,128)(2,1)S(1)} collective-permute-done((bf16[32,2048]{1,0:T(8,128)(2,1)S(1)}, bf16[32,2048]{1,0:T(8,128)(2,1)S(1)}, u32[]{:S(2)}, u32[]{:S(2)}) %collective-permute-start.6) | collective-permute-done | bytes 131104 | tf_op jit(solution)/shard_map/ppermute | solution.py:128
  28.1 1.9 %collective-permute-start.7 = (bf16[32,2048]{1,0:T(8,128)(2,1)S(1)}, bf16[32,2048]{1,0:T(8,128)(2,1)S(1)}, u32[]{:S(2)}, u32[]{:S(2)}) collective-permute-start(bf16[32,2048]{1,0:T(8,128)(2,1)S(1)} %collective-permute-done.6.own_f), channel_id=1, source_target_pairs={{0,2},{1,3},{2,0},{3,1},{4,6},{5,7},{6,4},{7,5},{8,10},{9,11},{10,... | collective-permute-start | bytes 393224 | tf_op jit(solution)/shard_map/ppermute | solution.py:128
  30.0 0.0 collective-permute-done.4
  30.0 0.1 pad_maximum_fusion.1
  30.1 0.0 collective-permute-start.2
  30.1 0.1 collective-permute-done.10.own_f
  30.2 1.3 %collective-permute-start.11 = (bf16[32,2048]{1,0:T(8,128)(2,1)S(1)}, bf16[32,2048]{1,0:T(8,128)(2,1)}, u32[]{:S(2)}, u32[]{:S(2)}) collective-permute-start(bf16[32,2048]{1,0:T(8,128)(2,1)S(1)} %collective-permute-done.10.own_f), channel_id=1, source_target_pairs={{0,2},{1,3},{2,0},{3,1},{4,6},{5,7},{6,4},{7,5},{8,10},{9,11},{10,... | collective-permute-start | bytes 393224 | tf_op jit(solution)/shard_map/ppermute | solution.py:128
  31.6 0.1 maximum_bitcast_fusion
  31.6 0.1 copy.38
  31.8 4.7 %collective-permute-done.14.own_f = bf16[32,2048]{1,0:T(8,128)(2,1)S(1)} collective-permute-done((bf16[32,2048]{1,0:T(8,128)(2,1)S(1)}, bf16[32,2048]{1,0:T(8,128)(2,1)S(1)}, u32[]{:S(2)}, u32[]{:S(2)}) %collective-permute-start.14) | collective-permute-done | bytes 131104 | tf_op jit(solution)/shard_map/ppermute | solution.py:128
  36.5 0.3 collective-permute-start.15
  36.8 0.0 collective-permute-done.7.other_f
  36.8 0.7 copy-done.4
  37.5 0.0 collective-permute-done.3.came_ref
  37.5 0.1 broadcast_in_dim.16.back_ref
  37.6 0.9 %copy-done.5 = bf16[32,2048]{1,0:T(8,128)(2,1)S(1)} copy-done((bf16[32,2048]{1,0:T(8,128)(2,1)S(1)}, bf16[32,2048]{1,0:T(8,128)(2,1)}, u32[]{:S(2)}) %copy-start.5) | copy-done | bytes 131096
  38.5 3.4 %shard_map.80 = (f32[32,2048]{1,0:T(8,128)S(1)}, bf16[32,2048]{1,0:T(8,128)(2,1)}, f32[32,128]{1,0:T(8,128)S(1)}) custom-call(s32[1]{0:T(128)} %bitcast.8.place, bf16[32,2048]{1,0:T(8,128)(2,1)S(1)} %collective-permute-done.6.own_f, bf16[32,2048]{1,0:T(8,128)(2,1)S(1)} %copy-done.5, bf16[4,2,64,2048]{3,2,1,0:T(8,128)(2,1)S(1)} %get-tuple-element.19.keep_ref, ...), custom_call_target="tpu_custom_call" | custom-call | flops 100663296 | bytes 1572864 | tf_op jit(solution)/shard_map/pallas_call | solution.py:92
  41.9 1.1 %collective-permute-start.8 = (bf16[32,2048]{1,0:T(8,128)(2,1)}, bf16[32,2048]{1,0:T(8,128)(2,1)}, u32[]{:S(2)}, u32[]{:S(2)}) collective-permute-start(bf16[32,2048]{1,0:T(8,128)(2,1)} %get-tuple-element.24), channel_id=1, source_target_pairs={{0,2},{1,3},{2,0},{3,1},{4,6},{5,7},{6,4},{7,5},{8,10},{9,11},{10,... | collective-permute-start | bytes 393224 | tf_op jit(solution)/shard_map/ppermute | solution.py:128
  43.0 0.0 collective-permute-done.2.other_f
  43.0 0.6 copy-done.2
  43.7 0.9 %copy-done.3 = bf16[32,2048]{1,0:T(8,128)(2,1)S(1)} copy-done((bf16[32,2048]{1,0:T(8,128)(2,1)S(1)}, bf16[32,2048]{1,0:T(8,128)(2,1)}, u32[]{:S(2)}) %copy-start.3) | copy-done | bytes 131096
  44.6 2.8 %shard_map.79 = (f32[32,2048]{1,0:T(8,128)S(1)}, bf16[32,2048]{1,0:T(8,128)(2,1)S(1)}, f32[32,128]{1,0:T(8,128)S(1)}) custom-call(s32[1]{0:T(128)} %bitcast.place, bf16[32,2048]{1,0:T(8,128)(2,1)S(1)} %get-tuple-element.18.own_f, bf16[32,2048]{1,0:T(8,128)(2,1)S(1)} %copy-done.3, bf16[4,2,64,2048]{3,2,1,0:T(8,128)(2,1)S(1)} %get-tuple-element.19.keep_ref, ...), custom_call_target="tpu_custom_call" | custom-call | flops 100663296 | bytes 1572864 | tf_op jit(solution)/shard_map/pallas_call | solution.py:92
  47.4 0.4 collective-permute-start.5
  47.8 0.0 collective-permute-done.11.other_f
  47.8 2.9 %shard_map.81 = (f32[32,2048]{1,0:T(8,128)S(1)}, bf16[32,2048]{1,0:T(8,128)(2,1)S(1)}, f32[32,128]{1,0:T(8,128)S(1)}) custom-call(s32[1]{0:T(128)} %bitcast.9.place, bf16[32,2048]{1,0:T(8,128)(2,1)S(1)} %collective-permute-done.10.own_f, bf16[32,2048]{1,0:T(8,128)(2,1)} %collective-permute-done.11.other_f, ...), custom_call_target="tpu_custom_call" | custom-call | flops 100663296 | bytes 1572864 | tf_op jit(solution)/shard_map/pallas_call | solution.py:92
  50.6 1.2 %collective-permute-start.12 = (bf16[32,2048]{1,0:T(8,128)(2,1)S(1)}, bf16[32,2048]{1,0:T(8,128)(2,1)S(1)}, u32[]{:S(2)}, u32[]{:S(2)}) collective-permute-start(bf16[32,2048]{1,0:T(8,128)(2,1)S(1)} %get-tuple-element.26), channel_id=1, source_target_pairs={{0,2},{1,3},{2,0},{3,1},{4,6},{5,7},{6,4},{7,5},{8,10},{9,11},{10,... | collective-permute-start | bytes 393224 | tf_op jit(solution)/shard_map/ppermute | solution.py:128
  51.8 0.0 collective-permute-done.15.other_f
  51.8 2.8 %shard_map.82 = (f32[32,2048]{1,0:T(8,128)S(1)}, bf16[32,2048]{1,0:T(8,128)(2,1)S(1)}, f32[32,128]{1,0:T(8,128)S(1)}) custom-call(s32[1]{0:T(128)} %bitcast.10.place, bf16[32,2048]{1,0:T(8,128)(2,1)S(1)} %collective-permute-done.14.own_f, bf16[32,2048]{1,0:T(8,128)(2,1)S(1)} %collective-permute-done.15.other_f, ...), custom_call_target="tpu_custom_call" | custom-call | flops 100663296 | bytes 1572864 | tf_op jit(solution)/shard_map/pallas_call | solution.py:92
  54.6 0.4 collective-permute-start.16
  55.0 0.0 collective-permute-done.8
  55.0 0.9 %add_convert_fusion.2 = bf16[32,2048]{1,0:T(8,128)(2,1)S(1)} fusion(f32[32,2048]{1,0:T(8,128)S(1)} %get-tuple-element.23, bf16[32,2048]{1,0:T(8,128)(2,1)} %collective-permute-done.8), kind=kLoop, calls=%fused_computation.3 | loop fusion | flops 196608 | bytes 524288 | tf_op jit(solution)/shard_map/convert_element_type | solution.py:175
  55.9 2.0 %collective-permute-start.9 = (bf16[32,2048]{1,0:T(8,128)(2,1)S(1)}, bf16[32,2048]{1,0:T(8,128)(2,1)S(1)}, u32[]{:S(2)}, u32[]{:S(2)}) collective-permute-start(bf16[32,2048]{1,0:T(8,128)(2,1)S(1)} %add_convert_fusion.2), channel_id=1, source_target_pairs={{0,12},{1,13},{2,14},{3,15},{4,0},{5,1},{6,2},{7,3},{8,4},{9,5},{1... | collective-permute-start | bytes 393224 | tf_op jit(solution)/shard_map/ppermute | solution.py:128
  57.9 0.0 collective-permute-done.12
  58.0 0.1 collective-permute-start.13
  58.0 0.4 collective-permute-done.16
  58.5 2.8 %collective-permute-start.17 = (bf16[32,2048]{1,0:T(8,128)(2,1)S(1)}, bf16[32,2048]{1,0:T(8,128)(2,1)S(1)}, u32[]{:S(2)}, u32[]{:S(2)}) collective-permute-start(bf16[32,2048]{1,0:T(8,128)(2,1)S(1)} %add_convert_fusion), channel_id=1, source_target_pairs={{0,8},{1,9},{2,10},{3,11},{4,12},{5,13},{6,14},{7,15},{8,0},{9,1},... | collective-permute-start | bytes 393224 | tf_op jit(solution)/shard_map/ppermute | solution.py:128
  61.3 0.1 slice.19
  61.4 2.6 %collective-permute-start.20 = (f32[32,64]{1,0:T(8,128)S(1)}, f32[32,64]{1,0:T(8,128)S(1)}, u32[]{:S(2)}, u32[]{:S(2)}) collective-permute-start(f32[32,64]{1,0:T(8,128)S(1)} %slice.19), channel_id=1, source_target_pairs={{0,1},{1,0},{2,3},{3,2},{4,5},{5,4},{6,7},{7,6},{8,9},{9,8},{10,11... | collective-permute-start | bytes 24584 | tf_op jit(solution)/shard_map/ppermute | solution.py:128
  64.0 0.0 collective-permute-done.5
  64.0 0.0 collective-permute-done.9
  64.0 0.0 collective-permute-done.13
  64.0 6.7 %collective-permute-done.17 = bf16[32,2048]{1,0:T(8,128)(2,1)S(1)} collective-permute-done((bf16[32,2048]{1,0:T(8,128)(2,1)S(1)}, bf16[32,2048]{1,0:T(8,128)(2,1)S(1)}, u32[]{:S(2)}, u32[]{:S(2)}) %collective-permute-start.17) | collective-permute-done | bytes 131104 | tf_op jit(solution)/shard_map/ppermute | solution.py:128
  70.6 0.1 fusion.1
  70.7 3.9 %collective-permute-start.18 = (bf16[32,2048]{1,0:T(8,128)(2,1)S(1)}, bf16[32,2048]{1,0:T(8,128)(2,1)S(1)}, u32[]{:S(2)}, u32[]{:S(2)}) collective-permute-start(bf16[32,2048]{1,0:T(8,128)(2,1)S(1)} %get-tuple-element.34), channel_id=1, source_target_pairs={{0,1},{1,2},{2,3},{3,4},{4,5},{5,6},{6,7},{7,8},{8,9},{9,10},{10,1... | collective-permute-start | bytes 393224 | tf_op jit(solution)/shard_map/ppermute | solution.py:132
  74.6 1.9 %collective-permute-start.19 = (bf16[32,2048]{1,0:T(8,128)(2,1)S(1)}, bf16[32,2048]{1,0:T(8,128)(2,1)S(1)}, u32[]{:S(2)}, u32[]{:S(2)}) collective-permute-start(bf16[32,2048]{1,0:T(8,128)(2,1)S(1)} %get-tuple-element.34), channel_id=1, source_target_pairs={{1,0},{2,1},{3,2},{4,3},{5,4},{6,5},{7,6},{8,7},{9,8},{10,9},{11,1... | collective-permute-start | bytes 393224 | tf_op jit(solution)/shard_map/ppermute | solution.py:133
  76.6 0.6 fusion
  77.2 0.0 collective-permute-done.18.up_ref
  77.2 3.7 %collective-permute-done.19.down_ref = bf16[32,2048]{1,0:T(8,128)(2,1)S(1)} collective-permute-done((bf16[32,2048]{1,0:T(8,128)(2,1)S(1)}, bf16[32,2048]{1,0:T(8,128)(2,1)S(1)}, u32[]{:S(2)}, u32[]{:S(2)}) %collective-permute-start.19) | collective-permute-done | bytes 131104 | tf_op jit(solution)/shard_map/ppermute | solution.py:133
  80.9 1.0 %shard_map.83 = f32[32,2048]{1,0:T(8,128)} custom-call(f32[32,2048]{1,0:T(8,128)S(1)} %get-tuple-element.35.own_ref, bf16[32,2048]{1,0:T(8,128)(2,1)S(1)} %collective-permute-done.18.up_ref, bf16[32,2048]{1,0:T(8,128)(2,1)S(1)} %collective-permute-done.19.down_ref, f32[32,1]{1,0:T(8,128)S(1)} %copy.31.strength_ref), custom_call_target="tpu_custom_call" | custom-call | flops 655360 | bytes 786432 | tf_op jit(solution)/shard_map/pallas_call | solution.py:180
  (21 shorter events, 0.1 us)
Async XLA Ops:
  0.7 3.4 %copy-start = (s32[64,32768]{1,0:T(8,128)S(1)}, s32[64,32768]{1,0:T(8,128)}, u32[]{:S(2)}) copy-start(s32[64,32768]{1,0:T(8,128)} %counts_ref.1) | copy-start | bytes 25165828
  4.1 4.1 %copy-start.1 = (f32[32,2048]{1,0:T(8,128)S(1)}, f32[32,2048]{1,0:T(8,128)}, u32[]{:S(2)}) copy-start(f32[32,2048]{1,0:T(8,128)} %latent_ref.1) | copy-start | bytes 786436
  4.1 10.6 %copy-start.8 = (f32[32]{0:T(128)S(1)}, f32[32]{0:T(128)}, u32[]{:S(2)}) copy-start(f32[32]{0:T(128)} %param.10) | copy-start | bytes 388
  4.1 18.1 %copy-start.6 = (bf16[32,64]{1,0:T(8,128)(2,1)S(1)}, bf16[32,64]{1,0:T(8,128)(2,1)}, u32[]{:S(2)}) copy-start(bf16[32,64]{1,0:T(8,128)(2,1)} %param.8) | copy-start | bytes 12292
  4.1 20.2 %copy-start.7 = (f32[64]{0:T(128)S(1)}, f32[64]{0:T(128)}, u32[]{:S(2)}) copy-start(f32[64]{0:T(128)} %param.9) | copy-start | bytes 772
  8.2 29.3 %collective-permute-start.3 = (bf16[4,2,64,2048]{3,2,1,0:T(8,128)(2,1)}, bf16[4,2,64,2048]{3,2,1,0:T(8,128)(2,1)}, u32[]{:S(2)}, u32[]{:S(2)}) collective-permute-start(bf16[4,2,64,2048]{3,2,1,0:T(8,128)(2,1)} %get-tuple-element.20), channel_id=1, source_target_pairs={{0,1},{1,0},{2,3},{3,2},{4,5},{5,4},{6,7},{7,6},{8,9},{9,8},{10,11... | collective-permute-start | bytes 6291464 | tf_op jit(solution)/shard_map/ppermute | solution.py:128
  8.2 7.8 %collective-permute-start = (f32[32,2048]{1,0:T(8,128)S(1)}, f32[32,2048]{1,0:T(8,128)S(1)}, u32[]{:S(2)}, u32[]{:S(2)}) collective-permute-start(f32[32,2048]{1,0:T(8,128)S(1)} %copy-done.1), channel_id=1, source_target_pairs={{0,1},{1,2},{2,3},{3,4},{4,5},{5,6},{6,7},{7,8},{8,9},{9,10},{10,1... | collective-permute-start | bytes 786440 | tf_op jit(solution)/shard_map/ppermute | solution.py:132
  12.7 7.7 %collective-permute-start.1 = (f32[32,2048]{1,0:T(8,128)S(1)}, f32[32,2048]{1,0:T(8,128)S(1)}, u32[]{:S(2)}, u32[]{:S(2)}) collective-permute-start(f32[32,2048]{1,0:T(8,128)S(1)} %copy-done.1), channel_id=1, source_target_pairs={{1,0},{2,1},{3,2},{4,3},{5,4},{6,5},{7,6},{8,7},{9,8},{10,9},{11,1... | collective-permute-start | bytes 786440 | tf_op jit(solution)/shard_map/ppermute | solution.py:133
  20.9 7.2 %collective-permute-start.6 = (bf16[32,2048]{1,0:T(8,128)(2,1)S(1)}, bf16[32,2048]{1,0:T(8,128)(2,1)S(1)}, u32[]{:S(2)}, u32[]{:S(2)}) collective-permute-start(bf16[32,2048]{1,0:T(8,128)(2,1)S(1)} %get-tuple-element.18.own_f), channel_id=1, source_target_pairs={{0,4},{1,5},{2,6},{3,7},{4,8},{5,9},{6,10},{7,11},{8,12},{9,13},{1... | collective-permute-start | bytes 393224 | tf_op jit(solution)/shard_map/ppermute | solution.py:128
  22.3 8.0 %collective-permute-start.10 = (bf16[32,2048]{1,0:T(8,128)(2,1)S(1)}, bf16[32,2048]{1,0:T(8,128)(2,1)S(1)}, u32[]{:S(2)}, u32[]{:S(2)}) collective-permute-start(bf16[32,2048]{1,0:T(8,128)(2,1)S(1)} %get-tuple-element.18.own_f), channel_id=1, source_target_pairs={{0,12},{1,13},{2,14},{3,15},{4,0},{5,1},{6,2},{7,3},{8,4},{9,5},{1... | collective-permute-start | bytes 393224 | tf_op jit(solution)/shard_map/ppermute | solution.py:128
  24.4 5.6 %collective-permute-start.4 = (f32[40,64]{1,0:T(8,128)S(1)}, f32[40,64]{1,0:T(8,128)S(1)}, u32[]{:S(2)}, u32[]{:S(2)}) collective-permute-start(f32[40,64]{1,0:T(8,128)S(1)} %pad_maximum_fusion), channel_id=1, source_target_pairs={{0,1},{1,0},{2,3},{3,2},{4,5},{5,4},{6,7},{7,6},{8,9},{9,8},{10,11... | collective-permute-start | bytes 30728 | tf_op jit(solution)/shard_map/ppermute | solution.py:128
  24.5 12.0 %collective-permute-start.14 = (bf16[32,2048]{1,0:T(8,128)(2,1)S(1)}, bf16[32,2048]{1,0:T(8,128)(2,1)S(1)}, u32[]{:S(2)}, u32[]{:S(2)}) collective-permute-start(bf16[32,2048]{1,0:T(8,128)(2,1)S(1)} %get-tuple-element.18.own_f), channel_id=1, source_target_pairs={{0,8},{1,9},{2,10},{3,11},{4,12},{5,13},{6,14},{7,15},{8,0},{9,1},... | collective-permute-start | bytes 393224 | tf_op jit(solution)/shard_map/ppermute | solution.py:128
  28.1 8.8 %collective-permute-start.7 = (bf16[32,2048]{1,0:T(8,128)(2,1)S(1)}, bf16[32,2048]{1,0:T(8,128)(2,1)S(1)}, u32[]{:S(2)}, u32[]{:S(2)}) collective-permute-start(bf16[32,2048]{1,0:T(8,128)(2,1)S(1)} %collective-permute-done.6.own_f), channel_id=1, source_target_pairs={{0,2},{1,3},{2,0},{3,1},{4,6},{5,7},{6,4},{7,5},{8,10},{9,11},{10,... | collective-permute-start | bytes 393224 | tf_op jit(solution)/shard_map/ppermute | solution.py:128
  30.1 12.9 %collective-permute-start.2 = (bf16[32,2048]{1,0:T(8,128)(2,1)S(1)}, bf16[32,2048]{1,0:T(8,128)(2,1)S(1)}, u32[]{:S(2)}, u32[]{:S(2)}) collective-permute-start(bf16[32,2048]{1,0:T(8,128)(2,1)S(1)} %get-tuple-element.18.own_f), channel_id=1, source_target_pairs={{0,2},{1,3},{2,0},{3,1},{4,6},{5,7},{6,4},{7,5},{8,10},{9,11},{10,... | collective-permute-start | bytes 393224 | tf_op jit(solution)/shard_map/ppermute | solution.py:128
  30.2 17.5 %collective-permute-start.11 = (bf16[32,2048]{1,0:T(8,128)(2,1)S(1)}, bf16[32,2048]{1,0:T(8,128)(2,1)}, u32[]{:S(2)}, u32[]{:S(2)}) collective-permute-start(bf16[32,2048]{1,0:T(8,128)(2,1)S(1)} %collective-permute-done.10.own_f), channel_id=1, source_target_pairs={{0,2},{1,3},{2,0},{3,1},{4,6},{5,7},{6,4},{7,5},{8,10},{9,11},{10,... | collective-permute-start | bytes 393224 | tf_op jit(solution)/shard_map/ppermute | solution.py:128
  36.5 15.3 %collective-permute-start.15 = (bf16[32,2048]{1,0:T(8,128)(2,1)S(1)}, bf16[32,2048]{1,0:T(8,128)(2,1)S(1)}, u32[]{:S(2)}, u32[]{:S(2)}) collective-permute-start(bf16[32,2048]{1,0:T(8,128)(2,1)S(1)} %collective-permute-done.14.own_f), channel_id=1, source_target_pairs={{0,2},{1,3},{2,0},{3,1},{4,6},{5,7},{6,4},{7,5},{8,10},{9,11},{10,... | collective-permute-start | bytes 393224 | tf_op jit(solution)/shard_map/ppermute | solution.py:128
  36.8 0.7 copy-start.4
  37.6 0.9 %copy-start.5 = (bf16[32,2048]{1,0:T(8,128)(2,1)S(1)}, bf16[32,2048]{1,0:T(8,128)(2,1)}, u32[]{:S(2)}) copy-start(bf16[32,2048]{1,0:T(8,128)(2,1)} %copy-done.4) | copy-start | bytes 393220
  41.9 13.1 %collective-permute-start.8 = (bf16[32,2048]{1,0:T(8,128)(2,1)}, bf16[32,2048]{1,0:T(8,128)(2,1)}, u32[]{:S(2)}, u32[]{:S(2)}) collective-permute-start(bf16[32,2048]{1,0:T(8,128)(2,1)} %get-tuple-element.24), channel_id=1, source_target_pairs={{0,2},{1,3},{2,0},{3,1},{4,6},{5,7},{6,4},{7,5},{8,10},{9,11},{10,... | collective-permute-start | bytes 393224 | tf_op jit(solution)/shard_map/ppermute | solution.py:128
  43.0 0.6 copy-start.2
  43.7 0.9 %copy-start.3 = (bf16[32,2048]{1,0:T(8,128)(2,1)S(1)}, bf16[32,2048]{1,0:T(8,128)(2,1)}, u32[]{:S(2)}) copy-start(bf16[32,2048]{1,0:T(8,128)(2,1)} %copy-done.2) | copy-start | bytes 393220
  47.4 16.6 %collective-permute-start.5 = (bf16[32,2048]{1,0:T(8,128)(2,1)S(1)}, bf16[32,2048]{1,0:T(8,128)(2,1)S(1)}, u32[]{:S(2)}, u32[]{:S(2)}) collective-permute-start(bf16[32,2048]{1,0:T(8,128)(2,1)S(1)} %get-tuple-element.22), channel_id=1, source_target_pairs={{0,2},{1,3},{2,0},{3,1},{4,6},{5,7},{6,4},{7,5},{8,10},{9,11},{10,... | collective-permute-start | bytes 393224 | tf_op jit(solution)/shard_map/ppermute | solution.py:128
  50.6 7.3 %collective-permute-start.12 = (bf16[32,2048]{1,0:T(8,128)(2,1)S(1)}, bf16[32,2048]{1,0:T(8,128)(2,1)S(1)}, u32[]{:S(2)}, u32[]{:S(2)}) collective-permute-start(bf16[32,2048]{1,0:T(8,128)(2,1)S(1)} %get-tuple-element.26), channel_id=1, source_target_pairs={{0,2},{1,3},{2,0},{3,1},{4,6},{5,7},{6,4},{7,5},{8,10},{9,11},{10,... | collective-permute-start | bytes 393224 | tf_op jit(solution)/shard_map/ppermute | solution.py:128
  54.6 3.8 %collective-permute-start.16 = (bf16[32,2048]{1,0:T(8,128)(2,1)S(1)}, bf16[32,2048]{1,0:T(8,128)(2,1)S(1)}, u32[]{:S(2)}, u32[]{:S(2)}) collective-permute-start(bf16[32,2048]{1,0:T(8,128)(2,1)S(1)} %get-tuple-element.28), channel_id=1, source_target_pairs={{0,2},{1,3},{2,0},{3,1},{4,6},{5,7},{6,4},{7,5},{8,10},{9,11},{10,... | collective-permute-start | bytes 393224 | tf_op jit(solution)/shard_map/ppermute | solution.py:128
  55.9 8.0 %collective-permute-start.9 = (bf16[32,2048]{1,0:T(8,128)(2,1)S(1)}, bf16[32,2048]{1,0:T(8,128)(2,1)S(1)}, u32[]{:S(2)}, u32[]{:S(2)}) collective-permute-start(bf16[32,2048]{1,0:T(8,128)(2,1)S(1)} %add_convert_fusion.2), channel_id=1, source_target_pairs={{0,12},{1,13},{2,14},{3,15},{4,0},{5,1},{6,2},{7,3},{8,4},{9,5},{1... | collective-permute-start | bytes 393224 | tf_op jit(solution)/shard_map/ppermute | solution.py:128
  58.0 6.0 %collective-permute-start.13 = (bf16[32,2048]{1,0:T(8,128)(2,1)S(1)}, bf16[32,2048]{1,0:T(8,128)(2,1)S(1)}, u32[]{:S(2)}, u32[]{:S(2)}) collective-permute-start(bf16[32,2048]{1,0:T(8,128)(2,1)S(1)} %add_convert_fusion.1), channel_id=1, source_target_pairs={{0,4},{1,5},{2,6},{3,7},{4,8},{5,9},{6,10},{7,11},{8,12},{9,13},{1... | collective-permute-start | bytes 393224 | tf_op jit(solution)/shard_map/ppermute | solution.py:128
  58.5 12.1 %collective-permute-start.17 = (bf16[32,2048]{1,0:T(8,128)(2,1)S(1)}, bf16[32,2048]{1,0:T(8,128)(2,1)S(1)}, u32[]{:S(2)}, u32[]{:S(2)}) collective-permute-start(bf16[32,2048]{1,0:T(8,128)(2,1)S(1)} %add_convert_fusion), channel_id=1, source_target_pairs={{0,8},{1,9},{2,10},{3,11},{4,12},{5,13},{6,14},{7,15},{8,0},{9,1},... | collective-permute-start | bytes 393224 | tf_op jit(solution)/shard_map/ppermute | solution.py:128
  61.4 15.2 %collective-permute-start.20 = (f32[32,64]{1,0:T(8,128)S(1)}, f32[32,64]{1,0:T(8,128)S(1)}, u32[]{:S(2)}, u32[]{:S(2)}) collective-permute-start(f32[32,64]{1,0:T(8,128)S(1)} %slice.19), channel_id=1, source_target_pairs={{0,1},{1,0},{2,3},{3,2},{4,5},{5,4},{6,7},{7,6},{8,9},{9,8},{10,11... | collective-permute-start | bytes 24584 | tf_op jit(solution)/shard_map/ppermute | solution.py:128
  70.7 6.4 %collective-permute-start.18 = (bf16[32,2048]{1,0:T(8,128)(2,1)S(1)}, bf16[32,2048]{1,0:T(8,128)(2,1)S(1)}, u32[]{:S(2)}, u32[]{:S(2)}) collective-permute-start(bf16[32,2048]{1,0:T(8,128)(2,1)S(1)} %get-tuple-element.34), channel_id=1, source_target_pairs={{0,1},{1,2},{2,3},{3,4},{4,5},{5,6},{6,7},{7,8},{8,9},{9,10},{10,1... | collective-permute-start | bytes 393224 | tf_op jit(solution)/shard_map/ppermute | solution.py:132
  74.6 6.3 %collective-permute-start.19 = (bf16[32,2048]{1,0:T(8,128)(2,1)S(1)}, bf16[32,2048]{1,0:T(8,128)(2,1)S(1)}, u32[]{:S(2)}, u32[]{:S(2)}) collective-permute-start(bf16[32,2048]{1,0:T(8,128)(2,1)S(1)} %get-tuple-element.34), channel_id=1, source_target_pairs={{1,0},{2,1},{3,2},{4,3},{5,4},{6,5},{7,6},{8,7},{9,8},{10,9},{11,1... | collective-permute-start | bytes 393224 | tf_op jit(solution)/shard_map/ppermute | solution.py:133

commit v2 on v1

v2 whole, which is shorter than its diff:
```python
import functools

import jax
import jax.numpy as jnp
from jax import lax
from jax.experimental import pallas as pl
from jax.experimental.pallas import tpu as pltpu
from jax.sharding import PartitionSpec as P

SPACE = "space"
MIB = 1024 * 1024
VMEM = pl.BlockSpec(memory_space=pltpu.VMEM)
SMEM = pl.BlockSpec(memory_space=pltpu.SMEM)


def params(mib):
    return pltpu.CompilerParams(vmem_limit_bytes=mib * MIB)


def cost(flops, nbytes, trans=0):
    return pl.CostEstimate(flops=flops, bytes_accessed=nbytes, transcendentals=trans)


def cast_kernel(place, counts_ref, out_ref, taken, arrived, *, turn):
    planes, rows, _, width = out_ref.shape
    parity = lax.rem(place[0] + turn, 2)
    copies = []
    for block in range(planes * rows):
        start = pl.multiple_of((2 * block + parity) * width, width)
        copies.append(pltpu.make_async_copy(counts_ref.at[:, pl.ds(start, width)], taken.at[block], arrived.at[block]))
        copies[-1].start()
    for block, copy in enumerate(copies):
        copy.wait()
        out_ref[block // rows, block % rows] = taken[block].astype(jnp.float32).astype(jnp.bfloat16)


def cast_counts(place, counts, planes, width, turn):
    genes = counts.shape[0]
    return pl.pallas_call(
        functools.partial(cast_kernel, turn=turn),
        in_specs=[SMEM, pl.BlockSpec(memory_space=pltpu.HBM)],
        out_specs=VMEM,
        out_shape=jax.ShapeDtypeStruct((planes, 2, genes, width), jnp.bfloat16),
        scratch_shapes=[pltpu.VMEM((2 * planes, genes, width), jnp.int32), pltpu.SemaphoreType.DMA((2 * planes,))],
        compiler_params=params(14),
        cost_estimate=cost(counts.size, counts.size * 3),
    )(place, counts)


def column(row_ref, rows, lanes):
    tile = jnp.broadcast_to(row_ref[...], (128, rows)).T
    return jnp.concatenate([tile] * (lanes // 128), axis=1)


def stencil(values, near, far, strength):
    width = values.shape[1]
    at = lax.broadcasted_iota(jnp.int32, values.shape, 1)
    left = jnp.where(at > 0, pltpu.roll(values, 1, 1), 0.0)
    right = jnp.where(at < width - 1, pltpu.roll(values, width - 1, 1), 0.0)
    return values + strength * (near + far + left + right - 4.0 * values)


def factor_kernel(
    place, latent_ref, near_ref, far_ref, strength_ref, tissue_ref, own_w, other_w, own_b, other_b,
    factor_ref, slope_ref, weight_ref, turned_ref, back_ref, *, scale,
):
    factors, width = latent_ref.shape
    strength = column(strength_ref, factors, width)
    smoothed = stencil(latent_ref[...], near_ref[...], far_ref[...], strength)
    small = jnp.exp(-jnp.abs(smoothed))
    inside = tissue_ref[:, pl.ds(pl.multiple_of(place[3] * width, width), width)] > 0
    soft = jnp.maximum(smoothed, 0.0) + jnp.log1p(small)
    factor_ref[...] = jnp.where(inside, soft, 0.0).astype(jnp.bfloat16)
    sigmoid = jnp.where(smoothed >= 0.0, 1.0, small) / (1.0 + small)
    slope_ref[...] = jnp.where(inside, sigmoid * scale, 0.0)
    weights = jnp.concatenate([own_w[...].astype(jnp.float32), other_w[...].astype(jnp.float32)], axis=1)
    weight_ref[...] = weights.astype(jnp.bfloat16)
    turned_ref[...] = weights.T.astype(jnp.bfloat16)
    genes = own_w.shape[1]
    back_ref[:genes] = column(own_b, genes, 128)
    back_ref[genes:] = column(other_b, genes, 128)


def gene_kernel(
    place, own_f, other_f, keep_ref, came_ref, weight_ref, turned_ref, back_ref, own_p, other_p, load_p, *, step, shift,
):
    width = own_f.shape[1]
    planes = keep_ref.shape[0]
    weights, turned = weight_ref[...], turned_ref[...]
    offset = jnp.concatenate([back_ref[...]] * (step // 128), axis=1)
    load = jnp.zeros(load_p.shape, jnp.float32)
    plane = lax.rem(place[2] + planes - shift, planes)
    for half, (field, out) in enumerate(((own_f, own_p), (other_f, other_p))):
        row = lax.rem(place[1] + half, 2)
        for at in range(0, width, step):
            f = field[:, at : at + step]
            rate = jnp.dot(turned, f, preferred_element_type=jnp.float32) + offset
            seen = jnp.concatenate(
                [keep_ref[plane, row, :, at : at + step], came_ref[plane, row, :, at : at + step]], axis=0
            ).astype(jnp.float32)
            residual = (1.0 - seen / rate).astype(jnp.bfloat16)
            out[:, at : at + step] = jnp.dot(weights, residual, preferred_element_type=jnp.float32).astype(out.dtype)
            load += lax.dot_general(f, residual, (((1,), (1,)), ((), ())), preferred_element_type=jnp.float32)
    load_p[...] = load


def gene_sums(place, shift, own_f, other_f, keep, came, weights, turned, back):
    factors, width = own_f.shape
    genes = keep.shape[2]
    work = 2 * genes * 2 * width
    return pl.pallas_call(
        functools.partial(gene_kernel, step=1024, shift=shift),
        in_specs=[SMEM] + [VMEM] * 7,
        out_specs=[VMEM] * 3,
        out_shape=[
            jax.ShapeDtypeStruct(own_f.shape, jnp.float32),
            jax.ShapeDtypeStruct(own_f.shape, jnp.bfloat16),
            jax.ShapeDtypeStruct((factors, 2 * genes), jnp.float32),
        ],
        compiler_params=params(12),
        cost_estimate=cost(6 * factors * work, 3 * work, work),
    )(place, own_f, other_f, keep, came, weights, turned, back)


def last_kernel(own_ref, near_ref, far_ref, strength_ref, out_ref):
    factors, width = own_ref.shape
    out_ref[...] = stencil(
        own_ref[...], near_ref[...].astype(jnp.float32), far_ref[...].astype(jnp.float32),
        column(strength_ref, factors, width),
    )


def after(x, *done):
    return lax.optimization_barrier((x, *done))[0]


def local(counts, latent, loading, background, coupling, tissue):
    factors, width = latent.shape
    genes, total_spots = counts.shape
    count = lax.axis_size(SPACE)
    planes = count // 4
    me = lax.axis_index(SPACE)
    place = jnp.stack([me & 1, (me >> 1) & 1, me >> 2, me])

    def send(x, to):
        return lax.ppermute(x, SPACE, [(i, to(i)) for i in range(count)])

    def across(i):
        return i + 1 if i % 2 else i - 1

    def chips(x):
        return lax.ppermute(x, SPACE, [(i, across(i)) for i in range(count) if 0 <= across(i) < count])

    over_core = lambda i: i ^ 1
    over_row = lambda i: i ^ 2
    along = lambda s: lambda i: (i + 4 * s) % count

    far = chips(latent)
    near = send(latent, over_core)
    away = cast_counts(place, counts, planes, width, 1)
    other_w, other_b = send(loading, over_core), send(background, over_core)
    came = send(away, over_core)
    strength = coupling.reshape(1, factors)
    full = jax.ShapeDtypeStruct
    field, slope, weights, turned, back = pl.pallas_call(
        functools.partial(factor_kernel, scale=1.0 / (genes * count)),
        in_specs=[SMEM] + [VMEM] * 9,
        out_specs=[VMEM] * 5,
        out_shape=[
            full(latent.shape, jnp.bfloat16), full(latent.shape, jnp.float32),
            full((factors, 2 * genes), jnp.bfloat16), full((2 * genes, factors), jnp.bfloat16),
            full((2 * genes, 128), jnp.float32),
        ],
        compiler_params=params(8),
        cost_estimate=cost(latent.size * 20, latent.size * 18, latent.size * 3),
    )(
        place, latent, near, far, strength, tissue.reshape(1, total_spots),
        loading, other_w, background.reshape(1, genes), other_b.reshape(1, genes),
    )

    keep = cast_counts(after(place, field), counts, planes, width, 0)
    order = [0] + sorted(range(1, planes), key=lambda s: -min(s, planes - s))
    fields = {s: field if s == 0 else send(field, along(s)) for s in order}
    total = loads = None
    done, returned = [], []
    for at, s in enumerate(order):
        mine = fields[s] if s == 0 else after(fields[s], done[max(0, at - 2)])
        other = send(mine, over_row)
        own_p, other_p, load = gene_sums(place, s, mine, other, keep, came, weights, turned, back)
        done.append(load)
        loads = load if loads is None else loads + load
        if s == 0:
            total, later = own_p, other_p
        else:
            summed = own_p + send(other_p, over_row).astype(jnp.float32)
            returned.append(send(summed.astype(jnp.bfloat16), along(-s)))
    total = total + send(after(later, done[-2]), over_row).astype(jnp.float32)
    for r in returned:
        total = total + r.astype(jnp.float32)
    grad_smooth = total * slope
    rounded = grad_smooth.astype(jnp.bfloat16)
    near2, far2 = send(rounded, over_core), chips(rounded)
    grad_latent = pl.pallas_call(
        last_kernel,
        in_specs=[VMEM] * 4,
        out_specs=VMEM,
        out_shape=full(latent.shape, jnp.float32),
        compiler_params=params(8),
        cost_estimate=cost(latent.size * 10, latent.size * 12),
    )(grad_smooth, near2, far2, strength)
    swapped = send(loads[:, genes:], over_core)
    grad_loading = (loads[:, :genes] + swapped) / total_spots
    return grad_latent, grad_loading


def solution(mesh):
    split = P(None, ("groups", SPACE))
    return jax.shard_map(
        local,
        mesh=mesh,
        in_specs=(P(SPACE, "groups"), split, split, P(("groups", SPACE)), P("groups"), P("groups")),
        out_specs=(split, split),
        check_vma=False,
    )
```

time: 82.4 us -> 69.5 us (0.84)
  waiting for transfers between devices: 23.8 us -> 16.1 us
  Pallas kernels: 17.4 us -> 11.1 us
  starting transfers between devices: 30.4 us -> 36.3 us
  local copies, waits for them, and re-layouts: 7.57 us -> 3.48 us
  other arithmetic: 1.96 us -> 0.87 us
    ppermute x17 -> x20, starting transfers between devices: 18.2 us -> 28.2 us  [send(): return lax.ppermute(x, SPACE, [(i, to(i)) for i in range(count)])]
    pallas_call x5 -> x6, Pallas kernels: 16 us -> 9.12 us  [the longest x4 6.82 us: gene_sums(): pl.pallas_call(functools.partial(gene_kernel, step=1024, shift=shift), in...]
    ppermute x17 -> x20, waiting for transfers between devices: 15.1 us -> 9.34 us  [send(): return lax.ppermute(x, SPACE, [(i, to(i)) for i in range(count)])]
    ppermute x4 -> x2, starting transfers between devices: 12.2 us -> 8.07 us  [chips(): lax.ppermute(x, SPACE, [(i, across(i)) for i in range(count) if 0 <= acro...]
    unnamed x19 -> x12, local copies, waits for them, and re-layouts: 6.63 us -> 3.4 us
    ppermute x4 -> x2, waiting for transfers between devices: 8.7 us -> 6.78 us  [chips(): lax.ppermute(x, SPACE, [(i, across(i)) for i in range(count) if 0 <= acro...]
    convert_element_type x3, other arithmetic: 1 us -> 0.08 us  [local(): returned.append(send(summed.astype(jnp.bfloat16), along(-s)))]
  transfers between devices with their start and end apart: 21 -> 22, of which waited for: 8 -> 8; matrix products, arithmetic and copies ran while one was open for 4% -> 1% of each run, Pallas kernels for 15% -> 13%
where the time goes in v2:
time: 69.5 us; the launch traced here: 68.7 us
  starting transfers between devices  36.3 us (52%)
  waiting for transfers between devices  16.1 us (23%)
  Pallas kernels  11.1 us (16%)
  local copies, waits for them, and re-layouts  3.48 us (5%)
  other arithmetic  0.87 us (1%)
  between operations  0.85 us (1%)
    ppermute x20, starting transfers between devices, send(): return lax.ppermute(x, SPACE, [(i, to(i)) for i in range(count)])  28.2 us
    ppermute x20, waiting for transfers between devices, send(): return lax.ppermute(x, SPACE, [(i, to(i)) for i in range(count)])  9.34 us
    ppermute x2, starting transfers between devices, chips(): lax.ppermute(x, SPACE, [(i, across(i)) for i in range(count) if 0 <= acro...  8.07 us
    pallas_call x4, Pallas kernels, gene_sums(): pl.pallas_call(functools.partial(gene_kernel, step=1024, shift=shift), in...  6.82 us
    ppermute x2, waiting for transfers between devices, chips(): lax.ppermute(x, SPACE, [(i, across(i)) for i in range(count) if 0 <= acro...  6.78 us
    unnamed x12, local copies, waits for them, and re-layouts  3.4 us
    pallas_call x2, Pallas kernels, cast_counts(): pl.pallas_call(functools.partial(cast_kernel, turn=turn), in_specs=[SMEM,...  2.3 us
  transfers between devices with their start and end apart: 22, of which 8 were waited for; matrix products, arithmetic and copies ran while one was open for 1% of the time, Pallas kernels for 13%

profile of v2, /device:TPU:1, one launch (start us, length us, event | category | flops | bytes accessed | tf_op | source)
XLA Modules:
  0.0 68.7 jit_solution(16242167945571847419)
XLA Ops:
  0.6 0.1 pad_add_fusion.place
  0.7 0.0 copy-start
  0.7 3.4 %copy-done = s32[64,32768]{1,0:T(8,128)S(1)} copy-done((s32[64,32768]{1,0:T(8,128)S(1)}, s32[64,32768]{1,0:T(8,128)}, u32[]{:S(2)}) %copy-start) | copy-done | bytes 8388632
  4.1 0.0 copy-start.4
  4.1 1.2 %shard_map.79 = bf16[4,2,64,2048]{3,2,1,0:T(8,128)(2,1)S(1)} custom-call(s32[4]{0:T(128)S(1)} %pad_add_fusion.place, s32[64,32768]{1,0:T(8,128)S(1)} %copy-done), custom_call_target="tpu_custom_call" | custom-call | flops 2097152 | bytes 6291456 | tf_op jit(solution)/shard_map/pallas_call | solution.py:39
  5.3 0.1 collective-permute-start.5
  5.4 0.0 copy-done.1
  5.4 0.5 collective-permute-start
  5.9 4.5 %collective-permute-start.1 = (f32[32,2048]{1,0:T(8,128)S(1)}, f32[32,2048]{1,0:T(8,128)S(1)}, u32[]{:S(2)}, u32[]{:S(2)}) collective-permute-start(f32[32,2048]{1,0:T(8,128)S(1)} %copy-done.1), channel_id=1, source_target_pairs={{1,2},{2,1},{3,4},{4,3},{5,6},{6,5},{7,8},{8,7},{9,10},{10,9},{11,... | collective-permute-start | bytes 786440 | tf_op jit(solution)/shard_map/ppermute | solution.py:152
  10.4 0.0 copy-done.3
  10.4 0.1 collective-permute-start.2
  10.5 0.0 copy-done.5
  10.5 0.5 collective-permute-start.3
  11.0 0.8 %collective-permute-done.3 = f32[64]{0:T(128)S(1)} collective-permute-done((f32[64]{0:T(128)S(1)}, f32[64]{0:T(128)S(1)}, u32[]{:S(2)}, u32[]{:S(2)}) %collective-permute-start.3) | collective-permute-done | bytes 288 | tf_op jit(solution)/shard_map/ppermute | solution.py:146
  11.8 0.0 collective-permute-done.2.other_w
  11.8 0.0 collective-permute-done.near_ref
  11.8 4.7 %collective-permute-done.1.far_ref = f32[32,2048]{1,0:T(8,128)S(1)} collective-permute-done((f32[32,2048]{1,0:T(8,128)S(1)}, f32[32,2048]{1,0:T(8,128)S(1)}, u32[]{:S(2)}, u32[]{:S(2)}) %collective-permute-start.1) | collective-permute-done | bytes 262176 | tf_op jit(solution)/shard_map/ppermute | solution.py:152
  16.5 0.0 copy-done.2
  16.5 0.0 copy-done.4
  16.5 1.0 %shard_map.77 = (bf16[32,2048]{1,0:T(8,128)(2,1)S(1)}, f32[32,2048]{1,0:T(8,128)S(1)}, bf16[32,128]{1,0:T(8,128)(2,1)S(1)}, bf16[128,32]{1,0:T(8,128)(2,1)S(1)}, f32[128,128]{1,0:T(8,128)S(1)}) custom-call(s32[4]{0:T(128)S(1)} %pad_add_fusion.place, f32[32,2048]{1,0:T(8,128)S(1)} %copy-done.1, f32[32,2048]{1,0:T(8,128)S(1)} %collective-permute-done.near_ref, ...), custom_call_target="tpu_custom_call" | custom-call | flops 1310720 | bytes 1179648 | tf_op jit(solution)/shard_map/pallas_call | solution.py:165
  17.6 0.4 collective-permute-start.4
  18.0 2.9 %collective-permute-start.9 = (bf16[32,2048]{1,0:T(8,128)(2,1)S(1)}, bf16[32,2048]{1,0:T(8,128)(2,1)S(1)}, u32[]{:S(2)}, u32[]{:S(2)}) collective-permute-start(bf16[32,2048]{1,0:T(8,128)(2,1)S(1)} %get-tuple-element.24.own_f), channel_id=1, source_target_pairs={{0,8},{1,9},{2,10},{3,11},{4,12},{5,13},{6,14},{7,15},{8,0},{9,1},... | collective-permute-start | bytes 393224 | tf_op jit(solution)/shard_map/ppermute | solution.py:146
  20.9 1.3 %collective-permute-start.6 = (bf16[32,2048]{1,0:T(8,128)(2,1)S(1)}, bf16[32,2048]{1,0:T(8,128)(2,1)S(1)}, u32[]{:S(2)}, u32[]{:S(2)}) collective-permute-start(bf16[32,2048]{1,0:T(8,128)(2,1)S(1)} %get-tuple-element.24.own_f), channel_id=1, source_target_pairs={{0,4},{1,5},{2,6},{3,7},{4,8},{5,9},{6,10},{7,11},{8,12},{9,13},{1... | collective-permute-start | bytes 393224 | tf_op jit(solution)/shard_map/ppermute | solution.py:146
  22.2 1.1 %shard_map.78.keep_ref = bf16[4,2,64,2048]{3,2,1,0:T(8,128)(2,1)S(1)} custom-call(s32[4]{0:T(128)S(1)} %pad_add_fusion.place, s32[64,32768]{1,0:T(8,128)S(1)} %copy-done), custom_call_target="tpu_custom_call" | custom-call | flops 2097152 | bytes 6291456 | tf_op jit(solution)/shard_map/pallas_call | solution.py:39
  23.4 0.0 collective-permute-done.4.other_f
  23.4 0.0 collective-permute-done.5.came_ref
  23.4 1.7 %shard_map.80 = (f32[32,2048]{1,0:T(8,128)S(1)}, bf16[32,2048]{1,0:T(8,128)(2,1)S(1)}, f32[32,128]{1,0:T(8,128)S(1)}) custom-call(s32[4]{0:T(128)S(1)} %pad_add_fusion.place, bf16[32,2048]{1,0:T(8,128)(2,1)S(1)} %get-tuple-element.24.own_f, bf16[32,2048]{1,0:T(8,128)(2,1)S(1)} %collective-permute-done.4.other_f, ...), custom_call_target="tpu_custom_call" | custom-call | flops 100663296 | bytes 1572864 | tf_op jit(solution)/shard_map/pallas_call | solution.py:111
  25.1 0.0 collective-permute-done.9.own_f
  25.2 6.1 %collective-permute-start.10 = (bf16[32,2048]{1,0:T(8,128)(2,1)S(1)}, bf16[32,2048]{1,0:T(8,128)(2,1)S(1)}, u32[]{:S(2)}, u32[]{:S(2)}) collective-permute-start(bf16[32,2048]{1,0:T(8,128)(2,1)S(1)} %collective-permute-done.9.own_f), channel_id=1, source_target_pairs={{0,2},{1,3},{2,0},{3,1},{4,6},{5,7},{6,4},{7,5},{8,10},{9,11},{10,... | collective-permute-start | bytes 393224 | tf_op jit(solution)/shard_map/ppermute | solution.py:146
  31.2 1.0 %collective-permute-start.15 = (bf16[32,2048]{1,0:T(8,128)(2,1)S(1)}, bf16[32,2048]{1,0:T(8,128)(2,1)S(1)}, u32[]{:S(2)}, u32[]{:S(2)}) collective-permute-start(bf16[32,2048]{1,0:T(8,128)(2,1)S(1)} %get-tuple-element.24.own_f), channel_id=1, source_target_pairs={{0,12},{1,13},{2,14},{3,15},{4,0},{5,1},{6,2},{7,3},{8,4},{9,5},{1... | collective-permute-start | bytes 393224 | tf_op jit(solution)/shard_map/ppermute | solution.py:146
  32.2 0.0 collective-permute-done.6.own_f
  32.2 0.3 collective-permute-start.7
  32.5 1.1 %collective-permute-done.10.other_f = bf16[32,2048]{1,0:T(8,128)(2,1)S(1)} collective-permute-done((bf16[32,2048]{1,0:T(8,128)(2,1)S(1)}, bf16[32,2048]{1,0:T(8,128)(2,1)S(1)}, u32[]{:S(2)}, u32[]{:S(2)}) %collective-permute-start.10) | collective-permute-done | bytes 131104 | tf_op jit(solution)/shard_map/ppermute | solution.py:146
  33.6 1.7 %shard_map.82 = (f32[32,2048]{1,0:T(8,128)S(1)}, bf16[32,2048]{1,0:T(8,128)(2,1)S(1)}, f32[32,128]{1,0:T(8,128)S(1)}) custom-call(s32[4]{0:T(128)S(1)} %pad_add_fusion.place, bf16[32,2048]{1,0:T(8,128)(2,1)S(1)} %collective-permute-done.9.own_f, bf16[32,2048]{1,0:T(8,128)(2,1)S(1)} %collective-permute-done.10.other_f, ...), custom_call_target="tpu_custom_call" | custom-call | flops 100663296 | bytes 1572864 | tf_op jit(solution)/shard_map/pallas_call | solution.py:111
  35.3 1.5 %collective-permute-start.11 = (bf16[32,2048]{1,0:T(8,128)(2,1)S(1)}, bf16[32,2048]{1,0:T(8,128)(2,1)S(1)}, u32[]{:S(2)}, u32[]{:S(2)}) collective-permute-start(bf16[32,2048]{1,0:T(8,128)(2,1)S(1)} %get-tuple-element.37), channel_id=1, source_target_pairs={{0,2},{1,3},{2,0},{3,1},{4,6},{5,7},{6,4},{7,5},{8,10},{9,11},{10,... | collective-permute-start | bytes 393224 | tf_op jit(solution)/shard_map/ppermute | solution.py:146
  36.8 0.0 collective-permute-done.15.own_f
  36.8 0.1 collective-permute-start.16
  36.9 0.7 %collective-permute-done.7.other_f = bf16[32,2048]{1,0:T(8,128)(2,1)S(1)} collective-permute-done((bf16[32,2048]{1,0:T(8,128)(2,1)S(1)}, bf16[32,2048]{1,0:T(8,128)(2,1)S(1)}, u32[]{:S(2)}, u32[]{:S(2)}) %collective-permute-start.7) | collective-permute-done | bytes 131104 | tf_op jit(solution)/shard_map/ppermute | solution.py:146
  37.7 1.7 %shard_map.81 = (f32[32,2048]{1,0:T(8,128)S(1)}, bf16[32,2048]{1,0:T(8,128)(2,1)S(1)}, f32[32,128]{1,0:T(8,128)S(1)}) custom-call(s32[4]{0:T(128)S(1)} %pad_add_fusion.place, bf16[32,2048]{1,0:T(8,128)(2,1)S(1)} %collective-permute-done.6.own_f, bf16[32,2048]{1,0:T(8,128)(2,1)S(1)} %collective-permute-done.7.other_f, ...), custom_call_target="tpu_custom_call" | custom-call | flops 100663296 | bytes 1572864 | tf_op jit(solution)/shard_map/pallas_call | solution.py:111
  39.4 0.7 %collective-permute-start.8 = (bf16[32,2048]{1,0:T(8,128)(2,1)S(1)}, bf16[32,2048]{1,0:T(8,128)(2,1)S(1)}, u32[]{:S(2)}, u32[]{:S(2)}) collective-permute-start(bf16[32,2048]{1,0:T(8,128)(2,1)S(1)} %get-tuple-element.34), channel_id=1, source_target_pairs={{0,2},{1,3},{2,0},{3,1},{4,6},{5,7},{6,4},{7,5},{8,10},{9,11},{10,... | collective-permute-start | bytes 393224 | tf_op jit(solution)/shard_map/ppermute | solution.py:146
  40.1 0.8 %collective-permute-start.13 = (bf16[32,2048]{1,0:T(8,128)(2,1)S(1)}, bf16[32,2048]{1,0:T(8,128)(2,1)S(1)}, u32[]{:S(2)}, u32[]{:S(2)}) collective-permute-start(bf16[32,2048]{1,0:T(8,128)(2,1)S(1)} %get-tuple-element.39), channel_id=1, source_target_pairs={{0,2},{1,3},{2,0},{3,1},{4,6},{5,7},{6,4},{7,5},{8,10},{9,11},{10,... | collective-permute-start | bytes 393224 | tf_op jit(solution)/shard_map/ppermute | solution.py:146
  40.9 0.0 collective-permute-done.11
  41.0 0.1 collective-permute-start.12
  41.0 0.0 collective-permute-done.16.other_f
  41.1 1.7 %shard_map.83 = (f32[32,2048]{1,0:T(8,128)S(1)}, bf16[32,2048]{1,0:T(8,128)(2,1)S(1)}, f32[32,128]{1,0:T(8,128)S(1)}) custom-call(s32[4]{0:T(128)S(1)} %pad_add_fusion.place, bf16[32,2048]{1,0:T(8,128)(2,1)S(1)} %collective-permute-done.15.own_f, bf16[32,2048]{1,0:T(8,128)(2,1)S(1)} %collective-permute-done.16.other_f, ...), custom_call_target="tpu_custom_call" | custom-call | flops 100663296 | bytes 1572864 | tf_op jit(solution)/shard_map/pallas_call | solution.py:111
  42.8 1.1 %collective-permute-start.17 = (bf16[32,2048]{1,0:T(8,128)(2,1)S(1)}, bf16[32,2048]{1,0:T(8,128)(2,1)S(1)}, u32[]{:S(2)}, u32[]{:S(2)}) collective-permute-start(bf16[32,2048]{1,0:T(8,128)(2,1)S(1)} %get-tuple-element.43), channel_id=1, source_target_pairs={{0,2},{1,3},{2,0},{3,1},{4,6},{5,7},{6,4},{7,5},{8,10},{9,11},{10,... | collective-permute-start | bytes 393224 | tf_op jit(solution)/shard_map/ppermute | solution.py:146
  43.9 3.8 %collective-permute-done.13 = bf16[32,2048]{1,0:T(8,128)(2,1)S(1)} collective-permute-done((bf16[32,2048]{1,0:T(8,128)(2,1)S(1)}, bf16[32,2048]{1,0:T(8,128)(2,1)S(1)}, u32[]{:S(2)}, u32[]{:S(2)}) %collective-permute-start.13) | collective-permute-done | bytes 131104 | tf_op jit(solution)/shard_map/ppermute | solution.py:146
  47.7 2.7 %collective-permute-start.14 = (bf16[32,2048]{1,0:T(8,128)(2,1)S(1)}, bf16[32,2048]{1,0:T(8,128)(2,1)S(1)}, u32[]{:S(2)}, u32[]{:S(2)}) collective-permute-start(bf16[32,2048]{1,0:T(8,128)(2,1)S(1)} %add_convert_fusion.1), channel_id=1, source_target_pairs={{0,12},{1,13},{2,14},{3,15},{4,0},{5,1},{6,2},{7,3},{8,4},{9,5},{1... | collective-permute-start | bytes 393224 | tf_op jit(solution)/shard_map/ppermute | solution.py:146
  50.4 0.1 collective-permute-done.17
  50.5 0.9 %collective-permute-start.18 = (bf16[32,2048]{1,0:T(8,128)(2,1)S(1)}, bf16[32,2048]{1,0:T(8,128)(2,1)S(1)}, u32[]{:S(2)}, u32[]{:S(2)}) collective-permute-start(bf16[32,2048]{1,0:T(8,128)(2,1)S(1)} %add_convert_fusion), channel_id=1, source_target_pairs={{0,4},{1,5},{2,6},{3,7},{4,8},{5,9},{6,10},{7,11},{8,12},{9,13},{1... | collective-permute-start | bytes 393224 | tf_op jit(solution)/shard_map/ppermute | solution.py:146
  51.5 0.1 slice.9
  51.5 3.1 %collective-permute-start.21 = (f32[32,64]{1,0:T(8,128)S(1)}, f32[32,64]{1,0:T(8,128)S(1)}, u32[]{:S(2)}, u32[]{:S(2)}) collective-permute-start(f32[32,64]{1,0:T(8,128)S(1)} %slice.9), channel_id=1, source_target_pairs={{0,1},{1,0},{2,3},{3,2},{4,5},{5,4},{6,7},{7,6},{8,9},{9,8},{10,11... | collective-permute-start | bytes 24584 | tf_op jit(solution)/shard_map/ppermute | solution.py:146
  54.7 0.0 collective-permute-done.8
  54.7 0.0 collective-permute-done.12
  54.7 0.0 collective-permute-done.14
  54.7 2.7 %collective-permute-done.18 = bf16[32,2048]{1,0:T(8,128)(2,1)S(1)} collective-permute-done((bf16[32,2048]{1,0:T(8,128)(2,1)S(1)}, bf16[32,2048]{1,0:T(8,128)(2,1)S(1)}, u32[]{:S(2)}, u32[]{:S(2)}) %collective-permute-start.18) | collective-permute-done | bytes 131104 | tf_op jit(solution)/shard_map/ppermute | solution.py:146
  57.4 0.1 fusion.1
  57.5 4.0 %collective-permute-start.19 = (bf16[32,2048]{1,0:T(8,128)(2,1)S(1)}, bf16[32,2048]{1,0:T(8,128)(2,1)S(1)}, u32[]{:S(2)}, u32[]{:S(2)}) collective-permute-start(bf16[32,2048]{1,0:T(8,128)(2,1)S(1)} %get-tuple-element.46), channel_id=1, source_target_pairs={{0,1},{1,0},{2,3},{3,2},{4,5},{5,4},{6,7},{7,6},{8,9},{9,8},{10,11... | collective-permute-start | bytes 393224 | tf_op jit(solution)/shard_map/ppermute | solution.py:146
  61.5 3.5 %collective-permute-start.20 = (bf16[32,2048]{1,0:T(8,128)(2,1)S(1)}, bf16[32,2048]{1,0:T(8,128)(2,1)S(1)}, u32[]{:S(2)}, u32[]{:S(2)}) collective-permute-start(bf16[32,2048]{1,0:T(8,128)(2,1)S(1)} %get-tuple-element.46), channel_id=1, source_target_pairs={{1,2},{2,1},{3,4},{4,3},{5,6},{6,5},{7,8},{8,7},{9,10},{10,9},{11,... | collective-permute-start | bytes 393224 | tf_op jit(solution)/shard_map/ppermute | solution.py:152
  65.0 0.0 collective-permute-done.21
  65.1 0.6 fusion
  65.7 0.0 collective-permute-done.19.near_ref
  65.7 2.1 %collective-permute-done.20.far_ref = bf16[32,2048]{1,0:T(8,128)(2,1)S(1)} collective-permute-done((bf16[32,2048]{1,0:T(8,128)(2,1)S(1)}, bf16[32,2048]{1,0:T(8,128)(2,1)S(1)}, u32[]{:S(2)}, u32[]{:S(2)}) %collective-permute-start.20) | collective-permute-done | bytes 131104 | tf_op jit(solution)/shard_map/ppermute | solution.py:152
  67.8 0.9 %shard_map.84 = f32[32,2048]{1,0:T(8,128)} custom-call(f32[32,2048]{1,0:T(8,128)S(1)} %get-tuple-element.47.own_ref, bf16[32,2048]{1,0:T(8,128)(2,1)S(1)} %collective-permute-done.19.near_ref, bf16[32,2048]{1,0:T(8,128)(2,1)S(1)} %collective-permute-done.20.far_ref, f32[1,32]{1,0:T(1,128)S(1)} %bitcast.10), custom_call_target="tpu_custom_call" | custom-call | flops 655360 | bytes 786432 | tf_op jit(solution)/shard_map/pallas_call | solution.py:203
  (8 shorter events, 0.1 us)
Async XLA Ops:
  0.7 3.4 %copy-start = (s32[64,32768]{1,0:T(8,128)S(1)}, s32[64,32768]{1,0:T(8,128)}, u32[]{:S(2)}) copy-start(s32[64,32768]{1,0:T(8,128)} %counts_ref.3) | copy-start | bytes 25165828
  4.1 1.3 %copy-start.1 = (f32[32,2048]{1,0:T(8,128)S(1)}, f32[32,2048]{1,0:T(8,128)}, u32[]{:S(2)}) copy-start(f32[32,2048]{1,0:T(8,128)} %latent_ref.1) | copy-start | bytes 786436
  4.1 6.3 %copy-start.3 = (bf16[32,64]{1,0:T(8,128)(2,1)S(1)}, bf16[32,64]{1,0:T(8,128)(2,1)}, u32[]{:S(2)}) copy-start(bf16[32,64]{1,0:T(8,128)(2,1)} %own_w.1) | copy-start | bytes 12292
  4.1 6.4 %copy-start.5 = (f32[64]{0:T(128)S(1)}, f32[64]{0:T(128)}, u32[]{:S(2)}) copy-start(f32[64]{0:T(128)} %param.9) | copy-start | bytes 772
  4.1 12.4 %copy-start.2 = (s32[32768]{0:T(1024)S(1)}, s32[32768]{0:T(1024)}, u32[]{:S(2)}) copy-start(s32[32768]{0:T(1024)} %param.11) | copy-start | bytes 393220
  4.1 12.4 %copy-start.4 = (f32[32]{0:T(128)S(1)}, f32[32]{0:T(128)}, u32[]{:S(2)}) copy-start(f32[32]{0:T(128)} %param.10) | copy-start | bytes 388
  5.3 18.1 %collective-permute-start.5 = (bf16[4,2,64,2048]{3,2,1,0:T(8,128)(2,1)S(1)}, bf16[4,2,64,2048]{3,2,1,0:T(8,128)(2,1)S(1)}, u32[]{:S(2)}, u32[]{:S(2)}) collective-permute-start(bf16[4,2,64,2048]{3,2,1,0:T(8,128)(2,1)S(1)} %shard_map.79), channel_id=1, source_target_pairs={{0,1},{1,0},{2,3},{3,2},{4,5},{5,4},{6,7},{7,6},{8,9},{9,8},{10,11... | collective-permute-start | bytes 6291464 | tf_op jit(solution)/shard_map/ppermute | solution.py:146
  5.4 6.4 %collective-permute-start = (f32[32,2048]{1,0:T(8,128)S(1)}, f32[32,2048]{1,0:T(8,128)S(1)}, u32[]{:S(2)}, u32[]{:S(2)}) collective-permute-start(f32[32,2048]{1,0:T(8,128)S(1)} %copy-done.1), channel_id=1, source_target_pairs={{0,1},{1,0},{2,3},{3,2},{4,5},{5,4},{6,7},{7,6},{8,9},{9,8},{10,11... | collective-permute-start | bytes 786440 | tf_op jit(solution)/shard_map/ppermute | solution.py:146
  5.9 10.6 %collective-permute-start.1 = (f32[32,2048]{1,0:T(8,128)S(1)}, f32[32,2048]{1,0:T(8,128)S(1)}, u32[]{:S(2)}, u32[]{:S(2)}) collective-permute-start(f32[32,2048]{1,0:T(8,128)S(1)} %copy-done.1), channel_id=1, source_target_pairs={{1,2},{2,1},{3,4},{4,3},{5,6},{6,5},{7,8},{8,7},{9,10},{10,9},{11,... | collective-permute-start | bytes 786440 | tf_op jit(solution)/shard_map/ppermute | solution.py:152
  10.4 1.4 %collective-permute-start.2 = (bf16[32,64]{1,0:T(8,128)(2,1)S(1)}, bf16[32,64]{1,0:T(8,128)(2,1)S(1)}, u32[]{:S(2)}, u32[]{:S(2)}) collective-permute-start(bf16[32,64]{1,0:T(8,128)(2,1)S(1)} %copy-done.3), channel_id=1, source_target_pairs={{0,1},{1,0},{2,3},{3,2},{4,5},{5,4},{6,7},{7,6},{8,9},{9,8},{10,11... | collective-permute-start | bytes 12296 | tf_op jit(solution)/shard_map/ppermute | solution.py:146
  10.5 1.3 %collective-permute-start.3 = (f32[64]{0:T(128)S(1)}, f32[64]{0:T(128)S(1)}, u32[]{:S(2)}, u32[]{:S(2)}) collective-permute-start(f32[64]{0:T(128)S(1)} %copy-done.5), channel_id=1, source_target_pairs={{0,1},{1,0},{2,3},{3,2},{4,5},{5,4},{6,7},{7,6},{8,9},{9,8},{10,11... | collective-permute-start | bytes 776 | tf_op jit(solution)/shard_map/ppermute | solution.py:146
  17.6 5.8 %collective-permute-start.4 = (bf16[32,2048]{1,0:T(8,128)(2,1)S(1)}, bf16[32,2048]{1,0:T(8,128)(2,1)S(1)}, u32[]{:S(2)}, u32[]{:S(2)}) collective-permute-start(bf16[32,2048]{1,0:T(8,128)(2,1)S(1)} %get-tuple-element.24.own_f), channel_id=1, source_target_pairs={{0,2},{1,3},{2,0},{3,1},{4,6},{5,7},{6,4},{7,5},{8,10},{9,11},{10,... | collective-permute-start | bytes 393224 | tf_op jit(solution)/shard_map/ppermute | solution.py:146
  18.0 7.2 %collective-permute-start.9 = (bf16[32,2048]{1,0:T(8,128)(2,1)S(1)}, bf16[32,2048]{1,0:T(8,128)(2,1)S(1)}, u32[]{:S(2)}, u32[]{:S(2)}) collective-permute-start(bf16[32,2048]{1,0:T(8,128)(2,1)S(1)} %get-tuple-element.24.own_f), channel_id=1, source_target_pairs={{0,8},{1,9},{2,10},{3,11},{4,12},{5,13},{6,14},{7,15},{8,0},{9,1},... | collective-permute-start | bytes 393224 | tf_op jit(solution)/shard_map/ppermute | solution.py:146
  20.9 11.3 %collective-permute-start.6 = (bf16[32,2048]{1,0:T(8,128)(2,1)S(1)}, bf16[32,2048]{1,0:T(8,128)(2,1)S(1)}, u32[]{:S(2)}, u32[]{:S(2)}) collective-permute-start(bf16[32,2048]{1,0:T(8,128)(2,1)S(1)} %get-tuple-element.24.own_f), channel_id=1, source_target_pairs={{0,4},{1,5},{2,6},{3,7},{4,8},{5,9},{6,10},{7,11},{8,12},{9,13},{1... | collective-permute-start | bytes 393224 | tf_op jit(solution)/shard_map/ppermute | solution.py:146
  25.2 8.4 %collective-permute-start.10 = (bf16[32,2048]{1,0:T(8,128)(2,1)S(1)}, bf16[32,2048]{1,0:T(8,128)(2,1)S(1)}, u32[]{:S(2)}, u32[]{:S(2)}) collective-permute-start(bf16[32,2048]{1,0:T(8,128)(2,1)S(1)} %collective-permute-done.9.own_f), channel_id=1, source_target_pairs={{0,2},{1,3},{2,0},{3,1},{4,6},{5,7},{6,4},{7,5},{8,10},{9,11},{10,... | collective-permute-start | bytes 393224 | tf_op jit(solution)/shard_map/ppermute | solution.py:146
  31.2 5.6 %collective-permute-start.15 = (bf16[32,2048]{1,0:T(8,128)(2,1)S(1)}, bf16[32,2048]{1,0:T(8,128)(2,1)S(1)}, u32[]{:S(2)}, u32[]{:S(2)}) collective-permute-start(bf16[32,2048]{1,0:T(8,128)(2,1)S(1)} %get-tuple-element.24.own_f), channel_id=1, source_target_pairs={{0,12},{1,13},{2,14},{3,15},{4,0},{5,1},{6,2},{7,3},{8,4},{9,5},{1... | collective-permute-start | bytes 393224 | tf_op jit(solution)/shard_map/ppermute | solution.py:146
  32.2 5.5 %collective-permute-start.7 = (bf16[32,2048]{1,0:T(8,128)(2,1)S(1)}, bf16[32,2048]{1,0:T(8,128)(2,1)S(1)}, u32[]{:S(2)}, u32[]{:S(2)}) collective-permute-start(bf16[32,2048]{1,0:T(8,128)(2,1)S(1)} %collective-permute-done.6.own_f), channel_id=1, source_target_pairs={{0,2},{1,3},{2,0},{3,1},{4,6},{5,7},{6,4},{7,5},{8,10},{9,11},{10,... | collective-permute-start | bytes 393224 | tf_op jit(solution)/shard_map/ppermute | solution.py:146
  35.3 5.6 %collective-permute-start.11 = (bf16[32,2048]{1,0:T(8,128)(2,1)S(1)}, bf16[32,2048]{1,0:T(8,128)(2,1)S(1)}, u32[]{:S(2)}, u32[]{:S(2)}) collective-permute-start(bf16[32,2048]{1,0:T(8,128)(2,1)S(1)} %get-tuple-element.37), channel_id=1, source_target_pairs={{0,2},{1,3},{2,0},{3,1},{4,6},{5,7},{6,4},{7,5},{8,10},{9,11},{10,... | collective-permute-start | bytes 393224 | tf_op jit(solution)/shard_map/ppermute | solution.py:146
  36.8 4.2 %collective-permute-start.16 = (bf16[32,2048]{1,0:T(8,128)(2,1)S(1)}, bf16[32,2048]{1,0:T(8,128)(2,1)S(1)}, u32[]{:S(2)}, u32[]{:S(2)}) collective-permute-start(bf16[32,2048]{1,0:T(8,128)(2,1)S(1)} %collective-permute-done.15.own_f), channel_id=1, source_target_pairs={{0,2},{1,3},{2,0},{3,1},{4,6},{5,7},{6,4},{7,5},{8,10},{9,11},{10,... | collective-permute-start | bytes 393224 | tf_op jit(solution)/shard_map/ppermute | solution.py:146
  39.4 15.3 %collective-permute-start.8 = (bf16[32,2048]{1,0:T(8,128)(2,1)S(1)}, bf16[32,2048]{1,0:T(8,128)(2,1)S(1)}, u32[]{:S(2)}, u32[]{:S(2)}) collective-permute-start(bf16[32,2048]{1,0:T(8,128)(2,1)S(1)} %get-tuple-element.34), channel_id=1, source_target_pairs={{0,2},{1,3},{2,0},{3,1},{4,6},{5,7},{6,4},{7,5},{8,10},{9,11},{10,... | collective-permute-start | bytes 393224 | tf_op jit(solution)/shard_map/ppermute | solution.py:146
  40.1 7.6 %collective-permute-start.13 = (bf16[32,2048]{1,0:T(8,128)(2,1)S(1)}, bf16[32,2048]{1,0:T(8,128)(2,1)S(1)}, u32[]{:S(2)}, u32[]{:S(2)}) collective-permute-start(bf16[32,2048]{1,0:T(8,128)(2,1)S(1)} %get-tuple-element.39), channel_id=1, source_target_pairs={{0,2},{1,3},{2,0},{3,1},{4,6},{5,7},{6,4},{7,5},{8,10},{9,11},{10,... | collective-permute-start | bytes 393224 | tf_op jit(solution)/shard_map/ppermute | solution.py:146
  41.0 13.7 %collective-permute-start.12 = (bf16[32,2048]{1,0:T(8,128)(2,1)S(1)}, bf16[32,2048]{1,0:T(8,128)(2,1)S(1)}, u32[]{:S(2)}, u32[]{:S(2)}) collective-permute-start(bf16[32,2048]{1,0:T(8,128)(2,1)S(1)} %add_convert_fusion.2), channel_id=1, source_target_pairs={{0,8},{1,9},{2,10},{3,11},{4,12},{5,13},{6,14},{7,15},{8,0},{9,1},... | collective-permute-start | bytes 393224 | tf_op jit(solution)/shard_map/ppermute | solution.py:146
  42.8 7.7 %collective-permute-start.17 = (bf16[32,2048]{1,0:T(8,128)(2,1)S(1)}, bf16[32,2048]{1,0:T(8,128)(2,1)S(1)}, u32[]{:S(2)}, u32[]{:S(2)}) collective-permute-start(bf16[32,2048]{1,0:T(8,128)(2,1)S(1)} %get-tuple-element.43), channel_id=1, source_target_pairs={{0,2},{1,3},{2,0},{3,1},{4,6},{5,7},{6,4},{7,5},{8,10},{9,11},{10,... | collective-permute-start | bytes 393224 | tf_op jit(solution)/shard_map/ppermute | solution.py:146
  47.7 7.0 %collective-permute-start.14 = (bf16[32,2048]{1,0:T(8,128)(2,1)S(1)}, bf16[32,2048]{1,0:T(8,128)(2,1)S(1)}, u32[]{:S(2)}, u32[]{:S(2)}) collective-permute-start(bf16[32,2048]{1,0:T(8,128)(2,1)S(1)} %add_convert_fusion.1), channel_id=1, source_target_pairs={{0,12},{1,13},{2,14},{3,15},{4,0},{5,1},{6,2},{7,3},{8,4},{9,5},{1... | collective-permute-start | bytes 393224 | tf_op jit(solution)/shard_map/ppermute | solution.py:146
  50.5 6.8 %collective-permute-start.18 = (bf16[32,2048]{1,0:T(8,128)(2,1)S(1)}, bf16[32,2048]{1,0:T(8,128)(2,1)S(1)}, u32[]{:S(2)}, u32[]{:S(2)}) collective-permute-start(bf16[32,2048]{1,0:T(8,128)(2,1)S(1)} %add_convert_fusion), channel_id=1, source_target_pairs={{0,4},{1,5},{2,6},{3,7},{4,8},{5,9},{6,10},{7,11},{8,12},{9,13},{1... | collective-permute-start | bytes 393224 | tf_op jit(solution)/shard_map/ppermute | solution.py:146
  51.5 13.5 %collective-permute-start.21 = (f32[32,64]{1,0:T(8,128)S(1)}, f32[32,64]{1,0:T(8,128)S(1)}, u32[]{:S(2)}, u32[]{:S(2)}) collective-permute-start(f32[32,64]{1,0:T(8,128)S(1)} %slice.9), channel_id=1, source_target_pairs={{0,1},{1,0},{2,3},{3,2},{4,5},{5,4},{6,7},{7,6},{8,9},{9,8},{10,11... | collective-permute-start | bytes 24584 | tf_op jit(solution)/shard_map/ppermute | solution.py:146
  57.5 8.2 %collective-permute-start.19 = (bf16[32,2048]{1,0:T(8,128)(2,1)S(1)}, bf16[32,2048]{1,0:T(8,128)(2,1)S(1)}, u32[]{:S(2)}, u32[]{:S(2)}) collective-permute-start(bf16[32,2048]{1,0:T(8,128)(2,1)S(1)} %get-tuple-element.46), channel_id=1, source_target_pairs={{0,1},{1,0},{2,3},{3,2},{4,5},{5,4},{6,7},{7,6},{8,9},{9,8},{10,11... | collective-permute-start | bytes 393224 | tf_op jit(solution)/shard_map/ppermute | solution.py:146
  61.5 6.3 %collective-permute-start.20 = (bf16[32,2048]{1,0:T(8,128)(2,1)S(1)}, bf16[32,2048]{1,0:T(8,128)(2,1)S(1)}, u32[]{:S(2)}, u32[]{:S(2)}) collective-permute-start(bf16[32,2048]{1,0:T(8,128)(2,1)S(1)} %get-tuple-element.46), channel_id=1, source_target_pairs={{1,2},{2,1},{3,4},{4,3},{5,6},{6,5},{7,8},{8,7},{9,10},{10,9},{11,... | collective-permute-start | bytes 393224 | tf_op jit(solution)/shard_map/ppermute | solution.py:152

commit v3 on v2

--- a/solution.py
+++ b/solution.py
@@ -89,7 +89,7 @@
     weights, turned = weight_ref[...], turned_ref[...]
     offset = jnp.concatenate([back_ref[...]] * (step // 128), axis=1)
     load = jnp.zeros(load_p.shape, jnp.float32)
-    plane = lax.rem(place[2] + planes - shift, planes)
+    plane = place[2] ^ shift
     for half, (field, out) in enumerate(((own_f, own_p), (other_f, other_p))):
         row = lax.rem(place[1] + half, 2)
         for at in range(0, width, step):
@@ -153,13 +153,13 @@
 
     over_core = lambda i: i ^ 1
     over_row = lambda i: i ^ 2
-    along = lambda s: lambda i: (i + 4 * s) % count
+    along = lambda s: lambda i: i ^ (4 * s)
 
     far = chips(latent)
     near = send(latent, over_core)
     away = cast_counts(place, counts, planes, width, 1)
+    keep = cast_counts(place, counts, planes, width, 0)
     other_w, other_b = send(loading, over_core), send(background, over_core)
-    came = send(away, over_core)
     strength = coupling.reshape(1, factors)
     full = jax.ShapeDtypeStruct
     field, slope, weights, turned, back = pl.pallas_call(
@@ -178,8 +178,8 @@
         loading, other_w, background.reshape(1, genes), other_b.reshape(1, genes),
     )
 
-    keep = cast_counts(after(place, field), counts, planes, width, 0)
-    order = [0] + sorted(range(1, planes), key=lambda s: -min(s, planes - s))
+    came = send(after(away, field), over_core)
+    order = [0, 3, 1, 2]
     fields = {s: field if s == 0 else send(field, along(s)) for s in order}
     total = loads = None
     done, returned = [], []
@@ -193,7 +193,7 @@
             total, later = own_p, other_p
         else:
             summed = own_p + send(other_p, over_row).astype(jnp.float32)
-            returned.append(send(summed.astype(jnp.bfloat16), along(-s)))
+            returned.append(send(summed.astype(jnp.bfloat16), along(s)))
     total = total + send(after(later, done[-2]), over_row).astype(jnp.float32)
     for r in returned:
         total = total + r.astype(jnp.float32)
@@ -208,7 +208,7 @@
         compiler_params=params(8),
         cost_estimate=cost(latent.size * 10, latent.size * 12),
     )(grad_smooth, near2, far2, strength)
-    swapped = send(loads[:, genes:], over_core)
+    swapped = send(after(loads, grad_smooth)[:, genes:], over_core)
     grad_loading = (loads[:, :genes] + swapped) / total_spots
     return grad_latent, grad_loading
 

time: 69.5 us -> 63.1 us (0.908)
  starting transfers between devices: 36.3 us -> 29.5 us
    ppermute x20, starting transfers between devices: 28.2 us -> 19.9 us  [send(): return lax.ppermute(x, SPACE, [(i, to(i)) for i in range(count)])]
    ppermute x20, waiting for transfers between devices: 9.34 us -> 13.5 us  [send(): return lax.ppermute(x, SPACE, [(i, to(i)) for i in range(count)])]
    ppermute x2, waiting for transfers between devices: 6.78 us -> 3.18 us  [chips(): lax.ppermute(x, SPACE, [(i, across(i)) for i in range(count) if 0 <= acro...]
    ppermute x2, starting transfers between devices: 8.07 us -> 9.59 us  [chips(): lax.ppermute(x, SPACE, [(i, across(i)) for i in range(count) if 0 <= acro...]
  transfers between devices with their start and end apart: 22 -> 22, of which waited for: 8 -> 9; matrix products, arithmetic and copies ran while one was open for 1% -> 1% of each run, Pallas kernels for 13% -> 15%
where the time goes in v3:
time: 63.1 us; the launch traced here: 62.4 us
  starting transfers between devices  29.5 us (47%)
  waiting for transfers between devices  16.7 us (26%)
  Pallas kernels  11.1 us (18%)
  local copies, waits for them, and re-layouts  3.48 us (6%)
  between operations  0.88 us (1%)
  other arithmetic  0.87 us (1%)
    ppermute x20, starting transfers between devices, send(): return lax.ppermute(x, SPACE, [(i, to(i)) for i in range(count)])  19.9 us
    ppermute x20, waiting for transfers between devices, send(): return lax.ppermute(x, SPACE, [(i, to(i)) for i in range(count)])  13.5 us
    ppermute x2, starting transfers between devices, chips(): lax.ppermute(x, SPACE, [(i, across(i)) for i in range(count) if 0 <= acro...  9.59 us
    pallas_call x4, Pallas kernels, gene_sums(): pl.pallas_call(functools.partial(gene_kernel, step=1024, shift=shift), in...  6.8 us
    unnamed x12, local copies, waits for them, and re-layouts  3.4 us
    ppermute x2, waiting for transfers between devices, chips(): lax.ppermute(x, SPACE, [(i, across(i)) for i in range(count) if 0 <= acro...  3.18 us
    pallas_call x2, Pallas kernels, cast_counts(): pl.pallas_call(functools.partial(cast_kernel, turn=turn), in_specs=[SMEM,...  2.3 us
  transfers between devices with their start and end apart: 22, of which 9 were waited for; matrix products, arithmetic and copies ran while one was open for 1% of the time, Pallas kernels for 15%

profile of v3, /device:TPU:1, one launch (start us, length us, event | category | flops | bytes accessed | tf_op | source)
XLA Modules:
  0.0 62.4 jit_solution(18409876105658335158)
XLA Ops:
  0.6 0.1 collective-permute-start
  0.8 4.5 %collective-permute-start.1 = (f32[32,2048]{1,0:T(8,128)}, f32[32,2048]{1,0:T(8,128)S(1)}, u32[]{:S(2)}, u32[]{:S(2)}) collective-permute-start(f32[32,2048]{1,0:T(8,128)} %latent_ref.1), channel_id=1, source_target_pairs={{1,2},{2,1},{3,4},{4,3},{5,6},{6,5},{7,8},{8,7},{9,10},{10,9},{11,... | collective-permute-start | bytes 786440 | tf_op jit(solution)/shard_map/ppermute | solution.py:152
  5.3 0.1 collective-permute-start.2
  5.3 0.5 collective-permute-start.3
  5.8 0.1 pad_add_fusion.place
  5.9 0.0 copy-start
  5.9 3.4 %copy-done = s32[64,32768]{1,0:T(8,128)S(1)} copy-done((s32[64,32768]{1,0:T(8,128)S(1)}, s32[64,32768]{1,0:T(8,128)}, u32[]{:S(2)}) %copy-start) | copy-done | bytes 8388632
  9.3 0.0 copy-start.5
  9.3 1.2 %shard_map.79 = bf16[4,2,64,2048]{3,2,1,0:T(8,128)(2,1)S(1)} custom-call(s32[4]{0:T(128)S(1)} %pad_add_fusion.place, s32[64,32768]{1,0:T(8,128)S(1)} %copy-done), custom_call_target="tpu_custom_call" | custom-call | flops 2097152 | bytes 6291456 | tf_op jit(solution)/shard_map/pallas_call | solution.py:39
  10.5 0.0 collective-permute-done.3
  10.5 0.0 collective-permute-done.2.other_w
  10.5 0.0 collective-permute-done.near_ref
  10.5 1.2 %collective-permute-done.1.far_ref = f32[32,2048]{1,0:T(8,128)S(1)} collective-permute-done((f32[32,2048]{1,0:T(8,128)}, f32[32,2048]{1,0:T(8,128)S(1)}, u32[]{:S(2)}, u32[]{:S(2)}) %collective-permute-start.1) | collective-permute-done | bytes 262176 | tf_op jit(solution)/shard_map/ppermute | solution.py:152
  11.7 0.0 copy-done.1
  11.7 0.0 copy-done.2
  11.7 0.0 copy-done.3
  11.7 0.0 copy-done.4
  11.7 0.0 copy-done.5
  11.7 1.1 %shard_map.77 = (bf16[32,2048]{1,0:T(8,128)(2,1)S(1)}, f32[32,2048]{1,0:T(8,128)S(1)}, bf16[32,128]{1,0:T(8,128)(2,1)S(1)}, bf16[128,32]{1,0:T(8,128)(2,1)S(1)}, f32[128,128]{1,0:T(8,128)S(1)}) custom-call(s32[4]{0:T(128)S(1)} %pad_add_fusion.place, f32[32,2048]{1,0:T(8,128)S(1)} %copy-done.1, f32[32,2048]{1,0:T(8,128)S(1)} %collective-permute-done.near_ref, ...), custom_call_target="tpu_custom_call" | custom-call | flops 1310720 | bytes 1179648 | tf_op jit(solution)/shard_map/pallas_call | solution.py:165
  12.8 0.1 collective-permute-start.5
  12.8 2.5 %collective-permute-start.4 = (bf16[32,2048]{1,0:T(8,128)(2,1)S(1)}, bf16[32,2048]{1,0:T(8,128)(2,1)S(1)}, u32[]{:S(2)}, u32[]{:S(2)}) collective-permute-start(bf16[32,2048]{1,0:T(8,128)(2,1)S(1)} %get-tuple-element.25.own_f), channel_id=1, source_target_pairs={{0,2},{1,3},{2,0},{3,1},{4,6},{5,7},{6,4},{7,5},{8,10},{9,11},{10,... | collective-permute-start | bytes 393224 | tf_op jit(solution)/shard_map/ppermute | solution.py:146
  15.3 2.2 %collective-permute-start.9 = (bf16[32,2048]{1,0:T(8,128)(2,1)S(1)}, bf16[32,2048]{1,0:T(8,128)(2,1)S(1)}, u32[]{:S(2)}, u32[]{:S(2)}) collective-permute-start(bf16[32,2048]{1,0:T(8,128)(2,1)S(1)} %get-tuple-element.25.own_f), channel_id=1, source_target_pairs={{0,12},{1,13},{2,14},{3,15},{4,8},{5,9},{6,10},{7,11},{8,4},{9,5},... | collective-permute-start | bytes 393224 | tf_op jit(solution)/shard_map/ppermute | solution.py:146
  17.5 1.1 %shard_map.78.keep_ref = bf16[4,2,64,2048]{3,2,1,0:T(8,128)(2,1)S(1)} custom-call(s32[4]{0:T(128)S(1)} %pad_add_fusion.place, s32[64,32768]{1,0:T(8,128)S(1)} %copy-done), custom_call_target="tpu_custom_call" | custom-call | flops 2097152 | bytes 6291456 | tf_op jit(solution)/shard_map/pallas_call | solution.py:39
  18.7 0.5 collective-permute-start.6
  19.1 0.0 collective-permute-done.4.other_f
  19.2 0.0 collective-permute-done.5.came_ref
  19.2 1.7 %shard_map.80 = (f32[32,2048]{1,0:T(8,128)S(1)}, bf16[32,2048]{1,0:T(8,128)(2,1)S(1)}, f32[32,128]{1,0:T(8,128)S(1)}) custom-call(s32[4]{0:T(128)S(1)} %pad_add_fusion.place, bf16[32,2048]{1,0:T(8,128)(2,1)S(1)} %get-tuple-element.25.own_f, bf16[32,2048]{1,0:T(8,128)(2,1)S(1)} %collective-permute-done.4.other_f, ...), custom_call_target="tpu_custom_call" | custom-call | flops 100663296 | bytes 1572864 | tf_op jit(solution)/shard_map/pallas_call | solution.py:111
  20.9 1.0 %collective-permute-done.9.own_f = bf16[32,2048]{1,0:T(8,128)(2,1)S(1)} collective-permute-done((bf16[32,2048]{1,0:T(8,128)(2,1)S(1)}, bf16[32,2048]{1,0:T(8,128)(2,1)S(1)}, u32[]{:S(2)}, u32[]{:S(2)}) %collective-permute-start.9) | collective-permute-done | bytes 131104 | tf_op jit(solution)/shard_map/ppermute | solution.py:146
  21.9 0.3 collective-permute-start.10
  22.2 3.0 %collective-permute-start.15 = (bf16[32,2048]{1,0:T(8,128)(2,1)S(1)}, bf16[32,2048]{1,0:T(8,128)(2,1)S(1)}, u32[]{:S(2)}, u32[]{:S(2)}) collective-permute-start(bf16[32,2048]{1,0:T(8,128)(2,1)S(1)} %get-tuple-element.25.own_f), channel_id=1, source_target_pairs={{0,8},{1,9},{2,10},{3,11},{4,12},{5,13},{6,14},{7,15},{8,0},{9,1},... | collective-permute-start | bytes 393224 | tf_op jit(solution)/shard_map/ppermute | solution.py:146
  25.2 0.1 collective-permute-done.6.own_f
  25.3 1.4 %collective-permute-start.7 = (bf16[32,2048]{1,0:T(8,128)(2,1)S(1)}, bf16[32,2048]{1,0:T(8,128)(2,1)S(1)}, u32[]{:S(2)}, u32[]{:S(2)}) collective-permute-start(bf16[32,2048]{1,0:T(8,128)(2,1)S(1)} %collective-permute-done.6.own_f), channel_id=1, source_target_pairs={{0,2},{1,3},{2,0},{3,1},{4,6},{5,7},{6,4},{7,5},{8,10},{9,11},{10,... | collective-permute-start | bytes 393224 | tf_op jit(solution)/shard_map/ppermute | solution.py:146
  26.7 0.0 collective-permute-done.10.other_f
  26.7 1.7 %shard_map.82 = (f32[32,2048]{1,0:T(8,128)S(1)}, bf16[32,2048]{1,0:T(8,128)(2,1)S(1)}, f32[32,128]{1,0:T(8,128)S(1)}) custom-call(s32[4]{0:T(128)S(1)} %pad_add_fusion.place, bf16[32,2048]{1,0:T(8,128)(2,1)S(1)} %collective-permute-done.9.own_f, bf16[32,2048]{1,0:T(8,128)(2,1)S(1)} %collective-permute-done.10.other_f, ...), custom_call_target="tpu_custom_call" | custom-call | flops 100663296 | bytes 1572864 | tf_op jit(solution)/shard_map/pallas_call | solution.py:111
  28.4 0.2 collective-permute-start.11
  28.5 0.8 %collective-permute-done.15.own_f = bf16[32,2048]{1,0:T(8,128)(2,1)S(1)} collective-permute-done((bf16[32,2048]{1,0:T(8,128)(2,1)S(1)}, bf16[32,2048]{1,0:T(8,128)(2,1)S(1)}, u32[]{:S(2)}, u32[]{:S(2)}) %collective-permute-start.15) | collective-permute-done | bytes 131104 | tf_op jit(solution)/shard_map/ppermute | solution.py:146
  29.4 2.9 %collective-permute-start.16 = (bf16[32,2048]{1,0:T(8,128)(2,1)S(1)}, bf16[32,2048]{1,0:T(8,128)(2,1)S(1)}, u32[]{:S(2)}, u32[]{:S(2)}) collective-permute-start(bf16[32,2048]{1,0:T(8,128)(2,1)S(1)} %collective-permute-done.15.own_f), channel_id=1, source_target_pairs={{0,2},{1,3},{2,0},{3,1},{4,6},{5,7},{6,4},{7,5},{8,10},{9,11},{10,... | collective-permute-start | bytes 393224 | tf_op jit(solution)/shard_map/ppermute | solution.py:146
  32.3 0.0 collective-permute-done.7.other_f
  32.3 1.7 %shard_map.81 = (f32[32,2048]{1,0:T(8,128)S(1)}, bf16[32,2048]{1,0:T(8,128)(2,1)S(1)}, f32[32,128]{1,0:T(8,128)S(1)}) custom-call(s32[4]{0:T(128)S(1)} %pad_add_fusion.place, bf16[32,2048]{1,0:T(8,128)(2,1)S(1)} %collective-permute-done.6.own_f, bf16[32,2048]{1,0:T(8,128)(2,1)S(1)} %collective-permute-done.7.other_f, ...), custom_call_target="tpu_custom_call" | custom-call | flops 100663296 | bytes 1572864 | tf_op jit(solution)/shard_map/pallas_call | solution.py:111
  34.0 0.1 collective-permute-start.8
  34.1 1.5 %collective-permute-start.13 = (bf16[32,2048]{1,0:T(8,128)(2,1)S(1)}, bf16[32,2048]{1,0:T(8,128)(2,1)S(1)}, u32[]{:S(2)}, u32[]{:S(2)}) collective-permute-start(bf16[32,2048]{1,0:T(8,128)(2,1)S(1)} %get-tuple-element.40), channel_id=1, source_target_pairs={{0,2},{1,3},{2,0},{3,1},{4,6},{5,7},{6,4},{7,5},{8,10},{9,11},{10,... | collective-permute-start | bytes 393224 | tf_op jit(solution)/shard_map/ppermute | solution.py:146
  35.5 0.0 collective-permute-done.11
  35.6 0.4 collective-permute-start.12
  36.0 0.0 collective-permute-done.16.other_f
  36.0 1.7 %shard_map.83 = (f32[32,2048]{1,0:T(8,128)S(1)}, bf16[32,2048]{1,0:T(8,128)(2,1)S(1)}, f32[32,128]{1,0:T(8,128)S(1)}) custom-call(s32[4]{0:T(128)S(1)} %pad_add_fusion.place, bf16[32,2048]{1,0:T(8,128)(2,1)S(1)} %collective-permute-done.15.own_f, bf16[32,2048]{1,0:T(8,128)(2,1)S(1)} %collective-permute-done.16.other_f, ...), custom_call_target="tpu_custom_call" | custom-call | flops 100663296 | bytes 1572864 | tf_op jit(solution)/shard_map/pallas_call | solution.py:111
  37.7 0.8 %collective-permute-start.17 = (bf16[32,2048]{1,0:T(8,128)(2,1)S(1)}, bf16[32,2048]{1,0:T(8,128)(2,1)S(1)}, u32[]{:S(2)}, u32[]{:S(2)}) collective-permute-start(bf16[32,2048]{1,0:T(8,128)(2,1)S(1)} %get-tuple-element.44), channel_id=1, source_target_pairs={{0,2},{1,3},{2,0},{3,1},{4,6},{5,7},{6,4},{7,5},{8,10},{9,11},{10,... | collective-permute-start | bytes 393224 | tf_op jit(solution)/shard_map/ppermute | solution.py:146
  38.5 3.4 %collective-permute-done.13 = bf16[32,2048]{1,0:T(8,128)(2,1)S(1)} collective-permute-done((bf16[32,2048]{1,0:T(8,128)(2,1)S(1)}, bf16[32,2048]{1,0:T(8,128)(2,1)S(1)}, u32[]{:S(2)}, u32[]{:S(2)}) %collective-permute-start.13) | collective-permute-done | bytes 131104 | tf_op jit(solution)/shard_map/ppermute | solution.py:146
  41.9 0.1 collective-permute-start.14
  42.0 2.7 %collective-permute-done.17 = bf16[32,2048]{1,0:T(8,128)(2,1)S(1)} collective-permute-done((bf16[32,2048]{1,0:T(8,128)(2,1)S(1)}, bf16[32,2048]{1,0:T(8,128)(2,1)S(1)}, u32[]{:S(2)}, u32[]{:S(2)}) %collective-permute-start.17) | collective-permute-done | bytes 131104 | tf_op jit(solution)/shard_map/ppermute | solution.py:146
  44.7 0.1 collective-permute-start.18
  44.8 0.0 collective-permute-done.8
  44.9 0.0 collective-permute-done.12
  44.9 1.3 %collective-permute-done.14 = bf16[32,2048]{1,0:T(8,128)(2,1)S(1)} collective-permute-done((bf16[32,2048]{1,0:T(8,128)(2,1)S(1)}, bf16[32,2048]{1,0:T(8,128)(2,1)S(1)}, u32[]{:S(2)}, u32[]{:S(2)}) %collective-permute-start.14) | collective-permute-done | bytes 131104 | tf_op jit(solution)/shard_map/ppermute | solution.py:146
  46.2 4.1 %collective-permute-done.18 = bf16[32,2048]{1,0:T(8,128)(2,1)S(1)} collective-permute-done((bf16[32,2048]{1,0:T(8,128)(2,1)S(1)}, bf16[32,2048]{1,0:T(8,128)(2,1)S(1)}, u32[]{:S(2)}, u32[]{:S(2)}) %collective-permute-start.18) | collective-permute-done | bytes 131104 | tf_op jit(solution)/shard_map/ppermute | solution.py:146
  50.2 0.1 fusion.1
  50.3 0.1 slice.7
  50.4 3.3 %collective-permute-start.21 = (f32[32,64]{1,0:T(8,128)S(1)}, f32[32,64]{1,0:T(8,128)S(1)}, u32[]{:S(2)}, u32[]{:S(2)}) collective-permute-start(f32[32,64]{1,0:T(8,128)S(1)} %slice.7), channel_id=1, source_target_pairs={{0,1},{1,0},{2,3},{3,2},{4,5},{5,4},{6,7},{7,6},{8,9},{9,8},{10,11... | collective-permute-start | bytes 24584 | tf_op jit(solution)/shard_map/ppermute | solution.py:146
  53.7 0.1 collective-permute-start.19
  53.8 5.1 %collective-permute-start.20 = (bf16[32,2048]{1,0:T(8,128)(2,1)S(1)}, bf16[32,2048]{1,0:T(8,128)(2,1)S(1)}, u32[]{:S(2)}, u32[]{:S(2)}) collective-permute-start(bf16[32,2048]{1,0:T(8,128)(2,1)S(1)} %get-tuple-element.48), channel_id=1, source_target_pairs={{1,2},{2,1},{3,4},{4,3},{5,6},{6,5},{7,8},{8,7},{9,10},{10,9},{11,... | collective-permute-start | bytes 393224 | tf_op jit(solution)/shard_map/ppermute | solution.py:152
  58.9 0.0 collective-permute-done.21
  58.9 0.6 fusion
  59.5 0.0 collective-permute-done.19.near_ref
  59.5 2.0 %collective-permute-done.20.far_ref = bf16[32,2048]{1,0:T(8,128)(2,1)S(1)} collective-permute-done((bf16[32,2048]{1,0:T(8,128)(2,1)S(1)}, bf16[32,2048]{1,0:T(8,128)(2,1)S(1)}, u32[]{:S(2)}, u32[]{:S(2)}) %collective-permute-start.20) | collective-permute-done | bytes 131104 | tf_op jit(solution)/shard_map/ppermute | solution.py:152
  61.5 0.9 %shard_map.84 = f32[32,2048]{1,0:T(8,128)} custom-call(f32[32,2048]{1,0:T(8,128)S(1)} %get-tuple-element.49.own_ref, bf16[32,2048]{1,0:T(8,128)(2,1)S(1)} %collective-permute-done.19.near_ref, bf16[32,2048]{1,0:T(8,128)(2,1)S(1)} %collective-permute-done.20.far_ref, f32[1,32]{1,0:T(1,128)S(1)} %bitcast.10), custom_call_target="tpu_custom_call" | custom-call | flops 655360 | bytes 786432 | tf_op jit(solution)/shard_map/pallas_call | solution.py:203
  (8 shorter events, 0.1 us)
Async XLA Ops:
  0.6 9.9 %collective-permute-start = (f32[32,2048]{1,0:T(8,128)}, f32[32,2048]{1,0:T(8,128)S(1)}, u32[]{:S(2)}, u32[]{:S(2)}) collective-permute-start(f32[32,2048]{1,0:T(8,128)} %latent_ref.1), channel_id=1, source_target_pairs={{0,1},{1,0},{2,3},{3,2},{4,5},{5,4},{6,7},{7,6},{8,9},{9,8},{10,11... | collective-permute-start | bytes 786440 | tf_op jit(solution)/shard_map/ppermute | solution.py:146
  0.8 10.9 %collective-permute-start.1 = (f32[32,2048]{1,0:T(8,128)}, f32[32,2048]{1,0:T(8,128)S(1)}, u32[]{:S(2)}, u32[]{:S(2)}) collective-permute-start(f32[32,2048]{1,0:T(8,128)} %latent_ref.1), channel_id=1, source_target_pairs={{1,2},{2,1},{3,4},{4,3},{5,6},{6,5},{7,8},{8,7},{9,10},{10,9},{11,... | collective-permute-start | bytes 786440 | tf_op jit(solution)/shard_map/ppermute | solution.py:152
  5.3 5.2 %collective-permute-start.2 = (bf16[32,64]{1,0:T(8,128)(2,1)}, bf16[32,64]{1,0:T(8,128)(2,1)S(1)}, u32[]{:S(2)}, u32[]{:S(2)}) collective-permute-start(bf16[32,64]{1,0:T(8,128)(2,1)} %own_w.1), channel_id=1, source_target_pairs={{0,1},{1,0},{2,3},{3,2},{4,5},{5,4},{6,7},{7,6},{8,9},{9,8},{10,11... | collective-permute-start | bytes 12296 | tf_op jit(solution)/shard_map/ppermute | solution.py:146
  5.3 5.1 %collective-permute-start.3 = (f32[64]{0:T(128)}, f32[64]{0:T(128)S(1)}, u32[]{:S(2)}, u32[]{:S(2)}) collective-permute-start(f32[64]{0:T(128)} %param.9), channel_id=1, source_target_pairs={{0,1},{1,0},{2,3},{3,2},{4,5},{5,4},{6,7},{7,6},{8,9},{9,8},{10,11... | collective-permute-start | bytes 776 | tf_op jit(solution)/shard_map/ppermute | solution.py:146
  5.9 3.4 %copy-start = (s32[64,32768]{1,0:T(8,128)S(1)}, s32[64,32768]{1,0:T(8,128)}, u32[]{:S(2)}) copy-start(s32[64,32768]{1,0:T(8,128)} %counts_ref.3) | copy-start | bytes 25165828
  9.3 2.4 %copy-start.1 = (f32[32,2048]{1,0:T(8,128)S(1)}, f32[32,2048]{1,0:T(8,128)}, u32[]{:S(2)}) copy-start(f32[32,2048]{1,0:T(8,128)} %latent_ref.1) | copy-start | bytes 786436
  9.3 2.4 %copy-start.2 = (s32[32768]{0:T(1024)S(1)}, s32[32768]{0:T(1024)}, u32[]{:S(2)}) copy-start(s32[32768]{0:T(1024)} %param.11) | copy-start | bytes 393220
  9.3 2.4 %copy-start.3 = (bf16[32,64]{1,0:T(8,128)(2,1)S(1)}, bf16[32,64]{1,0:T(8,128)(2,1)}, u32[]{:S(2)}) copy-start(bf16[32,64]{1,0:T(8,128)(2,1)} %own_w.1) | copy-start | bytes 12292
  9.3 2.4 %copy-start.4 = (f32[32]{0:T(128)S(1)}, f32[32]{0:T(128)}, u32[]{:S(2)}) copy-start(f32[32]{0:T(128)} %param.10) | copy-start | bytes 388
  9.3 2.4 %copy-start.5 = (f32[64]{0:T(128)S(1)}, f32[64]{0:T(128)}, u32[]{:S(2)}) copy-start(f32[64]{0:T(128)} %param.9) | copy-start | bytes 772
  12.8 6.4 %collective-permute-start.5 = (bf16[4,2,64,2048]{3,2,1,0:T(8,128)(2,1)S(1)}, bf16[4,2,64,2048]{3,2,1,0:T(8,128)(2,1)S(1)}, u32[]{:S(2)}, u32[]{:S(2)}) collective-permute-start(bf16[4,2,64,2048]{3,2,1,0:T(8,128)(2,1)S(1)} %shard_map.79), channel_id=1, source_target_pairs={{0,1},{1,0},{2,3},{3,2},{4,5},{5,4},{6,7},{7,6},{8,9},{9,8},{10,11... | collective-permute-start | bytes 6291464 | tf_op jit(solution)/shard_map/ppermute | solution.py:146
  12.8 6.3 %collective-permute-start.4 = (bf16[32,2048]{1,0:T(8,128)(2,1)S(1)}, bf16[32,2048]{1,0:T(8,128)(2,1)S(1)}, u32[]{:S(2)}, u32[]{:S(2)}) collective-permute-start(bf16[32,2048]{1,0:T(8,128)(2,1)S(1)} %get-tuple-element.25.own_f), channel_id=1, source_target_pairs={{0,2},{1,3},{2,0},{3,1},{4,6},{5,7},{6,4},{7,5},{8,10},{9,11},{10,... | collective-permute-start | bytes 393224 | tf_op jit(solution)/shard_map/ppermute | solution.py:146
  15.3 6.6 %collective-permute-start.9 = (bf16[32,2048]{1,0:T(8,128)(2,1)S(1)}, bf16[32,2048]{1,0:T(8,128)(2,1)S(1)}, u32[]{:S(2)}, u32[]{:S(2)}) collective-permute-start(bf16[32,2048]{1,0:T(8,128)(2,1)S(1)} %get-tuple-element.25.own_f), channel_id=1, source_target_pairs={{0,12},{1,13},{2,14},{3,15},{4,8},{5,9},{6,10},{7,11},{8,4},{9,5},... | collective-permute-start | bytes 393224 | tf_op jit(solution)/shard_map/ppermute | solution.py:146
  18.7 6.6 %collective-permute-start.6 = (bf16[32,2048]{1,0:T(8,128)(2,1)S(1)}, bf16[32,2048]{1,0:T(8,128)(2,1)S(1)}, u32[]{:S(2)}, u32[]{:S(2)}) collective-permute-start(bf16[32,2048]{1,0:T(8,128)(2,1)S(1)} %get-tuple-element.25.own_f), channel_id=1, source_target_pairs={{0,4},{1,5},{2,6},{3,7},{4,0},{5,1},{6,2},{7,3},{8,12},{9,13},{10,... | collective-permute-start | bytes 393224 | tf_op jit(solution)/shard_map/ppermute | solution.py:146
  21.9 4.8 %collective-permute-start.10 = (bf16[32,2048]{1,0:T(8,128)(2,1)S(1)}, bf16[32,2048]{1,0:T(8,128)(2,1)S(1)}, u32[]{:S(2)}, u32[]{:S(2)}) collective-permute-start(bf16[32,2048]{1,0:T(8,128)(2,1)S(1)} %collective-permute-done.9.own_f), channel_id=1, source_target_pairs={{0,2},{1,3},{2,0},{3,1},{4,6},{5,7},{6,4},{7,5},{8,10},{9,11},{10,... | collective-permute-start | bytes 393224 | tf_op jit(solution)/shard_map/ppermute | solution.py:146
  22.2 7.2 %collective-permute-start.15 = (bf16[32,2048]{1,0:T(8,128)(2,1)S(1)}, bf16[32,2048]{1,0:T(8,128)(2,1)S(1)}, u32[]{:S(2)}, u32[]{:S(2)}) collective-permute-start(bf16[32,2048]{1,0:T(8,128)(2,1)S(1)} %get-tuple-element.25.own_f), channel_id=1, source_target_pairs={{0,8},{1,9},{2,10},{3,11},{4,12},{5,13},{6,14},{7,15},{8,0},{9,1},... | collective-permute-start | bytes 393224 | tf_op jit(solution)/shard_map/ppermute | solution.py:146
  25.3 7.0 %collective-permute-start.7 = (bf16[32,2048]{1,0:T(8,128)(2,1)S(1)}, bf16[32,2048]{1,0:T(8,128)(2,1)S(1)}, u32[]{:S(2)}, u32[]{:S(2)}) collective-permute-start(bf16[32,2048]{1,0:T(8,128)(2,1)S(1)} %collective-permute-done.6.own_f), channel_id=1, source_target_pairs={{0,2},{1,3},{2,0},{3,1},{4,6},{5,7},{6,4},{7,5},{8,10},{9,11},{10,... | collective-permute-start | bytes 393224 | tf_op jit(solution)/shard_map/ppermute | solution.py:146
  28.4 7.2 %collective-permute-start.11 = (bf16[32,2048]{1,0:T(8,128)(2,1)S(1)}, bf16[32,2048]{1,0:T(8,128)(2,1)S(1)}, u32[]{:S(2)}, u32[]{:S(2)}) collective-permute-start(bf16[32,2048]{1,0:T(8,128)(2,1)S(1)} %get-tuple-element.38), channel_id=1, source_target_pairs={{0,2},{1,3},{2,0},{3,1},{4,6},{5,7},{6,4},{7,5},{8,10},{9,11},{10,... | collective-permute-start | bytes 393224 | tf_op jit(solution)/shard_map/ppermute | solution.py:146
  29.4 6.7 %collective-permute-start.16 = (bf16[32,2048]{1,0:T(8,128)(2,1)S(1)}, bf16[32,2048]{1,0:T(8,128)(2,1)S(1)}, u32[]{:S(2)}, u32[]{:S(2)}) collective-permute-start(bf16[32,2048]{1,0:T(8,128)(2,1)S(1)} %collective-permute-done.15.own_f), channel_id=1, source_target_pairs={{0,2},{1,3},{2,0},{3,1},{4,6},{5,7},{6,4},{7,5},{8,10},{9,11},{10,... | collective-permute-start | bytes 393224 | tf_op jit(solution)/shard_map/ppermute | solution.py:146
  34.0 10.8 %collective-permute-start.8 = (bf16[32,2048]{1,0:T(8,128)(2,1)S(1)}, bf16[32,2048]{1,0:T(8,128)(2,1)S(1)}, u32[]{:S(2)}, u32[]{:S(2)}) collective-permute-start(bf16[32,2048]{1,0:T(8,128)(2,1)S(1)} %get-tuple-element.35), channel_id=1, source_target_pairs={{0,2},{1,3},{2,0},{3,1},{4,6},{5,7},{6,4},{7,5},{8,10},{9,11},{10,... | collective-permute-start | bytes 393224 | tf_op jit(solution)/shard_map/ppermute | solution.py:146
  34.1 7.8 %collective-permute-start.13 = (bf16[32,2048]{1,0:T(8,128)(2,1)S(1)}, bf16[32,2048]{1,0:T(8,128)(2,1)S(1)}, u32[]{:S(2)}, u32[]{:S(2)}) collective-permute-start(bf16[32,2048]{1,0:T(8,128)(2,1)S(1)} %get-tuple-element.40), channel_id=1, source_target_pairs={{0,2},{1,3},{2,0},{3,1},{4,6},{5,7},{6,4},{7,5},{8,10},{9,11},{10,... | collective-permute-start | bytes 393224 | tf_op jit(solution)/shard_map/ppermute | solution.py:146
  35.6 9.3 %collective-permute-start.12 = (bf16[32,2048]{1,0:T(8,128)(2,1)S(1)}, bf16[32,2048]{1,0:T(8,128)(2,1)S(1)}, u32[]{:S(2)}, u32[]{:S(2)}) collective-permute-start(bf16[32,2048]{1,0:T(8,128)(2,1)S(1)} %add_convert_fusion.2), channel_id=1, source_target_pairs={{0,12},{1,13},{2,14},{3,15},{4,8},{5,9},{6,10},{7,11},{8,4},{9,5},... | collective-permute-start | bytes 393224 | tf_op jit(solution)/shard_map/ppermute | solution.py:146
  37.7 7.0 %collective-permute-start.17 = (bf16[32,2048]{1,0:T(8,128)(2,1)S(1)}, bf16[32,2048]{1,0:T(8,128)(2,1)S(1)}, u32[]{:S(2)}, u32[]{:S(2)}) collective-permute-start(bf16[32,2048]{1,0:T(8,128)(2,1)S(1)} %get-tuple-element.44), channel_id=1, source_target_pairs={{0,2},{1,3},{2,0},{3,1},{4,6},{5,7},{6,4},{7,5},{8,10},{9,11},{10,... | collective-permute-start | bytes 393224 | tf_op jit(solution)/shard_map/ppermute | solution.py:146
  41.9 4.2 %collective-permute-start.14 = (bf16[32,2048]{1,0:T(8,128)(2,1)S(1)}, bf16[32,2048]{1,0:T(8,128)(2,1)S(1)}, u32[]{:S(2)}, u32[]{:S(2)}) collective-permute-start(bf16[32,2048]{1,0:T(8,128)(2,1)S(1)} %add_convert_fusion.1), channel_id=1, source_target_pairs={{0,4},{1,5},{2,6},{3,7},{4,0},{5,1},{6,2},{7,3},{8,12},{9,13},{10,... | collective-permute-start | bytes 393224 | tf_op jit(solution)/shard_map/ppermute | solution.py:146
  44.7 5.5 %collective-permute-start.18 = (bf16[32,2048]{1,0:T(8,128)(2,1)S(1)}, bf16[32,2048]{1,0:T(8,128)(2,1)S(1)}, u32[]{:S(2)}, u32[]{:S(2)}) collective-permute-start(bf16[32,2048]{1,0:T(8,128)(2,1)S(1)} %add_convert_fusion), channel_id=1, source_target_pairs={{0,8},{1,9},{2,10},{3,11},{4,12},{5,13},{6,14},{7,15},{8,0},{9,1},... | collective-permute-start | bytes 393224 | tf_op jit(solution)/shard_map/ppermute | solution.py:146
  50.4 8.5 %collective-permute-start.21 = (f32[32,64]{1,0:T(8,128)S(1)}, f32[32,64]{1,0:T(8,128)S(1)}, u32[]{:S(2)}, u32[]{:S(2)}) collective-permute-start(f32[32,64]{1,0:T(8,128)S(1)} %slice.7), channel_id=1, source_target_pairs={{0,1},{1,0},{2,3},{3,2},{4,5},{5,4},{6,7},{7,6},{8,9},{9,8},{10,11... | collective-permute-start | bytes 24584 | tf_op jit(solution)/shard_map/ppermute | solution.py:146
  53.7 5.8 %collective-permute-start.19 = (bf16[32,2048]{1,0:T(8,128)(2,1)S(1)}, bf16[32,2048]{1,0:T(8,128)(2,1)S(1)}, u32[]{:S(2)}, u32[]{:S(2)}) collective-permute-start(bf16[32,2048]{1,0:T(8,128)(2,1)S(1)} %get-tuple-element.48), channel_id=1, source_target_pairs={{0,1},{1,0},{2,3},{3,2},{4,5},{5,4},{6,7},{7,6},{8,9},{9,8},{10,11... | collective-permute-start | bytes 393224 | tf_op jit(solution)/shard_map/ppermute | solution.py:146
  53.8 7.7 %collective-permute-start.20 = (bf16[32,2048]{1,0:T(8,128)(2,1)S(1)}, bf16[32,2048]{1,0:T(8,128)(2,1)S(1)}, u32[]{:S(2)}, u32[]{:S(2)}) collective-permute-start(bf16[32,2048]{1,0:T(8,128)(2,1)S(1)} %get-tuple-element.48), channel_id=1, source_target_pairs={{1,2},{2,1},{3,4},{4,3},{5,6},{6,5},{7,8},{8,7},{9,10},{10,9},{11,... | collective-permute-start | bytes 393224 | tf_op jit(solution)/shard_map/ppermute | solution.py:152

commit v4 on v3

--- a/solution.py
+++ b/solution.py
@@ -52,33 +52,55 @@
     return jnp.concatenate([tile] * (lanes // 128), axis=1)
 
 
-def stencil(values, near, far, strength):
-    width = values.shape[1]
+def base_kernel(values_ref, near_ref, strength_ref, base_ref, tile_ref):
+    factors, width = values_ref.shape
+    values = values_ref[...]
+    tile = column(strength_ref, factors, 128)
     at = lax.broadcasted_iota(jnp.int32, values.shape, 1)
     left = jnp.where(at > 0, pltpu.roll(values, 1, 1), 0.0)
     right = jnp.where(at < width - 1, pltpu.roll(values, width - 1, 1), 0.0)
-    return values + strength * (near + far + left + right - 4.0 * values)
-
-
-def factor_kernel(
-    place, latent_ref, near_ref, far_ref, strength_ref, tissue_ref, own_w, other_w, own_b, other_b,
-    factor_ref, slope_ref, weight_ref, turned_ref, back_ref, *, scale,
-):
-    factors, width = latent_ref.shape
-    strength = column(strength_ref, factors, width)
-    smoothed = stencil(latent_ref[...], near_ref[...], far_ref[...], strength)
+    around = near_ref[...].astype(jnp.float32) + left + right - 4.0 * values
+    base_ref[...] = values + jnp.concatenate([tile] * (width // 128), axis=1) * around
+    tile_ref[...] = tile
+
+
+def stencil_base(values, near, strength):
+    return pl.pallas_call(
+        base_kernel,
+        in_specs=[VMEM] * 3,
+        out_specs=[VMEM] * 2,
+        out_shape=[
+            jax.ShapeDtypeStruct(values.shape, jnp.float32),
+            jax.ShapeDtypeStruct((values.shape[0], 128), jnp.float32),
+        ],
+        compiler_params=params(8),
+        cost_estimate=cost(values.size * 9, values.size * 12),
+    )(values, near, strength)
+
+
+def with_far(base_ref, far_ref, tile_ref):
+    wide = jnp.concatenate([tile_ref[...]] * (base_ref.shape[1] // 128), axis=1)
+    return base_ref[...] + wide * far_ref[...].astype(jnp.float32)
+
+
+def weight_kernel(own_w, other_w, own_b, other_b, weight_ref, turned_ref, back_ref):
+    weights = jnp.concatenate([own_w[...].astype(jnp.float32), other_w[...].astype(jnp.float32)], axis=1)
+    weight_ref[...] = weights.astype(jnp.bfloat16)
+    turned_ref[...] = weights.T.astype(jnp.bfloat16)
+    genes = own_w.shape[1]
+    back_ref[:genes] = column(own_b, genes, 128)
+    back_ref[genes:] = column(other_b, genes, 128)
+
+
+def factor_kernel(place, base_ref, far_ref, tile_ref, tissue_ref, factor_ref, slope_ref, *, scale):
+    width = base_ref.shape[1]
+    smoothed = with_far(base_ref, far_ref, tile_ref)
     small = jnp.exp(-jnp.abs(smoothed))
     inside = tissue_ref[:, pl.ds(pl.multiple_of(place[3] * width, width), width)] > 0
     soft = jnp.maximum(smoothed, 0.0) + jnp.log1p(small)
     factor_ref[...] = jnp.where(inside, soft, 0.0).astype(jnp.bfloat16)
     sigmoid = jnp.where(smoothed >= 0.0, 1.0, small) / (1.0 + small)
     slope_ref[...] = jnp.where(inside, sigmoid * scale, 0.0)
-    weights = jnp.concatenate([own_w[...].astype(jnp.float32), other_w[...].astype(jnp.float32)], axis=1)
-    weight_ref[...] = weights.astype(jnp.bfloat16)
-    turned_ref[...] = weights.T.astype(jnp.bfloat16)
-    genes = own_w.shape[1]
-    back_ref[:genes] = column(own_b, genes, 128)
-    back_ref[genes:] = column(other_b, genes, 128)
 
 
 def gene_kernel(
@@ -104,7 +126,7 @@
     load_p[...] = load
 
 
-def gene_sums(place, shift, own_f, other_f, keep, came, weights, turned, back):
+def gene_sums(place, shift, own_f, other_f, keep, came, weights, turned, back, kinds):
     factors, width = own_f.shape
     genes = keep.shape[2]
     work = 2 * genes * 2 * width
@@ -113,8 +135,8 @@
         in_specs=[SMEM] + [VMEM] * 7,
         out_specs=[VMEM] * 3,
         out_shape=[
-            jax.ShapeDtypeStruct(own_f.shape, jnp.float32),
-            jax.ShapeDtypeStruct(own_f.shape, jnp.bfloat16),
+            jax.ShapeDtypeStruct(own_f.shape, kinds[0]),
+            jax.ShapeDtypeStruct(own_f.shape, kinds[1]),
             jax.ShapeDtypeStruct((factors, 2 * genes), jnp.float32),
         ],
         compiler_params=params(12),
@@ -122,12 +144,8 @@
     )(place, own_f, other_f, keep, came, weights, turned, back)
 
 
-def last_kernel(own_ref, near_ref, far_ref, strength_ref, out_ref):
-    factors, width = own_ref.shape
-    out_ref[...] = stencil(
-        own_ref[...], near_ref[...].astype(jnp.float32), far_ref[...].astype(jnp.float32),
-        column(strength_ref, factors, width),
-    )
+def last_kernel(base_ref, far_ref, tile_ref, out_ref):
+    out_ref[...] = with_far(base_ref, far_ref, tile_ref)
 
 
 def after(x, *done):
@@ -155,60 +173,83 @@
     over_row = lambda i: i ^ 2
     along = lambda s: lambda i: i ^ (4 * s)
 
-    far = chips(latent)
-    near = send(latent, over_core)
+    ready = after(latent, place)
+    far = chips(ready)
+    near = send(ready, over_core)
     away = cast_counts(place, counts, planes, width, 1)
     keep = cast_counts(place, counts, planes, width, 0)
     other_w, other_b = send(loading, over_core), send(background, over_core)
     strength = coupling.reshape(1, factors)
     full = jax.ShapeDtypeStruct
-    field, slope, weights, turned, back = pl.pallas_call(
-        functools.partial(factor_kernel, scale=1.0 / (genes * count)),
-        in_specs=[SMEM] + [VMEM] * 9,
-        out_specs=[VMEM] * 5,
+    base, tile = stencil_base(latent, near, strength)
+    weights, turned, back = pl.pallas_call(
+        weight_kernel,
+        in_specs=[VMEM] * 4,
+        out_specs=[VMEM] * 3,
         out_shape=[
-            full(latent.shape, jnp.bfloat16), full(latent.shape, jnp.float32),
             full((factors, 2 * genes), jnp.bfloat16), full((2 * genes, factors), jnp.bfloat16),
             full((2 * genes, 128), jnp.float32),
         ],
         compiler_params=params(8),
+        cost_estimate=cost(genes * 128, genes * 1024),
+    )(loading, other_w, background.reshape(1, genes), other_b.reshape(1, genes))
+    field, slope = pl.pallas_call(
+        functools.partial(factor_kernel, scale=1.0 / (genes * count)),
+        in_specs=[SMEM] + [VMEM] * 4,
+        out_specs=[VMEM] * 2,
+        out_shape=[full(latent.shape, jnp.bfloat16), full(latent.shape, jnp.float32)],
+        compiler_params=params(8),
         cost_estimate=cost(latent.size * 20, latent.size * 18, latent.size * 3),
-    )(
-        place, latent, near, far, strength, tissue.reshape(1, total_spots),
-        loading, other_w, background.reshape(1, genes), other_b.reshape(1, genes),
-    )
-
+    )(after(place, keep, weights), base, far, tile, tissue.reshape(1, total_spots))
     came = send(after(away, field), over_core)
-    order = [0, 3, 1, 2]
+
+    order = [0, 1, 2, 3]
+    send_ties, kernel_ties, sum_ties = {3: (('K', 0),), 2: (('K', 0),)}, {}, {}
+    marks = {}
+    held = lambda x, names: after(x, *[marks[n] for n in names if n in marks]) if names else x
+    narrow, full_width = jnp.bfloat16, jnp.float32
     fields = {s: field if s == 0 else send(field, along(s)) for s in order}
-    total = loads = None
-    done, returned = [], []
-    for at, s in enumerate(order):
-        mine = fields[s] if s == 0 else after(fields[s], done[max(0, at - 2)])
-        other = send(mine, over_row)
-        own_p, other_p, load = gene_sums(place, s, mine, other, keep, came, weights, turned, back)
-        done.append(load)
+    for s in order:
+        marks["G", s] = fields[s]
+    others = {0: send(field, over_row)}
+    marks["H", 0] = others[0]
+    loads = None
+    sums = {}
+    for s in order:
+        if s == 1:
+            others[1] = send(others[0], along(1))
+        elif s:
+            others[s] = send(held(fields[s], send_ties.get(s, ())), over_row)
+        kinds = (full_width if s != 1 else narrow, full_width if s == 0 else narrow)
+        own_p, other_p, load = gene_sums(
+            held(place, kernel_ties.get(s, ())), s, fields[s], others[s], keep, came, weights, turned, back, kinds
+        )
+        marks["K", s] = load
         loads = load if loads is None else loads + load
-        if s == 0:
-            total, later = own_p, other_p
-        else:
-            summed = own_p + send(other_p, over_row).astype(jnp.float32)
-            returned.append(send(summed.astype(jnp.bfloat16), along(s)))
-    total = total + send(after(later, done[-2]), over_row).astype(jnp.float32)
-    for r in returned:
-        total = total + r.astype(jnp.float32)
+        sums[s] = own_p, other_p
+    own_0 = sums[0][0] + send(sums[1][0], along(1)).astype(jnp.float32)
+    other_0 = sums[0][1] + send(sums[1][1], along(1)).astype(jnp.float32)
+    total = own_0 + send(held(other_0.astype(jnp.bfloat16), sum_ties.get(0, ())), over_row).astype(jnp.float32)
+    marks["S", 0] = total
+    for s in order:
+        if s > 1:
+            own_p, other_p = sums[s]
+            summed = own_p + send(held(other_p, sum_ties.get(s, ())), over_row).astype(jnp.float32)
+            total = total + send(summed.astype(jnp.bfloat16), along(s)).astype(jnp.float32)
     grad_smooth = total * slope
+    swapped = send(after(loads, grad_smooth)[:, genes:], over_core)
     rounded = grad_smooth.astype(jnp.bfloat16)
-    near2, far2 = send(rounded, over_core), chips(rounded)
+    far2 = chips(rounded)
+    near2 = send(after(rounded, swapped), over_core)
+    base2, tile2 = stencil_base(grad_smooth, near2, strength)
     grad_latent = pl.pallas_call(
         last_kernel,
-        in_specs=[VMEM] * 4,
+        in_specs=[VMEM] * 3,
         out_specs=VMEM,
         out_shape=full(latent.shape, jnp.float32),
         compiler_params=params(8),
         cost_estimate=cost(latent.size * 10, latent.size * 12),
-    )(grad_smooth, near2, far2, strength)
-    swapped = send(after(loads, grad_smooth)[:, genes:], over_core)
+    )(base2, far2, tile2)
     grad_loading = (loads[:, :genes] + swapped) / total_spots
     return grad_latent, grad_loading
 

time: 63.1 us -> 60.8 us (0.964)
  waiting for transfers between devices: 16.7 us -> 15.1 us
  starting transfers between devices: 29.5 us -> 28 us
    ppermute x2, starting transfers between devices: 9.59 us -> 6.95 us  [chips(): lax.ppermute(x, SPACE, [(i, across(i)) for i in range(count) if 0 <= acro...]
    ppermute x20, starting transfers between devices: 19.9 us -> 21 us  [send(): return lax.ppermute(x, SPACE, [(i, to(i)) for i in range(count)])]
    ppermute x2, waiting for transfers between devices: 3.18 us -> 2.14 us  [chips(): lax.ppermute(x, SPACE, [(i, across(i)) for i in range(count) if 0 <= acro...]
    pallas_call x1 -> x4, Pallas kernels: 0.95 us -> 1.39 us  [the longest x1 0.73 us: local(): pl.pallas_call(last_kernel, in_specs=[VMEM] * 3, out_specs=VMEM, out_shap...]
  transfers between devices with their start and end apart: 22 -> 22, of which waited for: 9 -> 9; matrix products, arithmetic and copies ran while one was open for 1% -> 1% of each run, Pallas kernels for 15% -> 16%
where the time goes in v4:
time: 60.8 us; the launch traced here: 59.7 us
  starting transfers between devices  28 us (46%)
  waiting for transfers between devices  15.1 us (25%)
  Pallas kernels  11.3 us (19%)
  local copies, waits for them, and re-layouts  3.49 us (6%)
  between operations  0.93 us (2%)
  other arithmetic  0.89 us (1%)
    ppermute x20, starting transfers between devices, send(): return lax.ppermute(x, SPACE, [(i, to(i)) for i in range(count)])  21 us
    ppermute x20, waiting for transfers between devices, send(): return lax.ppermute(x, SPACE, [(i, to(i)) for i in range(count)])  13 us
    ppermute x2, starting transfers between devices, chips(): lax.ppermute(x, SPACE, [(i, across(i)) for i in range(count) if 0 <= acro...  6.95 us
    pallas_call x4, Pallas kernels, gene_sums(): pl.pallas_call(functools.partial(gene_kernel, step=1024, shift=shift), in...  6.82 us
    unnamed x12, local copies, waits for them, and re-layouts  3.41 us
    pallas_call x2, Pallas kernels, cast_counts(): pl.pallas_call(functools.partial(cast_kernel, turn=turn), in_specs=[SMEM,...  2.3 us
    ppermute x2, waiting for transfers between devices, chips(): lax.ppermute(x, SPACE, [(i, across(i)) for i in range(count) if 0 <= acro...  2.14 us
  transfers between devices with their start and end apart: 22, of which 9 were waited for; matrix products, arithmetic and copies ran while one was open for 1% of the time, Pallas kernels for 16%

profile of v4, /device:TPU:1, one launch (start us, length us, event | category | flops | bytes accessed | tf_op | source)
XLA Modules:
  0.0 59.7 jit_solution(17923907415973180467)
XLA Ops:
  0.6 0.1 pad_add_fusion.place
  0.7 0.1 collective-permute-start.2
  0.8 4.5 %collective-permute-start.3 = (f32[32,2048]{1,0:T(8,128)}, f32[32,2048]{1,0:T(8,128)S(1)}, u32[]{:S(2)}, u32[]{:S(2)}) collective-permute-start(f32[32,2048]{1,0:T(8,128)} %values_ref.1), channel_id=1, source_target_pairs={{1,2},{2,1},{3,4},{4,3},{5,6},{6,5},{7,8},{8,7},{9,10},{10,9},{11,... | collective-permute-start | bytes 786440 | tf_op jit(solution)/shard_map/ppermute | solution.py:170
  5.3 0.1 collective-permute-start
  5.4 0.5 collective-permute-start.1
  5.9 3.4 %copy-done = s32[64,32768]{1,0:T(8,128)S(1)} copy-done((s32[64,32768]{1,0:T(8,128)S(1)}, s32[64,32768]{1,0:T(8,128)}, u32[]{:S(2)}) %copy-start) | copy-done | bytes 8388632
  9.2 1.1 %shard_map.77.keep_ref = bf16[4,2,64,2048]{3,2,1,0:T(8,128)(2,1)S(1)} custom-call(s32[4]{0:T(128)S(1)} %pad_add_fusion.place, s32[64,32768]{1,0:T(8,128)S(1)} %copy-done), custom_call_target="tpu_custom_call" | custom-call | flops 2097152 | bytes 6291456 | tf_op jit(solution)/shard_map/pallas_call | solution.py:39
  10.4 0.0 copy-start.3
  10.4 0.0 copy-start.5
  10.4 0.0 copy-start.1
  10.4 0.0 copy-start.4
  10.4 0.0 copy-start.2
  10.5 1.2 %shard_map.81 = bf16[4,2,64,2048]{3,2,1,0:T(8,128)(2,1)S(1)} custom-call(s32[4]{0:T(128)S(1)} %pad_add_fusion.place, s32[64,32768]{1,0:T(8,128)S(1)} %copy-done), custom_call_target="tpu_custom_call" | custom-call | flops 2097152 | bytes 6291456 | tf_op jit(solution)/shard_map/pallas_call | solution.py:39
  11.6 0.0 collective-permute-done.1
  11.6 0.0 collective-permute-done.other_w
  11.7 0.2 shard_map.78
  11.8 0.0 collective-permute-done.2.near_ref
  11.9 0.2 shard_map.79
  12.1 0.0 collective-permute-done.3.far_ref
  12.1 0.8 %shard_map.80 = (bf16[32,2048]{1,0:T(8,128)(2,1)S(1)}, f32[32,2048]{1,0:T(8,128)S(1)}) custom-call(s32[4]{0:T(128)S(1)} %pad_add_fusion.place, f32[32,2048]{1,0:T(8,128)S(1)} %get-tuple-element.33.base_ref, f32[32,2048]{1,0:T(8,128)S(1)} %collective-permute-done.3.far_ref, f32[32,128]{1,0:T(8,128)S(1)} %get-tuple-element.34.tile_ref, s32[1,32768]{1,0:T(1,128)S(1)} %bitcast.8), custom_call_target="tpu_custom_call" | custom-call | flops 1310720 | bytes 1179648 | tf_op jit(solution)/shard_map/pallas_call | solution.py:196
  12.9 0.1 collective-permute-start.5
  13.1 2.0 %collective-permute-start.4 = (bf16[32,2048]{1,0:T(8,128)(2,1)S(1)}, bf16[32,2048]{1,0:T(8,128)(2,1)S(1)}, u32[]{:S(2)}, u32[]{:S(2)}) collective-permute-start(bf16[32,2048]{1,0:T(8,128)(2,1)S(1)} %get-tuple-element.35.own_f), channel_id=1, source_target_pairs={{0,2},{1,3},{2,0},{3,1},{4,6},{5,7},{6,4},{7,5},{8,10},{9,11},{10,... | collective-permute-start | bytes 393224 | tf_op jit(solution)/shard_map/ppermute | solution.py:164
  15.1 2.3 %collective-permute-start.11 = (bf16[32,2048]{1,0:T(8,128)(2,1)S(1)}, bf16[32,2048]{1,0:T(8,128)(2,1)S(1)}, u32[]{:S(2)}, u32[]{:S(2)}) collective-permute-start(bf16[32,2048]{1,0:T(8,128)(2,1)S(1)} %get-tuple-element.35.own_f), channel_id=1, source_target_pairs={{0,8},{1,9},{2,10},{3,11},{4,12},{5,13},{6,14},{7,15},{8,0},{9,1},... | collective-permute-start | bytes 393224 | tf_op jit(solution)/shard_map/ppermute | solution.py:164
  17.4 0.2 collective-permute-start.6
  17.5 1.3 %collective-permute-done.4.other_f = bf16[32,2048]{1,0:T(8,128)(2,1)S(1)} collective-permute-done((bf16[32,2048]{1,0:T(8,128)(2,1)S(1)}, bf16[32,2048]{1,0:T(8,128)(2,1)S(1)}, u32[]{:S(2)}, u32[]{:S(2)}) %collective-permute-start.4) | collective-permute-done | bytes 131104 | tf_op jit(solution)/shard_map/ppermute | solution.py:164
  18.8 1.0 %collective-permute-start.7 = (bf16[32,2048]{1,0:T(8,128)(2,1)S(1)}, bf16[32,2048]{1,0:T(8,128)(2,1)S(1)}, u32[]{:S(2)}, u32[]{:S(2)}) collective-permute-start(bf16[32,2048]{1,0:T(8,128)(2,1)S(1)} %collective-permute-done.4.other_f), channel_id=1, source_target_pairs={{0,4},{1,5},{2,6},{3,7},{4,0},{5,1},{6,2},{7,3},{8,12},{9,13},{10,... | collective-permute-start | bytes 393224 | tf_op jit(solution)/shard_map/ppermute | solution.py:164
  19.8 2.2 %collective-permute-start.15 = (bf16[32,2048]{1,0:T(8,128)(2,1)S(1)}, bf16[32,2048]{1,0:T(8,128)(2,1)S(1)}, u32[]{:S(2)}, u32[]{:S(2)}) collective-permute-start(bf16[32,2048]{1,0:T(8,128)(2,1)S(1)} %get-tuple-element.35.own_f), channel_id=1, source_target_pairs={{0,12},{1,13},{2,14},{3,15},{4,8},{5,9},{6,10},{7,11},{8,4},{9,5},... | collective-permute-start | bytes 393224 | tf_op jit(solution)/shard_map/ppermute | solution.py:164
  22.0 0.0 collective-permute-done.5.came_ref
  22.0 1.7 %shard_map.82 = (f32[32,2048]{1,0:T(8,128)S(1)}, f32[32,2048]{1,0:T(8,128)S(1)}, f32[32,128]{1,0:T(8,128)S(1)}) custom-call(s32[4]{0:T(128)S(1)} %pad_add_fusion.place, bf16[32,2048]{1,0:T(8,128)(2,1)S(1)} %get-tuple-element.35.own_f, bf16[32,2048]{1,0:T(8,128)(2,1)S(1)} %collective-permute-done.4.other_f, bf16[4,2,64,2048]{3,2,1,0:T(8,128)(2,1)S(1)} %shard_map.77.keep_ref, ...), custom_call_target="tpu_custom_call" | custom-call | flops 100663296 | bytes 1572864 | tf_op jit(solution)/shard_map/pallas_call | solution.py:133
  23.7 0.0 collective-permute-done.11.own_f
  23.7 1.7 %collective-permute-start.12 = (bf16[32,2048]{1,0:T(8,128)(2,1)S(1)}, bf16[32,2048]{1,0:T(8,128)(2,1)S(1)}, u32[]{:S(2)}, u32[]{:S(2)}) collective-permute-start(bf16[32,2048]{1,0:T(8,128)(2,1)S(1)} %collective-permute-done.11.own_f), channel_id=1, source_target_pairs={{0,2},{1,3},{2,0},{3,1},{4,6},{5,7},{6,4},{7,5},{8,10},{9,11},{10,... | collective-permute-start | bytes 393224 | tf_op jit(solution)/shard_map/ppermute | solution.py:164
  25.4 0.0 collective-permute-done.6.own_f
  25.4 0.9 %collective-permute-done.7.other_f = bf16[32,2048]{1,0:T(8,128)(2,1)S(1)} collective-permute-done((bf16[32,2048]{1,0:T(8,128)(2,1)S(1)}, bf16[32,2048]{1,0:T(8,128)(2,1)S(1)}, u32[]{:S(2)}, u32[]{:S(2)}) %collective-permute-start.7) | collective-permute-done | bytes 131104 | tf_op jit(solution)/shard_map/ppermute | solution.py:164
  26.3 1.7 %shard_map.83 = (bf16[32,2048]{1,0:T(8,128)(2,1)S(1)}, bf16[32,2048]{1,0:T(8,128)(2,1)S(1)}, f32[32,128]{1,0:T(8,128)S(1)}) custom-call(s32[4]{0:T(128)S(1)} %pad_add_fusion.place, bf16[32,2048]{1,0:T(8,128)(2,1)S(1)} %collective-permute-done.6.own_f, bf16[32,2048]{1,0:T(8,128)(2,1)S(1)} %collective-permute-done.7.other_f, ...), custom_call_target="tpu_custom_call" | custom-call | flops 100663296 | bytes 1572864 | tf_op jit(solution)/shard_map/pallas_call | solution.py:133
  28.0 1.5 %collective-permute-start.9 = (bf16[32,2048]{1,0:T(8,128)(2,1)S(1)}, bf16[32,2048]{1,0:T(8,128)(2,1)S(1)}, u32[]{:S(2)}, u32[]{:S(2)}) collective-permute-start(bf16[32,2048]{1,0:T(8,128)(2,1)S(1)} %get-tuple-element.42), channel_id=1, source_target_pairs={{0,4},{1,5},{2,6},{3,7},{4,0},{5,1},{6,2},{7,3},{8,12},{9,13},{10,... | collective-permute-start | bytes 393224 | tf_op jit(solution)/shard_map/ppermute | solution.py:164
  29.6 0.6 %collective-permute-done.15.own_f = bf16[32,2048]{1,0:T(8,128)(2,1)S(1)} collective-permute-done((bf16[32,2048]{1,0:T(8,128)(2,1)S(1)}, bf16[32,2048]{1,0:T(8,128)(2,1)S(1)}, u32[]{:S(2)}, u32[]{:S(2)}) %collective-permute-start.15) | collective-permute-done | bytes 131104 | tf_op jit(solution)/shard_map/ppermute | solution.py:164
  30.2 0.4 collective-permute-start.16
  30.5 0.0 collective-permute-start.8
  30.5 0.0 collective-permute-done.12.other_f
  30.5 1.7 %shard_map.84 = (f32[32,2048]{1,0:T(8,128)S(1)}, bf16[32,2048]{1,0:T(8,128)(2,1)S(1)}, f32[32,128]{1,0:T(8,128)S(1)}) custom-call(s32[4]{0:T(128)S(1)} %pad_add_fusion.place, bf16[32,2048]{1,0:T(8,128)(2,1)S(1)} %collective-permute-done.11.own_f, bf16[32,2048]{1,0:T(8,128)(2,1)S(1)} %collective-permute-done.12.other_f, ...), custom_call_target="tpu_custom_call" | custom-call | flops 100663296 | bytes 1572864 | tf_op jit(solution)/shard_map/pallas_call | solution.py:133
  32.3 1.2 %collective-permute-start.13 = (bf16[32,2048]{1,0:T(8,128)(2,1)S(1)}, bf16[32,2048]{1,0:T(8,128)(2,1)S(1)}, u32[]{:S(2)}, u32[]{:S(2)}) collective-permute-start(bf16[32,2048]{1,0:T(8,128)(2,1)S(1)} %get-tuple-element.46), channel_id=1, source_target_pairs={{0,2},{1,3},{2,0},{3,1},{4,6},{5,7},{6,4},{7,5},{8,10},{9,11},{10,... | collective-permute-start | bytes 393224 | tf_op jit(solution)/shard_map/ppermute | solution.py:164
  33.4 0.0 collective-permute-done.9
  33.5 0.4 collective-permute-start.10
  33.9 0.4 collective-permute-done.16.other_f
  34.3 1.7 %shard_map.85 = (f32[32,2048]{1,0:T(8,128)S(1)}, bf16[32,2048]{1,0:T(8,128)(2,1)S(1)}, f32[32,128]{1,0:T(8,128)S(1)}) custom-call(s32[4]{0:T(128)S(1)} %pad_add_fusion.place, bf16[32,2048]{1,0:T(8,128)(2,1)S(1)} %collective-permute-done.15.own_f, bf16[32,2048]{1,0:T(8,128)(2,1)S(1)} %collective-permute-done.16.other_f, ...), custom_call_target="tpu_custom_call" | custom-call | flops 100663296 | bytes 1572864 | tf_op jit(solution)/shard_map/pallas_call | solution.py:133
  36.0 0.8 %collective-permute-start.17 = (bf16[32,2048]{1,0:T(8,128)(2,1)S(1)}, bf16[32,2048]{1,0:T(8,128)(2,1)S(1)}, u32[]{:S(2)}, u32[]{:S(2)}) collective-permute-start(bf16[32,2048]{1,0:T(8,128)(2,1)S(1)} %get-tuple-element.49), channel_id=1, source_target_pairs={{0,2},{1,3},{2,0},{3,1},{4,6},{5,7},{6,4},{7,5},{8,10},{9,11},{10,... | collective-permute-start | bytes 393224 | tf_op jit(solution)/shard_map/ppermute | solution.py:164
  36.8 0.9 %collective-permute-done.13 = bf16[32,2048]{1,0:T(8,128)(2,1)S(1)} collective-permute-done((bf16[32,2048]{1,0:T(8,128)(2,1)S(1)}, bf16[32,2048]{1,0:T(8,128)(2,1)S(1)}, u32[]{:S(2)}, u32[]{:S(2)}) %collective-permute-start.13) | collective-permute-done | bytes 131104 | tf_op jit(solution)/shard_map/ppermute | solution.py:164
  37.7 1.7 %collective-permute-start.14 = (bf16[32,2048]{1,0:T(8,128)(2,1)S(1)}, bf16[32,2048]{1,0:T(8,128)(2,1)S(1)}, u32[]{:S(2)}, u32[]{:S(2)}) collective-permute-start(bf16[32,2048]{1,0:T(8,128)(2,1)S(1)} %add_convert_fusion.1), channel_id=1, source_target_pairs={{0,8},{1,9},{2,10},{3,11},{4,12},{5,13},{6,14},{7,15},{8,0},{9,1},... | collective-permute-start | bytes 393224 | tf_op jit(solution)/shard_map/ppermute | solution.py:164
  39.4 4.0 %collective-permute-done.17 = bf16[32,2048]{1,0:T(8,128)(2,1)S(1)} collective-permute-done((bf16[32,2048]{1,0:T(8,128)(2,1)S(1)}, bf16[32,2048]{1,0:T(8,128)(2,1)S(1)}, u32[]{:S(2)}, u32[]{:S(2)}) %collective-permute-start.17) | collective-permute-done | bytes 131104 | tf_op jit(solution)/shard_map/ppermute | solution.py:164
  43.4 1.4 %collective-permute-start.18 = (bf16[32,2048]{1,0:T(8,128)(2,1)S(1)}, bf16[32,2048]{1,0:T(8,128)(2,1)S(1)}, u32[]{:S(2)}, u32[]{:S(2)}) collective-permute-start(bf16[32,2048]{1,0:T(8,128)(2,1)S(1)} %add_convert_fusion), channel_id=1, source_target_pairs={{0,12},{1,13},{2,14},{3,15},{4,8},{5,9},{6,10},{7,11},{8,4},{9,5},... | collective-permute-start | bytes 393224 | tf_op jit(solution)/shard_map/ppermute | solution.py:164
  44.8 0.0 collective-permute-done.8
  44.8 0.0 collective-permute-done.10
  44.8 0.0 collective-permute-done.14
  44.8 4.2 %collective-permute-done.18 = bf16[32,2048]{1,0:T(8,128)(2,1)S(1)} collective-permute-done((bf16[32,2048]{1,0:T(8,128)(2,1)S(1)}, bf16[32,2048]{1,0:T(8,128)(2,1)S(1)}, u32[]{:S(2)}, u32[]{:S(2)}) %collective-permute-start.18) | collective-permute-done | bytes 131104 | tf_op jit(solution)/shard_map/ppermute | solution.py:164
  49.0 0.1 fusion.1
  49.1 0.1 slice.6
  49.2 3.5 %collective-permute-start.19 = (f32[32,64]{1,0:T(8,128)S(1)}, f32[32,64]{1,0:T(8,128)S(1)}, u32[]{:S(2)}, u32[]{:S(2)}) collective-permute-start(f32[32,64]{1,0:T(8,128)S(1)} %slice.6), channel_id=1, source_target_pairs={{0,1},{1,0},{2,3},{3,2},{4,5},{5,4},{6,7},{7,6},{8,9},{9,8},{10,11... | collective-permute-start | bytes 24584 | tf_op jit(solution)/shard_map/ppermute | solution.py:164
  52.7 2.5 %collective-permute-start.21 = (bf16[32,2048]{1,0:T(8,128)(2,1)S(1)}, bf16[32,2048]{1,0:T(8,128)(2,1)S(1)}, u32[]{:S(2)}, u32[]{:S(2)}) collective-permute-start(bf16[32,2048]{1,0:T(8,128)(2,1)S(1)} %get-tuple-element.55), channel_id=1, source_target_pairs={{1,2},{2,1},{3,4},{4,3},{5,6},{6,5},{7,8},{8,7},{9,10},{10,9},{11,... | collective-permute-start | bytes 393224 | tf_op jit(solution)/shard_map/ppermute | solution.py:170
  55.2 0.1 collective-permute-start.20
  55.3 0.6 %fusion = f32[32,64]{1,0:T(8,128)} fusion(f32[32,64]{1,0:T(8,128)S(1)} %collective-permute-done.19, f32[32,128]{1,0:T(8,128)S(1)} %add_add_fusion), kind=kLoop, calls=%fused_computation.5 | loop fusion | flops 4096 | bytes 24576 | tf_op jit(solution)/shard_map/div | solution.py:253
  55.9 0.7 %collective-permute-done.20.near_ref = bf16[32,2048]{1,0:T(8,128)(2,1)S(1)} collective-permute-done((bf16[32,2048]{1,0:T(8,128)(2,1)S(1)}, bf16[32,2048]{1,0:T(8,128)(2,1)S(1)}, u32[]{:S(2)}, u32[]{:S(2)}) %collective-permute-start.20) | collective-permute-done | bytes 131104 | tf_op jit(solution)/shard_map/ppermute | solution.py:164
  56.6 0.2 shard_map.86
  56.8 2.1 %collective-permute-done.21.far_ref = bf16[32,2048]{1,0:T(8,128)(2,1)S(1)} collective-permute-done((bf16[32,2048]{1,0:T(8,128)(2,1)S(1)}, bf16[32,2048]{1,0:T(8,128)(2,1)S(1)}, u32[]{:S(2)}, u32[]{:S(2)}) %collective-permute-start.21) | collective-permute-done | bytes 131104 | tf_op jit(solution)/shard_map/ppermute | solution.py:170
  59.0 0.7 %shard_map.87 = f32[32,2048]{1,0:T(8,128)} custom-call(f32[32,2048]{1,0:T(8,128)S(1)} %get-tuple-element.56.base_ref, bf16[32,2048]{1,0:T(8,128)(2,1)S(1)} %collective-permute-done.21.far_ref, f32[32,128]{1,0:T(8,128)S(1)} %get-tuple-element.57.tile_ref), custom_call_target="tpu_custom_call" | custom-call | flops 655360 | bytes 786432 | tf_op jit(solution)/shard_map/pallas_call | solution.py:245
  (11 shorter events, 0.1 us)
Async XLA Ops:
  0.7 11.1 %collective-permute-start.2 = (f32[32,2048]{1,0:T(8,128)}, f32[32,2048]{1,0:T(8,128)S(1)}, u32[]{:S(2)}, u32[]{:S(2)}) collective-permute-start(f32[32,2048]{1,0:T(8,128)} %values_ref.1), channel_id=1, source_target_pairs={{0,1},{1,0},{2,3},{3,2},{4,5},{5,4},{6,7},{7,6},{8,9},{9,8},{10,11... | collective-permute-start | bytes 786440 | tf_op jit(solution)/shard_map/ppermute | solution.py:164
  0.8 11.3 %collective-permute-start.3 = (f32[32,2048]{1,0:T(8,128)}, f32[32,2048]{1,0:T(8,128)S(1)}, u32[]{:S(2)}, u32[]{:S(2)}) collective-permute-start(f32[32,2048]{1,0:T(8,128)} %values_ref.1), channel_id=1, source_target_pairs={{1,2},{2,1},{3,4},{4,3},{5,6},{6,5},{7,8},{8,7},{9,10},{10,9},{11,... | collective-permute-start | bytes 786440 | tf_op jit(solution)/shard_map/ppermute | solution.py:170
  5.3 6.3 %collective-permute-start = (bf16[32,64]{1,0:T(8,128)(2,1)}, bf16[32,64]{1,0:T(8,128)(2,1)S(1)}, u32[]{:S(2)}, u32[]{:S(2)}) collective-permute-start(bf16[32,64]{1,0:T(8,128)(2,1)} %own_w.1), channel_id=1, source_target_pairs={{0,1},{1,0},{2,3},{3,2},{4,5},{5,4},{6,7},{7,6},{8,9},{9,8},{10,11... | collective-permute-start | bytes 12296 | tf_op jit(solution)/shard_map/ppermute | solution.py:164
  5.4 6.3 %collective-permute-start.1 = (f32[64]{0:T(128)}, f32[64]{0:T(128)S(1)}, u32[]{:S(2)}, u32[]{:S(2)}) collective-permute-start(f32[64]{0:T(128)} %param.9), channel_id=1, source_target_pairs={{0,1},{1,0},{2,3},{3,2},{4,5},{5,4},{6,7},{7,6},{8,9},{9,8},{10,11... | collective-permute-start | bytes 776 | tf_op jit(solution)/shard_map/ppermute | solution.py:164
  5.9 3.4 %copy-start = (s32[64,32768]{1,0:T(8,128)S(1)}, s32[64,32768]{1,0:T(8,128)}, u32[]{:S(2)}) copy-start(s32[64,32768]{1,0:T(8,128)} %counts_ref.3) | copy-start | bytes 25165828
  10.4 1.2 %copy-start.3 = (bf16[32,64]{1,0:T(8,128)(2,1)S(1)}, bf16[32,64]{1,0:T(8,128)(2,1)}, u32[]{:S(2)}) copy-start(bf16[32,64]{1,0:T(8,128)(2,1)} %own_w.1) | copy-start | bytes 12292
  10.4 1.2 %copy-start.5 = (f32[64]{0:T(128)S(1)}, f32[64]{0:T(128)}, u32[]{:S(2)}) copy-start(f32[64]{0:T(128)} %param.9) | copy-start | bytes 772
  10.4 1.4 %copy-start.1 = (f32[32,2048]{1,0:T(8,128)S(1)}, f32[32,2048]{1,0:T(8,128)}, u32[]{:S(2)}) copy-start(f32[32,2048]{1,0:T(8,128)} %values_ref.1) | copy-start | bytes 786436
  10.4 1.4 %copy-start.4 = (f32[32]{0:T(128)S(1)}, f32[32]{0:T(128)}, u32[]{:S(2)}) copy-start(f32[32]{0:T(128)} %param.10) | copy-start | bytes 388
  10.4 1.7 %copy-start.2 = (s32[32768]{0:T(1024)S(1)}, s32[32768]{0:T(1024)}, u32[]{:S(2)}) copy-start(s32[32768]{0:T(1024)} %param.11) | copy-start | bytes 393220
  12.9 9.1 %collective-permute-start.5 = (bf16[4,2,64,2048]{3,2,1,0:T(8,128)(2,1)S(1)}, bf16[4,2,64,2048]{3,2,1,0:T(8,128)(2,1)S(1)}, u32[]{:S(2)}, u32[]{:S(2)}) collective-permute-start(bf16[4,2,64,2048]{3,2,1,0:T(8,128)(2,1)S(1)} %shard_map.81), channel_id=1, source_target_pairs={{0,1},{1,0},{2,3},{3,2},{4,5},{5,4},{6,7},{7,6},{8,9},{9,8},{10,11... | collective-permute-start | bytes 6291464 | tf_op jit(solution)/shard_map/ppermute | solution.py:164
  13.1 5.7 %collective-permute-start.4 = (bf16[32,2048]{1,0:T(8,128)(2,1)S(1)}, bf16[32,2048]{1,0:T(8,128)(2,1)S(1)}, u32[]{:S(2)}, u32[]{:S(2)}) collective-permute-start(bf16[32,2048]{1,0:T(8,128)(2,1)S(1)} %get-tuple-element.35.own_f), channel_id=1, source_target_pairs={{0,2},{1,3},{2,0},{3,1},{4,6},{5,7},{6,4},{7,5},{8,10},{9,11},{10,... | collective-permute-start | bytes 393224 | tf_op jit(solution)/shard_map/ppermute | solution.py:164
  15.1 8.7 %collective-permute-start.11 = (bf16[32,2048]{1,0:T(8,128)(2,1)S(1)}, bf16[32,2048]{1,0:T(8,128)(2,1)S(1)}, u32[]{:S(2)}, u32[]{:S(2)}) collective-permute-start(bf16[32,2048]{1,0:T(8,128)(2,1)S(1)} %get-tuple-element.35.own_f), channel_id=1, source_target_pairs={{0,8},{1,9},{2,10},{3,11},{4,12},{5,13},{6,14},{7,15},{8,0},{9,1},... | collective-permute-start | bytes 393224 | tf_op jit(solution)/shard_map/ppermute | solution.py:164
  17.4 8.0 %collective-permute-start.6 = (bf16[32,2048]{1,0:T(8,128)(2,1)S(1)}, bf16[32,2048]{1,0:T(8,128)(2,1)S(1)}, u32[]{:S(2)}, u32[]{:S(2)}) collective-permute-start(bf16[32,2048]{1,0:T(8,128)(2,1)S(1)} %get-tuple-element.35.own_f), channel_id=1, source_target_pairs={{0,4},{1,5},{2,6},{3,7},{4,0},{5,1},{6,2},{7,3},{8,12},{9,13},{10,... | collective-permute-start | bytes 393224 | tf_op jit(solution)/shard_map/ppermute | solution.py:164
  18.8 7.5 %collective-permute-start.7 = (bf16[32,2048]{1,0:T(8,128)(2,1)S(1)}, bf16[32,2048]{1,0:T(8,128)(2,1)S(1)}, u32[]{:S(2)}, u32[]{:S(2)}) collective-permute-start(bf16[32,2048]{1,0:T(8,128)(2,1)S(1)} %collective-permute-done.4.other_f), channel_id=1, source_target_pairs={{0,4},{1,5},{2,6},{3,7},{4,0},{5,1},{6,2},{7,3},{8,12},{9,13},{10,... | collective-permute-start | bytes 393224 | tf_op jit(solution)/shard_map/ppermute | solution.py:164
  19.8 10.4 %collective-permute-start.15 = (bf16[32,2048]{1,0:T(8,128)(2,1)S(1)}, bf16[32,2048]{1,0:T(8,128)(2,1)S(1)}, u32[]{:S(2)}, u32[]{:S(2)}) collective-permute-start(bf16[32,2048]{1,0:T(8,128)(2,1)S(1)} %get-tuple-element.35.own_f), channel_id=1, source_target_pairs={{0,12},{1,13},{2,14},{3,15},{4,8},{5,9},{6,10},{7,11},{8,4},{9,5},... | collective-permute-start | bytes 393224 | tf_op jit(solution)/shard_map/ppermute | solution.py:164
  23.7 6.8 %collective-permute-start.12 = (bf16[32,2048]{1,0:T(8,128)(2,1)S(1)}, bf16[32,2048]{1,0:T(8,128)(2,1)S(1)}, u32[]{:S(2)}, u32[]{:S(2)}) collective-permute-start(bf16[32,2048]{1,0:T(8,128)(2,1)S(1)} %collective-permute-done.11.own_f), channel_id=1, source_target_pairs={{0,2},{1,3},{2,0},{3,1},{4,6},{5,7},{6,4},{7,5},{8,10},{9,11},{10,... | collective-permute-start | bytes 393224 | tf_op jit(solution)/shard_map/ppermute | solution.py:164
  28.0 5.4 %collective-permute-start.9 = (bf16[32,2048]{1,0:T(8,128)(2,1)S(1)}, bf16[32,2048]{1,0:T(8,128)(2,1)S(1)}, u32[]{:S(2)}, u32[]{:S(2)}) collective-permute-start(bf16[32,2048]{1,0:T(8,128)(2,1)S(1)} %get-tuple-element.42), channel_id=1, source_target_pairs={{0,4},{1,5},{2,6},{3,7},{4,0},{5,1},{6,2},{7,3},{8,12},{9,13},{10,... | collective-permute-start | bytes 393224 | tf_op jit(solution)/shard_map/ppermute | solution.py:164
  30.2 4.1 %collective-permute-start.16 = (bf16[32,2048]{1,0:T(8,128)(2,1)S(1)}, bf16[32,2048]{1,0:T(8,128)(2,1)S(1)}, u32[]{:S(2)}, u32[]{:S(2)}) collective-permute-start(bf16[32,2048]{1,0:T(8,128)(2,1)S(1)} %collective-permute-done.15.own_f), channel_id=1, source_target_pairs={{0,2},{1,3},{2,0},{3,1},{4,6},{5,7},{6,4},{7,5},{8,10},{9,11},{10,... | collective-permute-start | bytes 393224 | tf_op jit(solution)/shard_map/ppermute | solution.py:164
  30.5 14.3 %collective-permute-start.8 = (bf16[32,2048]{1,0:T(8,128)(2,1)S(1)}, bf16[32,2048]{1,0:T(8,128)(2,1)S(1)}, u32[]{:S(2)}, u32[]{:S(2)}) collective-permute-start(bf16[32,2048]{1,0:T(8,128)(2,1)S(1)} %get-tuple-element.40), channel_id=1, source_target_pairs={{0,4},{1,5},{2,6},{3,7},{4,0},{5,1},{6,2},{7,3},{8,12},{9,13},{10,... | collective-permute-start | bytes 393224 | tf_op jit(solution)/shard_map/ppermute | solution.py:164
  32.3 5.4 %collective-permute-start.13 = (bf16[32,2048]{1,0:T(8,128)(2,1)S(1)}, bf16[32,2048]{1,0:T(8,128)(2,1)S(1)}, u32[]{:S(2)}, u32[]{:S(2)}) collective-permute-start(bf16[32,2048]{1,0:T(8,128)(2,1)S(1)} %get-tuple-element.46), channel_id=1, source_target_pairs={{0,2},{1,3},{2,0},{3,1},{4,6},{5,7},{6,4},{7,5},{8,10},{9,11},{10,... | collective-permute-start | bytes 393224 | tf_op jit(solution)/shard_map/ppermute | solution.py:164
  33.5 11.3 %collective-permute-start.10 = (bf16[32,2048]{1,0:T(8,128)(2,1)S(1)}, bf16[32,2048]{1,0:T(8,128)(2,1)S(1)}, u32[]{:S(2)}, u32[]{:S(2)}) collective-permute-start(bf16[32,2048]{1,0:T(8,128)(2,1)S(1)} %add_convert_fusion.2), channel_id=1, source_target_pairs={{0,2},{1,3},{2,0},{3,1},{4,6},{5,7},{6,4},{7,5},{8,10},{9,11},{10,... | collective-permute-start | bytes 393224 | tf_op jit(solution)/shard_map/ppermute | solution.py:164
  36.0 7.3 %collective-permute-start.17 = (bf16[32,2048]{1,0:T(8,128)(2,1)S(1)}, bf16[32,2048]{1,0:T(8,128)(2,1)S(1)}, u32[]{:S(2)}, u32[]{:S(2)}) collective-permute-start(bf16[32,2048]{1,0:T(8,128)(2,1)S(1)} %get-tuple-element.49), channel_id=1, source_target_pairs={{0,2},{1,3},{2,0},{3,1},{4,6},{5,7},{6,4},{7,5},{8,10},{9,11},{10,... | collective-permute-start | bytes 393224 | tf_op jit(solution)/shard_map/ppermute | solution.py:164
  37.7 7.1 %collective-permute-start.14 = (bf16[32,2048]{1,0:T(8,128)(2,1)S(1)}, bf16[32,2048]{1,0:T(8,128)(2,1)S(1)}, u32[]{:S(2)}, u32[]{:S(2)}) collective-permute-start(bf16[32,2048]{1,0:T(8,128)(2,1)S(1)} %add_convert_fusion.1), channel_id=1, source_target_pairs={{0,8},{1,9},{2,10},{3,11},{4,12},{5,13},{6,14},{7,15},{8,0},{9,1},... | collective-permute-start | bytes 393224 | tf_op jit(solution)/shard_map/ppermute | solution.py:164
  43.4 5.7 %collective-permute-start.18 = (bf16[32,2048]{1,0:T(8,128)(2,1)S(1)}, bf16[32,2048]{1,0:T(8,128)(2,1)S(1)}, u32[]{:S(2)}, u32[]{:S(2)}) collective-permute-start(bf16[32,2048]{1,0:T(8,128)(2,1)S(1)} %add_convert_fusion), channel_id=1, source_target_pairs={{0,12},{1,13},{2,14},{3,15},{4,8},{5,9},{6,10},{7,11},{8,4},{9,5},... | collective-permute-start | bytes 393224 | tf_op jit(solution)/shard_map/ppermute | solution.py:164
  49.2 5.9 %collective-permute-start.19 = (f32[32,64]{1,0:T(8,128)S(1)}, f32[32,64]{1,0:T(8,128)S(1)}, u32[]{:S(2)}, u32[]{:S(2)}) collective-permute-start(f32[32,64]{1,0:T(8,128)S(1)} %slice.6), channel_id=1, source_target_pairs={{0,1},{1,0},{2,3},{3,2},{4,5},{5,4},{6,7},{7,6},{8,9},{9,8},{10,11... | collective-permute-start | bytes 24584 | tf_op jit(solution)/shard_map/ppermute | solution.py:164
  52.7 6.3 %collective-permute-start.21 = (bf16[32,2048]{1,0:T(8,128)(2,1)S(1)}, bf16[32,2048]{1,0:T(8,128)(2,1)S(1)}, u32[]{:S(2)}, u32[]{:S(2)}) collective-permute-start(bf16[32,2048]{1,0:T(8,128)(2,1)S(1)} %get-tuple-element.55), channel_id=1, source_target_pairs={{1,2},{2,1},{3,4},{4,3},{5,6},{6,5},{7,8},{8,7},{9,10},{10,9},{11,... | collective-permute-start | bytes 393224 | tf_op jit(solution)/shard_map/ppermute | solution.py:170
  55.2 1.4 %collective-permute-start.20 = (bf16[32,2048]{1,0:T(8,128)(2,1)S(1)}, bf16[32,2048]{1,0:T(8,128)(2,1)S(1)}, u32[]{:S(2)}, u32[]{:S(2)}) collective-permute-start(bf16[32,2048]{1,0:T(8,128)(2,1)S(1)} %get-tuple-element.55), channel_id=1, source_target_pairs={{0,1},{1,0},{2,3},{3,2},{4,5},{5,4},{6,7},{7,6},{8,9},{9,8},{10,11... | collective-permute-start | bytes 393224 | tf_op jit(solution)/shard_map/ppermute | solution.py:164

commit v5 on v4

--- a/solution.py
+++ b/solution.py
@@ -10,7 +10,6 @@
 SPACE = "space"
 MIB = 1024 * 1024
 VMEM = pl.BlockSpec(memory_space=pltpu.VMEM)
-SMEM = pl.BlockSpec(memory_space=pltpu.SMEM)
 
 
 def params(mib):
@@ -21,9 +20,9 @@
     return pl.CostEstimate(flops=flops, bytes_accessed=nbytes, transcendentals=trans)
 
 
-def cast_kernel(place, counts_ref, out_ref, taken, arrived, *, turn):
+def cast_kernel(counts_ref, out_ref, taken, arrived, *, turn):
     planes, rows, _, width = out_ref.shape
-    parity = lax.rem(place[0] + turn, 2)
+    parity = (lax.axis_index(SPACE) + turn) & 1
     copies = []
     for block in range(planes * rows):
         start = pl.multiple_of((2 * block + parity) * width, width)
@@ -34,17 +33,17 @@
         out_ref[block // rows, block % rows] = taken[block].astype(jnp.float32).astype(jnp.bfloat16)
 
 
-def cast_counts(place, counts, planes, width, turn):
+def cast_counts(counts, planes, width, turn):
     genes = counts.shape[0]
     return pl.pallas_call(
         functools.partial(cast_kernel, turn=turn),
-        in_specs=[SMEM, pl.BlockSpec(memory_space=pltpu.HBM)],
+        in_specs=[pl.BlockSpec(memory_space=pltpu.HBM)],
         out_specs=VMEM,
         out_shape=jax.ShapeDtypeStruct((planes, 2, genes, width), jnp.bfloat16),
         scratch_shapes=[pltpu.VMEM((2 * planes, genes, width), jnp.int32), pltpu.SemaphoreType.DMA((2 * planes,))],
         compiler_params=params(14),
         cost_estimate=cost(counts.size, counts.size * 3),
-    )(place, counts)
+    )(counts)
 
 
 def column(row_ref, rows, lanes):
@@ -92,11 +91,11 @@
     back_ref[genes:] = column(other_b, genes, 128)
 
 
-def factor_kernel(place, base_ref, far_ref, tile_ref, tissue_ref, factor_ref, slope_ref, *, scale):
+def factor_kernel(base_ref, far_ref, tile_ref, tissue_ref, factor_ref, slope_ref, *, scale):
     width = base_ref.shape[1]
     smoothed = with_far(base_ref, far_ref, tile_ref)
     small = jnp.exp(-jnp.abs(smoothed))
-    inside = tissue_ref[:, pl.ds(pl.multiple_of(place[3] * width, width), width)] > 0
+    inside = tissue_ref[:, pl.ds(pl.multiple_of(lax.axis_index(SPACE) * width, width), width)] > 0
     soft = jnp.maximum(smoothed, 0.0) + jnp.log1p(small)
     factor_ref[...] = jnp.where(inside, soft, 0.0).astype(jnp.bfloat16)
     sigmoid = jnp.where(smoothed >= 0.0, 1.0, small) / (1.0 + small)
@@ -104,16 +103,17 @@
 
 
 def gene_kernel(
-    place, own_f, other_f, keep_ref, came_ref, weight_ref, turned_ref, back_ref, own_p, other_p, load_p, *, step, shift,
+    own_f, other_f, keep_ref, came_ref, weight_ref, turned_ref, back_ref, own_p, other_p, load_p, *, step, shift,
 ):
     width = own_f.shape[1]
     planes = keep_ref.shape[0]
     weights, turned = weight_ref[...], turned_ref[...]
     offset = jnp.concatenate([back_ref[...]] * (step // 128), axis=1)
     load = jnp.zeros(load_p.shape, jnp.float32)
-    plane = place[2] ^ shift
+    me = lax.axis_index(SPACE)
+    plane = (me >> 2) ^ shift
     for half, (field, out) in enumerate(((own_f, own_p), (other_f, other_p))):
-        row = lax.rem(place[1] + half, 2)
+        row = ((me >> 1) + half) & 1
         for at in range(0, width, step):
             f = field[:, at : at + step]
             rate = jnp.dot(turned, f, preferred_element_type=jnp.float32) + offset
@@ -126,13 +126,13 @@
     load_p[...] = load
 
 
-def gene_sums(place, shift, own_f, other_f, keep, came, weights, turned, back, kinds):
+def gene_sums(shift, own_f, other_f, keep, came, weights, turned, back, kinds):
     factors, width = own_f.shape
     genes = keep.shape[2]
     work = 2 * genes * 2 * width
     return pl.pallas_call(
         functools.partial(gene_kernel, step=1024, shift=shift),
-        in_specs=[SMEM] + [VMEM] * 7,
+        in_specs=[VMEM] * 7,
         out_specs=[VMEM] * 3,
         out_shape=[
             jax.ShapeDtypeStruct(own_f.shape, kinds[0]),
@@ -141,7 +141,7 @@
         ],
         compiler_params=params(12),
         cost_estimate=cost(6 * factors * work, 3 * work, work),
-    )(place, own_f, other_f, keep, came, weights, turned, back)
+    )(own_f, other_f, keep, came, weights, turned, back)
 
 
 def last_kernel(base_ref, far_ref, tile_ref, out_ref):
@@ -157,8 +157,6 @@
     genes, total_spots = counts.shape
     count = lax.axis_size(SPACE)
     planes = count // 4
-    me = lax.axis_index(SPACE)
-    place = jnp.stack([me & 1, (me >> 1) & 1, me >> 2, me])
 
     def send(x, to):
         return lax.ppermute(x, SPACE, [(i, to(i)) for i in range(count)])
@@ -171,13 +169,12 @@
 
     over_core = lambda i: i ^ 1
     over_row = lambda i: i ^ 2
-    along = lambda s: lambda i: i ^ (4 * s)
-
-    ready = after(latent, place)
-    far = chips(ready)
-    near = send(ready, over_core)
-    away = cast_counts(place, counts, planes, width, 1)
-    keep = cast_counts(place, counts, planes, width, 0)
+    along = lambda s: lambda i: i ^ 4 * s
+
+    far = chips(latent)
+    near = send(latent, over_core)
+    away = cast_counts(counts, planes, width, 1)
+    keep = cast_counts(counts, planes, width, 0)
     other_w, other_b = send(loading, over_core), send(background, over_core)
     strength = coupling.reshape(1, factors)
     full = jax.ShapeDtypeStruct
@@ -195,47 +192,32 @@
     )(loading, other_w, background.reshape(1, genes), other_b.reshape(1, genes))
     field, slope = pl.pallas_call(
         functools.partial(factor_kernel, scale=1.0 / (genes * count)),
-        in_specs=[SMEM] + [VMEM] * 4,
+        in_specs=[VMEM] * 4,
         out_specs=[VMEM] * 2,
         out_shape=[full(latent.shape, jnp.bfloat16), full(latent.shape, jnp.float32)],
         compiler_params=params(8),
         cost_estimate=cost(latent.size * 20, latent.size * 18, latent.size * 3),
-    )(after(place, keep, weights), base, far, tile, tissue.reshape(1, total_spots))
+    )(after(base, keep, weights), far, tile, tissue.reshape(1, total_spots))
     came = send(after(away, field), over_core)
 
-    order = [0, 1, 2, 3]
-    send_ties, kernel_ties, sum_ties = {3: (('K', 0),), 2: (('K', 0),)}, {}, {}
-    marks = {}
-    held = lambda x, names: after(x, *[marks[n] for n in names if n in marks]) if names else x
-    narrow, full_width = jnp.bfloat16, jnp.float32
-    fields = {s: field if s == 0 else send(field, along(s)) for s in order}
-    for s in order:
-        marks["G", s] = fields[s]
+    fields = {s: field if s == 0 else send(field, along(s)) for s in range(planes)}
     others = {0: send(field, over_row)}
-    marks["H", 0] = others[0]
+    sums = {}
     loads = None
-    sums = {}
-    for s in order:
+    for s in range(planes):
         if s == 1:
             others[1] = send(others[0], along(1))
         elif s:
-            others[s] = send(held(fields[s], send_ties.get(s, ())), over_row)
-        kinds = (full_width if s != 1 else narrow, full_width if s == 0 else narrow)
-        own_p, other_p, load = gene_sums(
-            held(place, kernel_ties.get(s, ())), s, fields[s], others[s], keep, came, weights, turned, back, kinds
-        )
-        marks["K", s] = load
-        loads = load if loads is None else loads + load
-        sums[s] = own_p, other_p
+            others[s] = send(after(fields[s], sums[0][2]), over_row)
+        kinds = {0: (jnp.float32, jnp.float32), 1: (jnp.bfloat16, jnp.bfloat16)}.get(s, (jnp.float32, jnp.bfloat16))
+        sums[s] = gene_sums(s, fields[s], others[s], keep, came, weights, turned, back, kinds)
+        loads = sums[s][2] if loads is None else loads + sums[s][2]
     own_0 = sums[0][0] + send(sums[1][0], along(1)).astype(jnp.float32)
-    other_0 = sums[0][1] + send(sums[1][1], along(1)).astype(jnp.float32)
-    total = own_0 + send(held(other_0.astype(jnp.bfloat16), sum_ties.get(0, ())), over_row).astype(jnp.float32)
-    marks["S", 0] = total
-    for s in order:
-        if s > 1:
-            own_p, other_p = sums[s]
-            summed = own_p + send(held(other_p, sum_ties.get(s, ())), over_row).astype(jnp.float32)
-            total = total + send(summed.astype(jnp.bfloat16), along(s)).astype(jnp.float32)
+    other_0 = (sums[0][1] + send(sums[1][1], along(1)).astype(jnp.float32)).astype(jnp.bfloat16)
+    total = own_0 + send(other_0, over_row).astype(jnp.float32)
+    for s in range(2, planes):
+        summed = sums[s][0] + send(sums[s][1], over_row).astype(jnp.float32)
+        total = total + send(summed.astype(jnp.bfloat16), along(s)).astype(jnp.float32)
     grad_smooth = total * slope
     swapped = send(after(loads, grad_smooth)[:, genes:], over_core)
     rounded = grad_smooth.astype(jnp.bfloat16)

time: 60.8 us -> 59.7 us (0.982)
  Pallas kernels: 11.3 us -> 7.49 us
  waiting for transfers between devices: 15.1 us -> 18.8 us
  starting transfers between devices: 28 us -> 27 us
    ppermute x20, waiting for transfers between devices: 13 us -> 15.7 us  [send(): return lax.ppermute(x, SPACE, [(i, to(i)) for i in range(count)])]
    pallas_call x4, Pallas kernels: 6.82 us -> 4.66 us  [gene_sums(): pl.pallas_call(functools.partial(gene_kernel, step=1024, shift=shift), in...]
    pallas_call x2, Pallas kernels: 2.3 us -> 1.21 us  [cast_counts(): pl.pallas_call(functools.partial(cast_kernel, turn=turn), in_specs=[pl.Bl...]
    ppermute x2, waiting for transfers between devices: 2.14 us -> 3.08 us  [chips(): lax.ppermute(x, SPACE, [(i, across(i)) for i in range(count) if 0 <= acro...]
    ppermute x20, starting transfers between devices: 21 us -> 20.4 us  [send(): return lax.ppermute(x, SPACE, [(i, to(i)) for i in range(count)])]
  transfers between devices with their start and end apart: 22 -> 22, of which waited for: 9 -> 11; matrix products, arithmetic and copies ran while one was open for 1% -> 1% of each run, Pallas kernels for 16% -> 11%
where the time goes in v5:
time: 59.7 us; the launch traced here: 58.5 us
  starting transfers between devices  27 us (45%)
  waiting for transfers between devices  18.8 us (31%)
  Pallas kernels  7.49 us (13%)
  local copies, waits for them, and re-layouts  3.55 us (6%)
  between operations  0.85 us (1%)
  other arithmetic  0.78 us (1%)
    ppermute x20, starting transfers between devices, send(): return lax.ppermute(x, SPACE, [(i, to(i)) for i in range(count)])  20.4 us
    ppermute x20, waiting for transfers between devices, send(): return lax.ppermute(x, SPACE, [(i, to(i)) for i in range(count)])  15.7 us
    ppermute x2, starting transfers between devices, chips(): lax.ppermute(x, SPACE, [(i, across(i)) for i in range(count) if 0 <= acro...  6.64 us
    pallas_call x4, Pallas kernels, gene_sums(): pl.pallas_call(functools.partial(gene_kernel, step=1024, shift=shift), in...  4.66 us
    unnamed x12, local copies, waits for them, and re-layouts  3.48 us
    ppermute x2, waiting for transfers between devices, chips(): lax.ppermute(x, SPACE, [(i, across(i)) for i in range(count) if 0 <= acro...  3.08 us
    pallas_call x2, Pallas kernels, cast_counts(): pl.pallas_call(functools.partial(cast_kernel, turn=turn), in_specs=[pl.Bl...  1.21 us
  transfers between devices with their start and end apart: 22, of which 11 were waited for; matrix products, arithmetic and copies ran while one was open for 1% of the time, Pallas kernels for 11%

profile of v5, /device:TPU:1, one launch (start us, length us, event | category | flops | bytes accessed | tf_op | source)
XLA Modules:
  0.0 58.5 jit_solution(13339093364551607362)
XLA Ops:
  0.6 0.1 collective-permute-start
  0.8 4.5 %collective-permute-start.3 = (f32[32,2048]{1,0:T(8,128)}, f32[32,2048]{1,0:T(8,128)S(1)}, u32[]{:S(2)}, u32[]{:S(2)}) collective-permute-start(f32[32,2048]{1,0:T(8,128)} %values_ref.1), channel_id=1, source_target_pairs={{1,2},{2,1},{3,4},{4,3},{5,6},{6,5},{7,8},{8,7},{9,10},{10,9},{11,... | collective-permute-start | bytes 786440 | tf_op jit(solution)/shard_map/ppermute | solution.py:168
  5.3 0.1 collective-permute-start.1
  5.3 0.5 collective-permute-start.2
  5.8 3.4 %copy-done = s32[64,32768]{1,0:T(8,128)S(1)} copy-done((s32[64,32768]{1,0:T(8,128)S(1)}, s32[64,32768]{1,0:T(8,128)}, u32[]{:S(2)}) %copy-start) | copy-done | bytes 8388632
  9.2 0.6 %shard_map.78.keep_ref = bf16[4,2,64,2048]{3,2,1,0:T(8,128)(2,1)S(1)} custom-call(s32[64,32768]{1,0:T(8,128)S(1)} %copy-done), custom_call_target="tpu_custom_call" | custom-call | flops 2097152 | bytes 6291456 | tf_op jit(solution)/shard_map/pallas_call | solution.py:38
  9.8 0.0 copy-start.3
  9.8 0.0 copy-start.5
  9.8 0.0 copy-start.1
  9.9 0.0 copy-start.4
  9.9 0.0 copy-start.2
  9.9 0.6 %shard_map.81 = bf16[4,2,64,2048]{3,2,1,0:T(8,128)(2,1)S(1)} custom-call(s32[64,32768]{1,0:T(8,128)S(1)} %copy-done), custom_call_target="tpu_custom_call" | custom-call | flops 2097152 | bytes 6291456 | tf_op jit(solution)/shard_map/pallas_call | solution.py:38
  10.5 0.0 collective-permute-done.2
  10.5 0.0 collective-permute-done.1.other_w
  10.5 0.2 shard_map.79
  10.7 0.0 collective-permute-done.near_ref
  10.7 0.1 copy-done.1
  10.8 0.2 shard_map.77
  11.0 0.6 %collective-permute-done.3.far_ref = f32[32,2048]{1,0:T(8,128)S(1)} collective-permute-done((f32[32,2048]{1,0:T(8,128)}, f32[32,2048]{1,0:T(8,128)S(1)}, u32[]{:S(2)}, u32[]{:S(2)}) %collective-permute-start.3) | collective-permute-done | bytes 262176 | tf_op jit(solution)/shard_map/ppermute | solution.py:168
  11.7 0.2 shard_map.80
  11.9 0.1 collective-permute-start.5
  12.0 2.5 %collective-permute-start.4 = (bf16[32,2048]{1,0:T(8,128)(2,1)S(1)}, bf16[32,2048]{1,0:T(8,128)(2,1)S(1)}, u32[]{:S(2)}, u32[]{:S(2)}) collective-permute-start(bf16[32,2048]{1,0:T(8,128)(2,1)S(1)} %get-tuple-element.33.own_f), channel_id=1, source_target_pairs={{0,2},{1,3},{2,0},{3,1},{4,6},{5,7},{6,4},{7,5},{8,10},{9,11},{10,... | collective-permute-start | bytes 393224 | tf_op jit(solution)/shard_map/ppermute | solution.py:162
  14.5 2.3 %collective-permute-start.11 = (bf16[32,2048]{1,0:T(8,128)(2,1)S(1)}, bf16[32,2048]{1,0:T(8,128)(2,1)S(1)}, u32[]{:S(2)}, u32[]{:S(2)}) collective-permute-start(bf16[32,2048]{1,0:T(8,128)(2,1)S(1)} %get-tuple-element.33.own_f), channel_id=1, source_target_pairs={{0,8},{1,9},{2,10},{3,11},{4,12},{5,13},{6,14},{7,15},{8,0},{9,1},... | collective-permute-start | bytes 393224 | tf_op jit(solution)/shard_map/ppermute | solution.py:162
  16.8 0.2 collective-permute-start.6
  17.0 1.3 %collective-permute-done.4.other_f = bf16[32,2048]{1,0:T(8,128)(2,1)S(1)} collective-permute-done((bf16[32,2048]{1,0:T(8,128)(2,1)S(1)}, bf16[32,2048]{1,0:T(8,128)(2,1)S(1)}, u32[]{:S(2)}, u32[]{:S(2)}) %collective-permute-start.4) | collective-permute-done | bytes 131104 | tf_op jit(solution)/shard_map/ppermute | solution.py:162
  18.3 1.0 %collective-permute-start.7 = (bf16[32,2048]{1,0:T(8,128)(2,1)S(1)}, bf16[32,2048]{1,0:T(8,128)(2,1)S(1)}, u32[]{:S(2)}, u32[]{:S(2)}) collective-permute-start(bf16[32,2048]{1,0:T(8,128)(2,1)S(1)} %collective-permute-done.4.other_f), channel_id=1, source_target_pairs={{0,4},{1,5},{2,6},{3,7},{4,0},{5,1},{6,2},{7,3},{8,12},{9,13},{10,... | collective-permute-start | bytes 393224 | tf_op jit(solution)/shard_map/ppermute | solution.py:162
  19.2 2.2 %collective-permute-start.15 = (bf16[32,2048]{1,0:T(8,128)(2,1)S(1)}, bf16[32,2048]{1,0:T(8,128)(2,1)S(1)}, u32[]{:S(2)}, u32[]{:S(2)}) collective-permute-start(bf16[32,2048]{1,0:T(8,128)(2,1)S(1)} %get-tuple-element.33.own_f), channel_id=1, source_target_pairs={{0,12},{1,13},{2,14},{3,15},{4,8},{5,9},{6,10},{7,11},{8,4},{9,5},... | collective-permute-start | bytes 393224 | tf_op jit(solution)/shard_map/ppermute | solution.py:162
  21.4 0.0 collective-permute-done.5.came_ref
  21.4 1.2 %shard_map.82 = (f32[32,2048]{1,0:T(8,128)S(1)}, f32[32,2048]{1,0:T(8,128)S(1)}, f32[32,128]{1,0:T(8,128)S(1)}) custom-call(bf16[32,2048]{1,0:T(8,128)(2,1)S(1)} %get-tuple-element.33.own_f, bf16[32,2048]{1,0:T(8,128)(2,1)S(1)} %collective-permute-done.4.other_f, bf16[4,2,64,2048]{3,2,1,0:T(8,128)(2,1)S(1)} %shard_map.78.keep_ref, ...), custom_call_target="tpu_custom_call" | custom-call | flops 100663296 | bytes 1572864 | tf_op jit(solution)/shard_map/pallas_call | solution.py:133
  22.6 0.3 collective-permute-done.11.own_f
  22.9 1.4 %collective-permute-start.12 = (bf16[32,2048]{1,0:T(8,128)(2,1)S(1)}, bf16[32,2048]{1,0:T(8,128)(2,1)S(1)}, u32[]{:S(2)}, u32[]{:S(2)}) collective-permute-start(bf16[32,2048]{1,0:T(8,128)(2,1)S(1)} %collective-permute-done.11.own_f), channel_id=1, source_target_pairs={{0,2},{1,3},{2,0},{3,1},{4,6},{5,7},{6,4},{7,5},{8,10},{9,11},{10,... | collective-permute-start | bytes 393224 | tf_op jit(solution)/shard_map/ppermute | solution.py:162
  24.3 0.0 collective-permute-done.6.own_f
  24.3 1.4 %collective-permute-done.7.other_f = bf16[32,2048]{1,0:T(8,128)(2,1)S(1)} collective-permute-done((bf16[32,2048]{1,0:T(8,128)(2,1)S(1)}, bf16[32,2048]{1,0:T(8,128)(2,1)S(1)}, u32[]{:S(2)}, u32[]{:S(2)}) %collective-permute-start.7) | collective-permute-done | bytes 131104 | tf_op jit(solution)/shard_map/ppermute | solution.py:162
  25.7 1.2 %shard_map.83 = (bf16[32,2048]{1,0:T(8,128)(2,1)S(1)}, bf16[32,2048]{1,0:T(8,128)(2,1)S(1)}, f32[32,128]{1,0:T(8,128)S(1)}) custom-call(bf16[32,2048]{1,0:T(8,128)(2,1)S(1)} %collective-permute-done.6.own_f, bf16[32,2048]{1,0:T(8,128)(2,1)S(1)} %collective-permute-done.7.other_f, bf16[4,2,64,2048]{3,2,1,0:T(8,128)(2,1)S(1)} %shard_map.78.keep_ref, ...), custom_call_target="tpu_custom_call" | custom-call | flops 100663296 | bytes 1572864 | tf_op jit(solution)/shard_map/pallas_call | solution.py:133
  26.9 1.6 %collective-permute-start.9 = (bf16[32,2048]{1,0:T(8,128)(2,1)S(1)}, bf16[32,2048]{1,0:T(8,128)(2,1)S(1)}, u32[]{:S(2)}, u32[]{:S(2)}) collective-permute-start(bf16[32,2048]{1,0:T(8,128)(2,1)S(1)} %get-tuple-element.40), channel_id=1, source_target_pairs={{0,4},{1,5},{2,6},{3,7},{4,0},{5,1},{6,2},{7,3},{8,12},{9,13},{10,... | collective-permute-start | bytes 393224 | tf_op jit(solution)/shard_map/ppermute | solution.py:162
  28.4 1.2 %collective-permute-done.15.own_f = bf16[32,2048]{1,0:T(8,128)(2,1)S(1)} collective-permute-done((bf16[32,2048]{1,0:T(8,128)(2,1)S(1)}, bf16[32,2048]{1,0:T(8,128)(2,1)S(1)}, u32[]{:S(2)}, u32[]{:S(2)}) %collective-permute-start.15) | collective-permute-done | bytes 131104 | tf_op jit(solution)/shard_map/ppermute | solution.py:162
  29.6 0.4 collective-permute-start.16
  30.0 0.0 collective-permute-start.8
  30.0 0.0 collective-permute-done.12.other_f
  30.0 1.2 %shard_map.84 = (f32[32,2048]{1,0:T(8,128)S(1)}, bf16[32,2048]{1,0:T(8,128)(2,1)S(1)}, f32[32,128]{1,0:T(8,128)S(1)}) custom-call(bf16[32,2048]{1,0:T(8,128)(2,1)S(1)} %collective-permute-done.11.own_f, bf16[32,2048]{1,0:T(8,128)(2,1)S(1)} %collective-permute-done.12.other_f, bf16[4,2,64,2048]{3,2,1,0:T(8,128)(2,1)S(1)} %shard_map.78.keep_ref, ...), custom_call_target="tpu_custom_call" | custom-call | flops 100663296 | bytes 1572864 | tf_op jit(solution)/shard_map/pallas_call | solution.py:133
  31.1 1.2 %collective-permute-start.13 = (bf16[32,2048]{1,0:T(8,128)(2,1)S(1)}, bf16[32,2048]{1,0:T(8,128)(2,1)S(1)}, u32[]{:S(2)}, u32[]{:S(2)}) collective-permute-start(bf16[32,2048]{1,0:T(8,128)(2,1)S(1)} %get-tuple-element.44), channel_id=1, source_target_pairs={{0,2},{1,3},{2,0},{3,1},{4,6},{5,7},{6,4},{7,5},{8,10},{9,11},{10,... | collective-permute-start | bytes 393224 | tf_op jit(solution)/shard_map/ppermute | solution.py:162
  32.3 0.0 collective-permute-done.9
  32.4 0.4 collective-permute-start.10
  32.8 1.0 %collective-permute-done.16.other_f = bf16[32,2048]{1,0:T(8,128)(2,1)S(1)} collective-permute-done((bf16[32,2048]{1,0:T(8,128)(2,1)S(1)}, bf16[32,2048]{1,0:T(8,128)(2,1)S(1)}, u32[]{:S(2)}, u32[]{:S(2)}) %collective-permute-start.16) | collective-permute-done | bytes 131104 | tf_op jit(solution)/shard_map/ppermute | solution.py:162
  33.7 1.2 %shard_map.85 = (f32[32,2048]{1,0:T(8,128)S(1)}, bf16[32,2048]{1,0:T(8,128)(2,1)S(1)}, f32[32,128]{1,0:T(8,128)S(1)}) custom-call(bf16[32,2048]{1,0:T(8,128)(2,1)S(1)} %collective-permute-done.15.own_f, bf16[32,2048]{1,0:T(8,128)(2,1)S(1)} %collective-permute-done.16.other_f, bf16[4,2,64,2048]{3,2,1,0:T(8,128)(2,1)S(1)} %shard_map.78.keep_ref, ...), custom_call_target="tpu_custom_call" | custom-call | flops 100663296 | bytes 1572864 | tf_op jit(solution)/shard_map/pallas_call | solution.py:133
  34.9 0.2 collective-permute-start.17
  35.1 1.5 %collective-permute-done.13 = bf16[32,2048]{1,0:T(8,128)(2,1)S(1)} collective-permute-done((bf16[32,2048]{1,0:T(8,128)(2,1)S(1)}, bf16[32,2048]{1,0:T(8,128)(2,1)S(1)}, u32[]{:S(2)}, u32[]{:S(2)}) %collective-permute-start.13) | collective-permute-done | bytes 131104 | tf_op jit(solution)/shard_map/ppermute | solution.py:162
  36.6 1.1 %collective-permute-start.14 = (bf16[32,2048]{1,0:T(8,128)(2,1)S(1)}, bf16[32,2048]{1,0:T(8,128)(2,1)S(1)}, u32[]{:S(2)}, u32[]{:S(2)}) collective-permute-start(bf16[32,2048]{1,0:T(8,128)(2,1)S(1)} %add_convert_fusion.1), channel_id=1, source_target_pairs={{0,8},{1,9},{2,10},{3,11},{4,12},{5,13},{6,14},{7,15},{8,0},{9,1},... | collective-permute-start | bytes 393224 | tf_op jit(solution)/shard_map/ppermute | solution.py:162
  37.7 4.5 %collective-permute-done.17 = bf16[32,2048]{1,0:T(8,128)(2,1)S(1)} collective-permute-done((bf16[32,2048]{1,0:T(8,128)(2,1)S(1)}, bf16[32,2048]{1,0:T(8,128)(2,1)S(1)}, u32[]{:S(2)}, u32[]{:S(2)}) %collective-permute-start.17) | collective-permute-done | bytes 131104 | tf_op jit(solution)/shard_map/ppermute | solution.py:162
  42.3 1.9 %collective-permute-start.18 = (bf16[32,2048]{1,0:T(8,128)(2,1)S(1)}, bf16[32,2048]{1,0:T(8,128)(2,1)S(1)}, u32[]{:S(2)}, u32[]{:S(2)}) collective-permute-start(bf16[32,2048]{1,0:T(8,128)(2,1)S(1)} %add_convert_fusion), channel_id=1, source_target_pairs={{0,12},{1,13},{2,14},{3,15},{4,8},{5,9},{6,10},{7,11},{8,4},{9,5},... | collective-permute-start | bytes 393224 | tf_op jit(solution)/shard_map/ppermute | solution.py:162
  44.1 0.0 collective-permute-done.8
  44.1 0.0 collective-permute-done.10
  44.2 3.8 %collective-permute-done.18 = bf16[32,2048]{1,0:T(8,128)(2,1)S(1)} collective-permute-done((bf16[32,2048]{1,0:T(8,128)(2,1)S(1)}, bf16[32,2048]{1,0:T(8,128)(2,1)S(1)}, u32[]{:S(2)}, u32[]{:S(2)}) %collective-permute-start.18) | collective-permute-done | bytes 131104 | tf_op jit(solution)/shard_map/ppermute | solution.py:162
  47.9 0.1 fusion.1
  48.0 0.1 slice.6
  48.1 3.4 %collective-permute-start.19 = (f32[32,64]{1,0:T(8,128)S(1)}, f32[32,64]{1,0:T(8,128)S(1)}, u32[]{:S(2)}, u32[]{:S(2)}) collective-permute-start(f32[32,64]{1,0:T(8,128)S(1)} %slice.6), channel_id=1, source_target_pairs={{0,1},{1,0},{2,3},{3,2},{4,5},{5,4},{6,7},{7,6},{8,9},{9,8},{10,11... | collective-permute-start | bytes 24584 | tf_op jit(solution)/shard_map/ppermute | solution.py:162
  51.5 2.1 %collective-permute-start.21 = (bf16[32,2048]{1,0:T(8,128)(2,1)S(1)}, bf16[32,2048]{1,0:T(8,128)(2,1)S(1)}, u32[]{:S(2)}, u32[]{:S(2)}) collective-permute-start(bf16[32,2048]{1,0:T(8,128)(2,1)S(1)} %get-tuple-element.53), channel_id=1, source_target_pairs={{1,2},{2,1},{3,4},{4,3},{5,6},{6,5},{7,8},{8,7},{9,10},{10,9},{11,... | collective-permute-start | bytes 393224 | tf_op jit(solution)/shard_map/ppermute | solution.py:168
  53.6 0.0 collective-permute-done.19
  53.7 0.1 collective-permute-start.20
  53.7 0.6 %fusion = f32[32,64]{1,0:T(8,128)} fusion(f32[32,64]{1,0:T(8,128)S(1)} %collective-permute-done.19, f32[32,128]{1,0:T(8,128)S(1)} %add_add_fusion), kind=kLoop, calls=%fused_computation.5 | loop fusion | flops 4096 | bytes 24576 | tf_op jit(solution)/shard_map/div | solution.py:235
  54.3 0.7 %collective-permute-done.20.near_ref = bf16[32,2048]{1,0:T(8,128)(2,1)S(1)} collective-permute-done((bf16[32,2048]{1,0:T(8,128)(2,1)S(1)}, bf16[32,2048]{1,0:T(8,128)(2,1)S(1)}, u32[]{:S(2)}, u32[]{:S(2)}) %collective-permute-start.20) | collective-permute-done | bytes 131104 | tf_op jit(solution)/shard_map/ppermute | solution.py:162
  55.1 0.2 shard_map.86
  55.3 2.4 %collective-permute-done.21.far_ref = bf16[32,2048]{1,0:T(8,128)(2,1)S(1)} collective-permute-done((bf16[32,2048]{1,0:T(8,128)(2,1)S(1)}, bf16[32,2048]{1,0:T(8,128)(2,1)S(1)}, u32[]{:S(2)}, u32[]{:S(2)}) %collective-permute-start.21) | collective-permute-done | bytes 131104 | tf_op jit(solution)/shard_map/ppermute | solution.py:168
  57.8 0.7 %shard_map.87 = f32[32,2048]{1,0:T(8,128)} custom-call(f32[32,2048]{1,0:T(8,128)S(1)} %get-tuple-element.54.base_ref, bf16[32,2048]{1,0:T(8,128)(2,1)S(1)} %collective-permute-done.21.far_ref, f32[32,128]{1,0:T(8,128)S(1)} %get-tuple-element.55.tile_ref), custom_call_target="tpu_custom_call" | custom-call | flops 655360 | bytes 786432 | tf_op jit(solution)/shard_map/pallas_call | solution.py:227
  (10 shorter events, 0.1 us)
Async XLA Ops:
  0.6 10.1 %collective-permute-start = (f32[32,2048]{1,0:T(8,128)}, f32[32,2048]{1,0:T(8,128)S(1)}, u32[]{:S(2)}, u32[]{:S(2)}) collective-permute-start(f32[32,2048]{1,0:T(8,128)} %values_ref.1), channel_id=1, source_target_pairs={{0,1},{1,0},{2,3},{3,2},{4,5},{5,4},{6,7},{7,6},{8,9},{9,8},{10,11... | collective-permute-start | bytes 786440 | tf_op jit(solution)/shard_map/ppermute | solution.py:162
  0.8 10.9 %collective-permute-start.3 = (f32[32,2048]{1,0:T(8,128)}, f32[32,2048]{1,0:T(8,128)S(1)}, u32[]{:S(2)}, u32[]{:S(2)}) collective-permute-start(f32[32,2048]{1,0:T(8,128)} %values_ref.1), channel_id=1, source_target_pairs={{1,2},{2,1},{3,4},{4,3},{5,6},{6,5},{7,8},{8,7},{9,10},{10,9},{11,... | collective-permute-start | bytes 786440 | tf_op jit(solution)/shard_map/ppermute | solution.py:168
  5.3 5.3 %collective-permute-start.1 = (bf16[32,64]{1,0:T(8,128)(2,1)}, bf16[32,64]{1,0:T(8,128)(2,1)S(1)}, u32[]{:S(2)}, u32[]{:S(2)}) collective-permute-start(bf16[32,64]{1,0:T(8,128)(2,1)} %own_w.1), channel_id=1, source_target_pairs={{0,1},{1,0},{2,3},{3,2},{4,5},{5,4},{6,7},{7,6},{8,9},{9,8},{10,11... | collective-permute-start | bytes 12296 | tf_op jit(solution)/shard_map/ppermute | solution.py:162
  5.3 5.2 %collective-permute-start.2 = (f32[64]{0:T(128)}, f32[64]{0:T(128)S(1)}, u32[]{:S(2)}, u32[]{:S(2)}) collective-permute-start(f32[64]{0:T(128)} %param.9), channel_id=1, source_target_pairs={{0,1},{1,0},{2,3},{3,2},{4,5},{5,4},{6,7},{7,6},{8,9},{9,8},{10,11... | collective-permute-start | bytes 776 | tf_op jit(solution)/shard_map/ppermute | solution.py:162
  5.8 3.4 %copy-start = (s32[64,32768]{1,0:T(8,128)S(1)}, s32[64,32768]{1,0:T(8,128)}, u32[]{:S(2)}) copy-start(s32[64,32768]{1,0:T(8,128)} %counts_ref.3) | copy-start | bytes 25165828
  9.8 0.7 %copy-start.3 = (bf16[32,64]{1,0:T(8,128)(2,1)S(1)}, bf16[32,64]{1,0:T(8,128)(2,1)}, u32[]{:S(2)}) copy-start(bf16[32,64]{1,0:T(8,128)(2,1)} %own_w.1) | copy-start | bytes 12292
  9.8 0.7 %copy-start.5 = (f32[64]{0:T(128)S(1)}, f32[64]{0:T(128)}, u32[]{:S(2)}) copy-start(f32[64]{0:T(128)} %param.9) | copy-start | bytes 772
  9.8 1.0 %copy-start.1 = (f32[32,2048]{1,0:T(8,128)S(1)}, f32[32,2048]{1,0:T(8,128)}, u32[]{:S(2)}) copy-start(f32[32,2048]{1,0:T(8,128)} %values_ref.1) | copy-start | bytes 786436
  9.9 1.0 %copy-start.4 = (f32[32]{0:T(128)S(1)}, f32[32]{0:T(128)}, u32[]{:S(2)}) copy-start(f32[32]{0:T(128)} %param.10) | copy-start | bytes 388
  9.9 1.8 %copy-start.2 = (s32[32768]{0:T(1024)S(1)}, s32[32768]{0:T(1024)}, u32[]{:S(2)}) copy-start(s32[32768]{0:T(1024)} %param.11) | copy-start | bytes 393220
  11.9 9.5 %collective-permute-start.5 = (bf16[4,2,64,2048]{3,2,1,0:T(8,128)(2,1)S(1)}, bf16[4,2,64,2048]{3,2,1,0:T(8,128)(2,1)S(1)}, u32[]{:S(2)}, u32[]{:S(2)}) collective-permute-start(bf16[4,2,64,2048]{3,2,1,0:T(8,128)(2,1)S(1)} %shard_map.81), channel_id=1, source_target_pairs={{0,1},{1,0},{2,3},{3,2},{4,5},{5,4},{6,7},{7,6},{8,9},{9,8},{10,11... | collective-permute-start | bytes 6291464 | tf_op jit(solution)/shard_map/ppermute | solution.py:162
  12.0 6.3 %collective-permute-start.4 = (bf16[32,2048]{1,0:T(8,128)(2,1)S(1)}, bf16[32,2048]{1,0:T(8,128)(2,1)S(1)}, u32[]{:S(2)}, u32[]{:S(2)}) collective-permute-start(bf16[32,2048]{1,0:T(8,128)(2,1)S(1)} %get-tuple-element.33.own_f), channel_id=1, source_target_pairs={{0,2},{1,3},{2,0},{3,1},{4,6},{5,7},{6,4},{7,5},{8,10},{9,11},{10,... | collective-permute-start | bytes 393224 | tf_op jit(solution)/shard_map/ppermute | solution.py:162
  14.5 8.4 %collective-permute-start.11 = (bf16[32,2048]{1,0:T(8,128)(2,1)S(1)}, bf16[32,2048]{1,0:T(8,128)(2,1)S(1)}, u32[]{:S(2)}, u32[]{:S(2)}) collective-permute-start(bf16[32,2048]{1,0:T(8,128)(2,1)S(1)} %get-tuple-element.33.own_f), channel_id=1, source_target_pairs={{0,8},{1,9},{2,10},{3,11},{4,12},{5,13},{6,14},{7,15},{8,0},{9,1},... | collective-permute-start | bytes 393224 | tf_op jit(solution)/shard_map/ppermute | solution.py:162
  16.8 7.5 %collective-permute-start.6 = (bf16[32,2048]{1,0:T(8,128)(2,1)S(1)}, bf16[32,2048]{1,0:T(8,128)(2,1)S(1)}, u32[]{:S(2)}, u32[]{:S(2)}) collective-permute-start(bf16[32,2048]{1,0:T(8,128)(2,1)S(1)} %get-tuple-element.33.own_f), channel_id=1, source_target_pairs={{0,4},{1,5},{2,6},{3,7},{4,0},{5,1},{6,2},{7,3},{8,12},{9,13},{10,... | collective-permute-start | bytes 393224 | tf_op jit(solution)/shard_map/ppermute | solution.py:162
  18.3 7.5 %collective-permute-start.7 = (bf16[32,2048]{1,0:T(8,128)(2,1)S(1)}, bf16[32,2048]{1,0:T(8,128)(2,1)S(1)}, u32[]{:S(2)}, u32[]{:S(2)}) collective-permute-start(bf16[32,2048]{1,0:T(8,128)(2,1)S(1)} %collective-permute-done.4.other_f), channel_id=1, source_target_pairs={{0,4},{1,5},{2,6},{3,7},{4,0},{5,1},{6,2},{7,3},{8,12},{9,13},{10,... | collective-permute-start | bytes 393224 | tf_op jit(solution)/shard_map/ppermute | solution.py:162
  19.2 10.4 %collective-permute-start.15 = (bf16[32,2048]{1,0:T(8,128)(2,1)S(1)}, bf16[32,2048]{1,0:T(8,128)(2,1)S(1)}, u32[]{:S(2)}, u32[]{:S(2)}) collective-permute-start(bf16[32,2048]{1,0:T(8,128)(2,1)S(1)} %get-tuple-element.33.own_f), channel_id=1, source_target_pairs={{0,12},{1,13},{2,14},{3,15},{4,8},{5,9},{6,10},{7,11},{8,4},{9,5},... | collective-permute-start | bytes 393224 | tf_op jit(solution)/shard_map/ppermute | solution.py:162
  22.9 7.0 %collective-permute-start.12 = (bf16[32,2048]{1,0:T(8,128)(2,1)S(1)}, bf16[32,2048]{1,0:T(8,128)(2,1)S(1)}, u32[]{:S(2)}, u32[]{:S(2)}) collective-permute-start(bf16[32,2048]{1,0:T(8,128)(2,1)S(1)} %collective-permute-done.11.own_f), channel_id=1, source_target_pairs={{0,2},{1,3},{2,0},{3,1},{4,6},{5,7},{6,4},{7,5},{8,10},{9,11},{10,... | collective-permute-start | bytes 393224 | tf_op jit(solution)/shard_map/ppermute | solution.py:162
  26.9 5.4 %collective-permute-start.9 = (bf16[32,2048]{1,0:T(8,128)(2,1)S(1)}, bf16[32,2048]{1,0:T(8,128)(2,1)S(1)}, u32[]{:S(2)}, u32[]{:S(2)}) collective-permute-start(bf16[32,2048]{1,0:T(8,128)(2,1)S(1)} %get-tuple-element.40), channel_id=1, source_target_pairs={{0,4},{1,5},{2,6},{3,7},{4,0},{5,1},{6,2},{7,3},{8,12},{9,13},{10,... | collective-permute-start | bytes 393224 | tf_op jit(solution)/shard_map/ppermute | solution.py:162
  29.6 4.1 %collective-permute-start.16 = (bf16[32,2048]{1,0:T(8,128)(2,1)S(1)}, bf16[32,2048]{1,0:T(8,128)(2,1)S(1)}, u32[]{:S(2)}, u32[]{:S(2)}) collective-permute-start(bf16[32,2048]{1,0:T(8,128)(2,1)S(1)} %collective-permute-done.15.own_f), channel_id=1, source_target_pairs={{0,2},{1,3},{2,0},{3,1},{4,6},{5,7},{6,4},{7,5},{8,10},{9,11},{10,... | collective-permute-start | bytes 393224 | tf_op jit(solution)/shard_map/ppermute | solution.py:162
  30.0 14.2 %collective-permute-start.8 = (bf16[32,2048]{1,0:T(8,128)(2,1)S(1)}, bf16[32,2048]{1,0:T(8,128)(2,1)S(1)}, u32[]{:S(2)}, u32[]{:S(2)}) collective-permute-start(bf16[32,2048]{1,0:T(8,128)(2,1)S(1)} %get-tuple-element.38), channel_id=1, source_target_pairs={{0,4},{1,5},{2,6},{3,7},{4,0},{5,1},{6,2},{7,3},{8,12},{9,13},{10,... | collective-permute-start | bytes 393224 | tf_op jit(solution)/shard_map/ppermute | solution.py:162
  31.1 5.5 %collective-permute-start.13 = (bf16[32,2048]{1,0:T(8,128)(2,1)S(1)}, bf16[32,2048]{1,0:T(8,128)(2,1)S(1)}, u32[]{:S(2)}, u32[]{:S(2)}) collective-permute-start(bf16[32,2048]{1,0:T(8,128)(2,1)S(1)} %get-tuple-element.44), channel_id=1, source_target_pairs={{0,2},{1,3},{2,0},{3,1},{4,6},{5,7},{6,4},{7,5},{8,10},{9,11},{10,... | collective-permute-start | bytes 393224 | tf_op jit(solution)/shard_map/ppermute | solution.py:162
  32.4 11.8 %collective-permute-start.10 = (bf16[32,2048]{1,0:T(8,128)(2,1)S(1)}, bf16[32,2048]{1,0:T(8,128)(2,1)S(1)}, u32[]{:S(2)}, u32[]{:S(2)}) collective-permute-start(bf16[32,2048]{1,0:T(8,128)(2,1)S(1)} %add_convert_fusion.2), channel_id=1, source_target_pairs={{0,2},{1,3},{2,0},{3,1},{4,6},{5,7},{6,4},{7,5},{8,10},{9,11},{10,... | collective-permute-start | bytes 393224 | tf_op jit(solution)/shard_map/ppermute | solution.py:162
  34.9 7.3 %collective-permute-start.17 = (bf16[32,2048]{1,0:T(8,128)(2,1)S(1)}, bf16[32,2048]{1,0:T(8,128)(2,1)S(1)}, u32[]{:S(2)}, u32[]{:S(2)}) collective-permute-start(bf16[32,2048]{1,0:T(8,128)(2,1)S(1)} %get-tuple-element.47), channel_id=1, source_target_pairs={{0,2},{1,3},{2,0},{3,1},{4,6},{5,7},{6,4},{7,5},{8,10},{9,11},{10,... | collective-permute-start | bytes 393224 | tf_op jit(solution)/shard_map/ppermute | solution.py:162
  36.6 7.5 %collective-permute-start.14 = (bf16[32,2048]{1,0:T(8,128)(2,1)S(1)}, bf16[32,2048]{1,0:T(8,128)(2,1)S(1)}, u32[]{:S(2)}, u32[]{:S(2)}) collective-permute-start(bf16[32,2048]{1,0:T(8,128)(2,1)S(1)} %add_convert_fusion.1), channel_id=1, source_target_pairs={{0,8},{1,9},{2,10},{3,11},{4,12},{5,13},{6,14},{7,15},{8,0},{9,1},... | collective-permute-start | bytes 393224 | tf_op jit(solution)/shard_map/ppermute | solution.py:162
  42.3 5.7 %collective-permute-start.18 = (bf16[32,2048]{1,0:T(8,128)(2,1)S(1)}, bf16[32,2048]{1,0:T(8,128)(2,1)S(1)}, u32[]{:S(2)}, u32[]{:S(2)}) collective-permute-start(bf16[32,2048]{1,0:T(8,128)(2,1)S(1)} %add_convert_fusion), channel_id=1, source_target_pairs={{0,12},{1,13},{2,14},{3,15},{4,8},{5,9},{6,10},{7,11},{8,4},{9,5},... | collective-permute-start | bytes 393224 | tf_op jit(solution)/shard_map/ppermute | solution.py:162
  48.1 5.5 %collective-permute-start.19 = (f32[32,64]{1,0:T(8,128)S(1)}, f32[32,64]{1,0:T(8,128)S(1)}, u32[]{:S(2)}, u32[]{:S(2)}) collective-permute-start(f32[32,64]{1,0:T(8,128)S(1)} %slice.6), channel_id=1, source_target_pairs={{0,1},{1,0},{2,3},{3,2},{4,5},{5,4},{6,7},{7,6},{8,9},{9,8},{10,11... | collective-permute-start | bytes 24584 | tf_op jit(solution)/shard_map/ppermute | solution.py:162
  51.5 6.3 %collective-permute-start.21 = (bf16[32,2048]{1,0:T(8,128)(2,1)S(1)}, bf16[32,2048]{1,0:T(8,128)(2,1)S(1)}, u32[]{:S(2)}, u32[]{:S(2)}) collective-permute-start(bf16[32,2048]{1,0:T(8,128)(2,1)S(1)} %get-tuple-element.53), channel_id=1, source_target_pairs={{1,2},{2,1},{3,4},{4,3},{5,6},{6,5},{7,8},{8,7},{9,10},{10,9},{11,... | collective-permute-start | bytes 393224 | tf_op jit(solution)/shard_map/ppermute | solution.py:168
  53.7 1.4 %collective-permute-start.20 = (bf16[32,2048]{1,0:T(8,128)(2,1)S(1)}, bf16[32,2048]{1,0:T(8,128)(2,1)S(1)}, u32[]{:S(2)}, u32[]{:S(2)}) collective-permute-start(bf16[32,2048]{1,0:T(8,128)(2,1)S(1)} %get-tuple-element.53), channel_id=1, source_target_pairs={{0,1},{1,0},{2,3},{3,2},{4,5},{5,4},{6,7},{7,6},{8,9},{9,8},{10,11... | collective-permute-start | bytes 393224 | tf_op jit(solution)/shard_map/ppermute | solution.py:162

commit v6 on v5

--- a/solution.py
+++ b/solution.py
@@ -9,6 +9,7 @@
 
 SPACE = "space"
 MIB = 1024 * 1024
+STEPS = 8191.0
 VMEM = pl.BlockSpec(memory_space=pltpu.VMEM)
 
 
@@ -77,8 +78,12 @@
     )(values, near, strength)
 
 
-def with_far(base_ref, far_ref, tile_ref):
-    wide = jnp.concatenate([tile_ref[...]] * (base_ref.shape[1] // 128), axis=1)
+def code_kernel(values_ref, out_ref):
+    out_ref[...] = jnp.round(values_ref[...] * STEPS).astype(jnp.int32).astype(jnp.int16)
+
+
+def with_far(base_ref, far_ref, tile_ref, step=1.0):
+    wide = jnp.concatenate([tile_ref[...] * step] * (base_ref.shape[1] // 128), axis=1)
     return base_ref[...] + wide * far_ref[...].astype(jnp.float32)
 
 
@@ -93,7 +98,7 @@
 
 def factor_kernel(base_ref, far_ref, tile_ref, tissue_ref, factor_ref, slope_ref, *, scale):
     width = base_ref.shape[1]
-    smoothed = with_far(base_ref, far_ref, tile_ref)
+    smoothed = with_far(base_ref, far_ref, tile_ref, 1.0 / STEPS)
     small = jnp.exp(-jnp.abs(smoothed))
     inside = tissue_ref[:, pl.ds(pl.multiple_of(lax.axis_index(SPACE) * width, width), width)] > 0
     soft = jnp.maximum(smoothed, 0.0) + jnp.log1p(small)
@@ -171,7 +176,15 @@
     over_row = lambda i: i ^ 2
     along = lambda s: lambda i: i ^ 4 * s
 
-    far = chips(latent)
+    coded = pl.pallas_call(
+        code_kernel,
+        in_specs=[VMEM],
+        out_specs=VMEM,
+        out_shape=jax.ShapeDtypeStruct(latent.shape, jnp.int16),
+        compiler_params=params(8),
+        cost_estimate=cost(latent.size * 2, latent.size * 6),
+    )(latent)
+    far = chips(coded)
     near = send(latent, over_core)
     away = cast_counts(counts, planes, width, 1)
     keep = cast_counts(counts, planes, width, 0)
@@ -197,7 +210,7 @@
         out_shape=[full(latent.shape, jnp.bfloat16), full(latent.shape, jnp.float32)],
         compiler_params=params(8),
         cost_estimate=cost(latent.size * 20, latent.size * 18, latent.size * 3),
-    )(after(base, keep, weights), far, tile, tissue.reshape(1, total_spots))
+    )(after(base, weights), far, tile, tissue.reshape(1, total_spots))
     came = send(after(away, field), over_core)
 
     fields = {s: field if s == 0 else send(field, along(s)) for s in range(planes)}

time: 59.7 us -> 58.5 us (0.980)
  the two profiles are of different devices: /device:TPU:1 before, /device:TPU:17 now
where the time goes in v6:
time: 58.5 us; the launch traced here: 58.3 us
  starting transfers between devices  22.4 us (38%)
  waiting for transfers between devices  22.2 us (38%)
  Pallas kernels  7.51 us (13%)
  local copies, waits for them, and re-layouts  4.48 us (8%)
  between operations  0.82 us (1%)
  other arithmetic  0.81 us (1%)
    ppermute x20, waiting for transfers between devices, send(): return lax.ppermute(x, SPACE, [(i, to(i)) for i in range(count)])  18.6 us
    ppermute x20, starting transfers between devices, send(): return lax.ppermute(x, SPACE, [(i, to(i)) for i in range(count)])  17 us
    ppermute x2, starting transfers between devices, chips(): lax.ppermute(x, SPACE, [(i, across(i)) for i in range(count) if 0 <= acro...  5.43 us
    pallas_call x4, Pallas kernels, gene_sums(): pl.pallas_call(functools.partial(gene_kernel, step=1024, shift=shift), in...  4.65 us
    unnamed x14, local copies, waits for them, and re-layouts  4.41 us
    ppermute x2, waiting for transfers between devices, chips(): lax.ppermute(x, SPACE, [(i, across(i)) for i in range(count) if 0 <= acro...  3.6 us
    pallas_call x2, Pallas kernels, cast_counts(): pl.pallas_call(functools.partial(cast_kernel, turn=turn), in_specs=[pl.Bl...  1.19 us
  transfers between devices with their start and end apart: 22, of which 7 were waited for; matrix products, arithmetic and copies ran while one was open for 1% of the time, Pallas kernels for 11%

profile of v6, /device:TPU:17, one launch (start us, length us, event | category | flops | bytes accessed | tf_op | source)
XLA Modules:
  0.0 58.3 jit_solution(6502472359559891436)
XLA Ops:
  0.6 0.7 %collective-permute-start = (f32[32,2048]{1,0:T(8,128)}, f32[32,2048]{1,0:T(8,128)S(1)}, u32[]{:S(2)}, u32[]{:S(2)}) collective-permute-start(f32[32,2048]{1,0:T(8,128)} %values_ref.3), channel_id=1, source_target_pairs={{0,1},{1,0},{2,3},{3,2},{4,5},{5,4},{6,7},{7,6},{8,9},{9,8},{10,11... | collective-permute-start | bytes 786440 | tf_op jit(solution)/shard_map/ppermute | solution.py:167
  1.4 0.9 %copy-done.1 = f32[32,2048]{1,0:T(8,128)S(1)} copy-done((f32[32,2048]{1,0:T(8,128)S(1)}, f32[32,2048]{1,0:T(8,128)}, u32[]{:S(2)}) %copy-start.1) | copy-done | bytes 262168
  2.4 3.2 %collective-permute-start.3 = (s16[32,2048]{1,0:T(8,128)(2,1)S(1)}, s16[32,2048]{1,0:T(8,128)(2,1)S(1)}, u32[]{:S(2)}, u32[]{:S(2)}) collective-permute-start(s16[32,2048]{1,0:T(8,128)(2,1)S(1)} %shard_map.79), channel_id=1, source_target_pairs={{1,2},{2,1},{3,4},{4,3},{5,6},{6,5},{7,8},{8,7},{9,10},{10,9},{11,... | collective-permute-start | bytes 393224 | tf_op jit(solution)/shard_map/ppermute | solution.py:173
  5.5 0.4 collective-permute-start.1
  6.0 0.1 collective-permute-start.2
  6.1 3.4 %copy-done = s32[64,32768]{1,0:T(8,128)S(1)} copy-done((s32[64,32768]{1,0:T(8,128)S(1)}, s32[64,32768]{1,0:T(8,128)}, u32[]{:S(2)}) %copy-start) | copy-done | bytes 8388632
  9.5 0.6 %shard_map.82 = bf16[4,2,64,2048]{3,2,1,0:T(8,128)(2,1)S(1)} custom-call(s32[64,32768]{1,0:T(8,128)S(1)} %copy-done), custom_call_target="tpu_custom_call" | custom-call | flops 2097152 | bytes 6291456 | tf_op jit(solution)/shard_map/pallas_call | solution.py:39
  10.1 0.0 collective-permute-done.2
  10.1 0.0 collective-permute-done.1.other_w
  10.1 0.1 copy-done.4
  10.2 0.0 copy-done.6
  10.2 0.2 shard_map.78
  10.4 0.0 collective-permute-done.near_ref
  10.4 0.0 copy-done.2
  10.4 0.2 shard_map.77
  10.7 0.0 collective-permute-done.3.far_ref
  10.7 0.0 copy-done.3
  10.7 0.3 shard_map.80
  10.9 0.4 collective-permute-start.5
  11.4 0.9 %collective-permute-start.4 = (bf16[32,2048]{1,0:T(8,128)(2,1)S(1)}, bf16[32,2048]{1,0:T(8,128)(2,1)S(1)}, u32[]{:S(2)}, u32[]{:S(2)}) collective-permute-start(bf16[32,2048]{1,0:T(8,128)(2,1)S(1)} %get-tuple-element.33.own_f), channel_id=1, source_target_pairs={{0,2},{1,3},{2,0},{3,1},{4,6},{5,7},{6,4},{7,5},{8,10},{9,11},{10,... | collective-permute-start | bytes 393224 | tf_op jit(solution)/shard_map/ppermute | solution.py:167
  12.3 0.1 collective-permute-start.11
  12.4 1.3 %collective-permute-start.6 = (bf16[32,2048]{1,0:T(8,128)(2,1)S(1)}, bf16[32,2048]{1,0:T(8,128)(2,1)S(1)}, u32[]{:S(2)}, u32[]{:S(2)}) collective-permute-start(bf16[32,2048]{1,0:T(8,128)(2,1)S(1)} %get-tuple-element.33.own_f), channel_id=1, source_target_pairs={{0,4},{1,5},{2,6},{3,7},{4,0},{5,1},{6,2},{7,3},{8,12},{9,13},{10,... | collective-permute-start | bytes 393224 | tf_op jit(solution)/shard_map/ppermute | solution.py:167
  13.7 2.7 %collective-permute-done.4.other_f = bf16[32,2048]{1,0:T(8,128)(2,1)S(1)} collective-permute-done((bf16[32,2048]{1,0:T(8,128)(2,1)S(1)}, bf16[32,2048]{1,0:T(8,128)(2,1)S(1)}, u32[]{:S(2)}, u32[]{:S(2)}) %collective-permute-start.4) | collective-permute-done | bytes 131104 | tf_op jit(solution)/shard_map/ppermute | solution.py:167
  16.4 1.3 %collective-permute-start.7 = (bf16[32,2048]{1,0:T(8,128)(2,1)S(1)}, bf16[32,2048]{1,0:T(8,128)(2,1)S(1)}, u32[]{:S(2)}, u32[]{:S(2)}) collective-permute-start(bf16[32,2048]{1,0:T(8,128)(2,1)S(1)} %collective-permute-done.4.other_f), channel_id=1, source_target_pairs={{0,4},{1,5},{2,6},{3,7},{4,0},{5,1},{6,2},{7,3},{8,12},{9,13},{10,... | collective-permute-start | bytes 393224 | tf_op jit(solution)/shard_map/ppermute | solution.py:167
  17.6 0.6 %shard_map.81.keep_ref = bf16[4,2,64,2048]{3,2,1,0:T(8,128)(2,1)S(1)} custom-call(s32[64,32768]{1,0:T(8,128)S(1)} %copy-done), custom_call_target="tpu_custom_call" | custom-call | flops 2097152 | bytes 6291456 | tf_op jit(solution)/shard_map/pallas_call | solution.py:39
  18.3 0.1 collective-permute-start.15
  18.3 0.0 collective-permute-done.5.came_ref
  18.3 1.2 %shard_map.83 = (f32[32,2048]{1,0:T(8,128)S(1)}, f32[32,2048]{1,0:T(8,128)S(1)}, f32[32,128]{1,0:T(8,128)S(1)}) custom-call(bf16[32,2048]{1,0:T(8,128)(2,1)S(1)} %get-tuple-element.33.own_f, bf16[32,2048]{1,0:T(8,128)(2,1)S(1)} %collective-permute-done.4.other_f, bf16[4,2,64,2048]{3,2,1,0:T(8,128)(2,1)S(1)} %shard_map.81.keep_ref, ...), custom_call_target="tpu_custom_call" | custom-call | flops 100663296 | bytes 1572864 | tf_op jit(solution)/shard_map/pallas_call | solution.py:138
  19.5 0.0 collective-permute-done.11.own_f
  19.5 0.5 collective-permute-start.12
  20.1 0.0 collective-permute-done.6.own_f
  20.1 2.2 %collective-permute-done.7.other_f = bf16[32,2048]{1,0:T(8,128)(2,1)S(1)} collective-permute-done((bf16[32,2048]{1,0:T(8,128)(2,1)S(1)}, bf16[32,2048]{1,0:T(8,128)(2,1)S(1)}, u32[]{:S(2)}, u32[]{:S(2)}) %collective-permute-start.7) | collective-permute-done | bytes 131104 | tf_op jit(solution)/shard_map/ppermute | solution.py:167
  22.2 1.2 %shard_map.84 = (bf16[32,2048]{1,0:T(8,128)(2,1)S(1)}, bf16[32,2048]{1,0:T(8,128)(2,1)S(1)}, f32[32,128]{1,0:T(8,128)S(1)}) custom-call(bf16[32,2048]{1,0:T(8,128)(2,1)S(1)} %collective-permute-done.6.own_f, bf16[32,2048]{1,0:T(8,128)(2,1)S(1)} %collective-permute-done.7.other_f, bf16[4,2,64,2048]{3,2,1,0:T(8,128)(2,1)S(1)} %shard_map.81.keep_ref, ...), custom_call_target="tpu_custom_call" | custom-call | flops 100663296 | bytes 1572864 | tf_op jit(solution)/shard_map/pallas_call | solution.py:138
  23.4 2.2 %collective-permute-start.9 = (bf16[32,2048]{1,0:T(8,128)(2,1)S(1)}, bf16[32,2048]{1,0:T(8,128)(2,1)S(1)}, u32[]{:S(2)}, u32[]{:S(2)}) collective-permute-start(bf16[32,2048]{1,0:T(8,128)(2,1)S(1)} %get-tuple-element.40), channel_id=1, source_target_pairs={{0,4},{1,5},{2,6},{3,7},{4,0},{5,1},{6,2},{7,3},{8,12},{9,13},{10,... | collective-permute-start | bytes 393224 | tf_op jit(solution)/shard_map/ppermute | solution.py:167
  25.6 0.0 collective-permute-done.15.own_f
  25.6 1.1 %collective-permute-start.16 = (bf16[32,2048]{1,0:T(8,128)(2,1)S(1)}, bf16[32,2048]{1,0:T(8,128)(2,1)S(1)}, u32[]{:S(2)}, u32[]{:S(2)}) collective-permute-start(bf16[32,2048]{1,0:T(8,128)(2,1)S(1)} %collective-permute-done.15.own_f), channel_id=1, source_target_pairs={{0,2},{1,3},{2,0},{3,1},{4,6},{5,7},{6,4},{7,5},{8,10},{9,11},{10,... | collective-permute-start | bytes 393224 | tf_op jit(solution)/shard_map/ppermute | solution.py:167
  26.8 1.3 %collective-permute-start.8 = (bf16[32,2048]{1,0:T(8,128)(2,1)S(1)}, bf16[32,2048]{1,0:T(8,128)(2,1)S(1)}, u32[]{:S(2)}, u32[]{:S(2)}) collective-permute-start(bf16[32,2048]{1,0:T(8,128)(2,1)S(1)} %get-tuple-element.38), channel_id=1, source_target_pairs={{0,4},{1,5},{2,6},{3,7},{4,0},{5,1},{6,2},{7,3},{8,12},{9,13},{10,... | collective-permute-start | bytes 393224 | tf_op jit(solution)/shard_map/ppermute | solution.py:167
  28.0 0.0 collective-permute-done.12.other_f
  28.1 1.2 %shard_map.85 = (f32[32,2048]{1,0:T(8,128)S(1)}, bf16[32,2048]{1,0:T(8,128)(2,1)S(1)}, f32[32,128]{1,0:T(8,128)S(1)}) custom-call(bf16[32,2048]{1,0:T(8,128)(2,1)S(1)} %collective-permute-done.11.own_f, bf16[32,2048]{1,0:T(8,128)(2,1)S(1)} %collective-permute-done.12.other_f, bf16[4,2,64,2048]{3,2,1,0:T(8,128)(2,1)S(1)} %shard_map.81.keep_ref, ...), custom_call_target="tpu_custom_call" | custom-call | flops 100663296 | bytes 1572864 | tf_op jit(solution)/shard_map/pallas_call | solution.py:138
  29.2 0.7 %collective-permute-start.13 = (bf16[32,2048]{1,0:T(8,128)(2,1)S(1)}, bf16[32,2048]{1,0:T(8,128)(2,1)S(1)}, u32[]{:S(2)}, u32[]{:S(2)}) collective-permute-start(bf16[32,2048]{1,0:T(8,128)(2,1)S(1)} %get-tuple-element.44), channel_id=1, source_target_pairs={{0,2},{1,3},{2,0},{3,1},{4,6},{5,7},{6,4},{7,5},{8,10},{9,11},{10,... | collective-permute-start | bytes 393224 | tf_op jit(solution)/shard_map/ppermute | solution.py:167
  30.0 0.0 collective-permute-done.9
  30.0 0.9 %collective-permute-start.10 = (bf16[32,2048]{1,0:T(8,128)(2,1)S(1)}, bf16[32,2048]{1,0:T(8,128)(2,1)S(1)}, u32[]{:S(2)}, u32[]{:S(2)}) collective-permute-start(bf16[32,2048]{1,0:T(8,128)(2,1)S(1)} %add_convert_fusion.2), channel_id=1, source_target_pairs={{0,2},{1,3},{2,0},{3,1},{4,6},{5,7},{6,4},{7,5},{8,10},{9,11},{10,... | collective-permute-start | bytes 393224 | tf_op jit(solution)/shard_map/ppermute | solution.py:167
  30.9 0.0 collective-permute-done.16.other_f
  30.9 1.2 %shard_map.86 = (f32[32,2048]{1,0:T(8,128)S(1)}, bf16[32,2048]{1,0:T(8,128)(2,1)S(1)}, f32[32,128]{1,0:T(8,128)S(1)}) custom-call(bf16[32,2048]{1,0:T(8,128)(2,1)S(1)} %collective-permute-done.15.own_f, bf16[32,2048]{1,0:T(8,128)(2,1)S(1)} %collective-permute-done.16.other_f, bf16[4,2,64,2048]{3,2,1,0:T(8,128)(2,1)S(1)} %shard_map.81.keep_ref, ...), custom_call_target="tpu_custom_call" | custom-call | flops 100663296 | bytes 1572864 | tf_op jit(solution)/shard_map/pallas_call | solution.py:138
  32.0 0.7 %collective-permute-start.17 = (bf16[32,2048]{1,0:T(8,128)(2,1)S(1)}, bf16[32,2048]{1,0:T(8,128)(2,1)S(1)}, u32[]{:S(2)}, u32[]{:S(2)}) collective-permute-start(bf16[32,2048]{1,0:T(8,128)(2,1)S(1)} %get-tuple-element.47), channel_id=1, source_target_pairs={{0,2},{1,3},{2,0},{3,1},{4,6},{5,7},{6,4},{7,5},{8,10},{9,11},{10,... | collective-permute-start | bytes 393224 | tf_op jit(solution)/shard_map/ppermute | solution.py:167
  32.8 0.6 %collective-permute-done.13 = bf16[32,2048]{1,0:T(8,128)(2,1)S(1)} collective-permute-done((bf16[32,2048]{1,0:T(8,128)(2,1)S(1)}, bf16[32,2048]{1,0:T(8,128)(2,1)S(1)}, u32[]{:S(2)}, u32[]{:S(2)}) %collective-permute-start.13) | collective-permute-done | bytes 131104 | tf_op jit(solution)/shard_map/ppermute | solution.py:167
  33.4 1.2 %collective-permute-start.14 = (bf16[32,2048]{1,0:T(8,128)(2,1)S(1)}, bf16[32,2048]{1,0:T(8,128)(2,1)S(1)}, u32[]{:S(2)}, u32[]{:S(2)}) collective-permute-start(bf16[32,2048]{1,0:T(8,128)(2,1)S(1)} %add_convert_fusion.1), channel_id=1, source_target_pairs={{0,8},{1,9},{2,10},{3,11},{4,12},{5,13},{6,14},{7,15},{8,0},{9,1},... | collective-permute-start | bytes 393224 | tf_op jit(solution)/shard_map/ppermute | solution.py:167
  34.6 3.5 %collective-permute-done.17 = bf16[32,2048]{1,0:T(8,128)(2,1)S(1)} collective-permute-done((bf16[32,2048]{1,0:T(8,128)(2,1)S(1)}, bf16[32,2048]{1,0:T(8,128)(2,1)S(1)}, u32[]{:S(2)}, u32[]{:S(2)}) %collective-permute-start.17) | collective-permute-done | bytes 131104 | tf_op jit(solution)/shard_map/ppermute | solution.py:167
  38.1 0.2 collective-permute-start.18
  38.3 0.0 collective-permute-done.8
  38.3 0.0 collective-permute-done.10
  38.3 0.0 collective-permute-done.14
  38.3 9.2 %collective-permute-done.18 = bf16[32,2048]{1,0:T(8,128)(2,1)S(1)} collective-permute-done((bf16[32,2048]{1,0:T(8,128)(2,1)S(1)}, bf16[32,2048]{1,0:T(8,128)(2,1)S(1)}, u32[]{:S(2)}, u32[]{:S(2)}) %collective-permute-start.18) | collective-permute-done | bytes 131104 | tf_op jit(solution)/shard_map/ppermute | solution.py:167
  47.5 0.1 fusion.1
  47.6 0.1 slice.6
  47.7 2.2 %collective-permute-start.19 = (f32[32,64]{1,0:T(8,128)S(1)}, f32[32,64]{1,0:T(8,128)S(1)}, u32[]{:S(2)}, u32[]{:S(2)}) collective-permute-start(f32[32,64]{1,0:T(8,128)S(1)} %slice.6), channel_id=1, source_target_pairs={{0,1},{1,0},{2,3},{3,2},{4,5},{5,4},{6,7},{7,6},{8,9},{9,8},{10,11... | collective-permute-start | bytes 24584 | tf_op jit(solution)/shard_map/ppermute | solution.py:167
  49.9 2.2 %collective-permute-start.21 = (bf16[32,2048]{1,0:T(8,128)(2,1)S(1)}, bf16[32,2048]{1,0:T(8,128)(2,1)S(1)}, u32[]{:S(2)}, u32[]{:S(2)}) collective-permute-start(bf16[32,2048]{1,0:T(8,128)(2,1)S(1)} %get-tuple-element.53), channel_id=1, source_target_pairs={{1,2},{2,1},{3,4},{4,3},{5,6},{6,5},{7,8},{8,7},{9,10},{10,9},{11,... | collective-permute-start | bytes 393224 | tf_op jit(solution)/shard_map/ppermute | solution.py:173
  52.1 0.0 collective-permute-done.19
  52.1 0.6 %collective-permute-start.20 = (bf16[32,2048]{1,0:T(8,128)(2,1)S(1)}, bf16[32,2048]{1,0:T(8,128)(2,1)S(1)}, u32[]{:S(2)}, u32[]{:S(2)}) collective-permute-start(bf16[32,2048]{1,0:T(8,128)(2,1)S(1)} %get-tuple-element.53), channel_id=1, source_target_pairs={{0,1},{1,0},{2,3},{3,2},{4,5},{5,4},{6,7},{7,6},{8,9},{9,8},{10,11... | collective-permute-start | bytes 393224 | tf_op jit(solution)/shard_map/ppermute | solution.py:167
  52.7 0.6 %fusion = f32[32,64]{1,0:T(8,128)} fusion(f32[32,64]{1,0:T(8,128)S(1)} %collective-permute-done.19, f32[32,128]{1,0:T(8,128)S(1)} %add_add_fusion), kind=kLoop, calls=%fused_computation.5 | loop fusion | flops 4096 | bytes 24576 | tf_op jit(solution)/shard_map/div | solution.py:248
  53.3 0.4 collective-permute-done.20.near_ref
  53.7 0.2 shard_map.87
  53.9 3.6 %collective-permute-done.21.far_ref = bf16[32,2048]{1,0:T(8,128)(2,1)S(1)} collective-permute-done((bf16[32,2048]{1,0:T(8,128)(2,1)S(1)}, bf16[32,2048]{1,0:T(8,128)(2,1)S(1)}, u32[]{:S(2)}, u32[]{:S(2)}) %collective-permute-start.21) | collective-permute-done | bytes 131104 | tf_op jit(solution)/shard_map/ppermute | solution.py:173
  57.5 0.7 %shard_map.88 = f32[32,2048]{1,0:T(8,128)} custom-call(f32[32,2048]{1,0:T(8,128)S(1)} %get-tuple-element.54.base_ref, bf16[32,2048]{1,0:T(8,128)(2,1)S(1)} %collective-permute-done.21.far_ref, f32[32,128]{1,0:T(8,128)S(1)} %get-tuple-element.55.tile_ref), custom_call_target="tpu_custom_call" | custom-call | flops 655360 | bytes 786432 | tf_op jit(solution)/shard_map/pallas_call | solution.py:240
  (13 shorter events, 0.1 us)
Async XLA Ops:
  0.6 9.8 %collective-permute-start = (f32[32,2048]{1,0:T(8,128)}, f32[32,2048]{1,0:T(8,128)S(1)}, u32[]{:S(2)}, u32[]{:S(2)}) collective-permute-start(f32[32,2048]{1,0:T(8,128)} %values_ref.3), channel_id=1, source_target_pairs={{0,1},{1,0},{2,3},{3,2},{4,5},{5,4},{6,7},{7,6},{8,9},{9,8},{10,11... | collective-permute-start | bytes 786440 | tf_op jit(solution)/shard_map/ppermute | solution.py:167
  1.4 0.9 %copy-start.1 = (f32[32,2048]{1,0:T(8,128)S(1)}, f32[32,2048]{1,0:T(8,128)}, u32[]{:S(2)}) copy-start(f32[32,2048]{1,0:T(8,128)} %values_ref.3) | copy-start | bytes 786436
  2.3 8.1 %copy-start.2 = (f32[32,2048]{1,0:T(8,128)S(1)}, f32[32,2048]{1,0:T(8,128)}, u32[]{:S(2)}) copy-start(f32[32,2048]{1,0:T(8,128)} %values_ref.3) | copy-start | bytes 786436
  2.3 8.3 %copy-start.3 = (s32[32768]{0:T(1024)S(1)}, s32[32768]{0:T(1024)}, u32[]{:S(2)}) copy-start(s32[32768]{0:T(1024)} %param.11) | copy-start | bytes 393220
  2.4 8.3 %collective-permute-start.3 = (s16[32,2048]{1,0:T(8,128)(2,1)S(1)}, s16[32,2048]{1,0:T(8,128)(2,1)S(1)}, u32[]{:S(2)}, u32[]{:S(2)}) collective-permute-start(s16[32,2048]{1,0:T(8,128)(2,1)S(1)} %shard_map.79), channel_id=1, source_target_pairs={{1,2},{2,1},{3,4},{4,3},{5,6},{6,5},{7,8},{8,7},{9,10},{10,9},{11,... | collective-permute-start | bytes 393224 | tf_op jit(solution)/shard_map/ppermute | solution.py:173
  5.5 4.6 %collective-permute-start.1 = (bf16[32,64]{1,0:T(8,128)(2,1)}, bf16[32,64]{1,0:T(8,128)(2,1)S(1)}, u32[]{:S(2)}, u32[]{:S(2)}) collective-permute-start(bf16[32,64]{1,0:T(8,128)(2,1)} %own_w.1), channel_id=1, source_target_pairs={{0,1},{1,0},{2,3},{3,2},{4,5},{5,4},{6,7},{7,6},{8,9},{9,8},{10,11... | collective-permute-start | bytes 12296 | tf_op jit(solution)/shard_map/ppermute | solution.py:167
  6.0 4.1 %collective-permute-start.2 = (f32[64]{0:T(128)}, f32[64]{0:T(128)S(1)}, u32[]{:S(2)}, u32[]{:S(2)}) collective-permute-start(f32[64]{0:T(128)} %param.9), channel_id=1, source_target_pairs={{0,1},{1,0},{2,3},{3,2},{4,5},{5,4},{6,7},{7,6},{8,9},{9,8},{10,11... | collective-permute-start | bytes 776 | tf_op jit(solution)/shard_map/ppermute | solution.py:167
  6.1 3.4 %copy-start = (s32[64,32768]{1,0:T(8,128)S(1)}, s32[64,32768]{1,0:T(8,128)}, u32[]{:S(2)}) copy-start(s32[64,32768]{1,0:T(8,128)} %counts_ref.3) | copy-start | bytes 25165828
  9.5 0.7 %copy-start.4 = (bf16[32,64]{1,0:T(8,128)(2,1)S(1)}, bf16[32,64]{1,0:T(8,128)(2,1)}, u32[]{:S(2)}) copy-start(bf16[32,64]{1,0:T(8,128)(2,1)} %own_w.1) | copy-start | bytes 12292
  9.5 0.7 %copy-start.6 = (f32[64]{0:T(128)S(1)}, f32[64]{0:T(128)}, u32[]{:S(2)}) copy-start(f32[64]{0:T(128)} %param.9) | copy-start | bytes 772
  9.5 0.9 %copy-start.5 = (f32[32]{0:T(128)S(1)}, f32[32]{0:T(128)}, u32[]{:S(2)}) copy-start(f32[32]{0:T(128)} %param.10) | copy-start | bytes 388
  10.9 7.4 %collective-permute-start.5 = (bf16[4,2,64,2048]{3,2,1,0:T(8,128)(2,1)S(1)}, bf16[4,2,64,2048]{3,2,1,0:T(8,128)(2,1)S(1)}, u32[]{:S(2)}, u32[]{:S(2)}) collective-permute-start(bf16[4,2,64,2048]{3,2,1,0:T(8,128)(2,1)S(1)} %shard_map.82), channel_id=1, source_target_pairs={{0,1},{1,0},{2,3},{3,2},{4,5},{5,4},{6,7},{7,6},{8,9},{9,8},{10,11... | collective-permute-start | bytes 6291464 | tf_op jit(solution)/shard_map/ppermute | solution.py:167
  11.4 5.0 %collective-permute-start.4 = (bf16[32,2048]{1,0:T(8,128)(2,1)S(1)}, bf16[32,2048]{1,0:T(8,128)(2,1)S(1)}, u32[]{:S(2)}, u32[]{:S(2)}) collective-permute-start(bf16[32,2048]{1,0:T(8,128)(2,1)S(1)} %get-tuple-element.33.own_f), channel_id=1, source_target_pairs={{0,2},{1,3},{2,0},{3,1},{4,6},{5,7},{6,4},{7,5},{8,10},{9,11},{10,... | collective-permute-start | bytes 393224 | tf_op jit(solution)/shard_map/ppermute | solution.py:167
  12.3 7.2 %collective-permute-start.11 = (bf16[32,2048]{1,0:T(8,128)(2,1)S(1)}, bf16[32,2048]{1,0:T(8,128)(2,1)S(1)}, u32[]{:S(2)}, u32[]{:S(2)}) collective-permute-start(bf16[32,2048]{1,0:T(8,128)(2,1)S(1)} %get-tuple-element.33.own_f), channel_id=1, source_target_pairs={{0,8},{1,9},{2,10},{3,11},{4,12},{5,13},{6,14},{7,15},{8,0},{9,1},... | collective-permute-start | bytes 393224 | tf_op jit(solution)/shard_map/ppermute | solution.py:167
  12.4 7.7 %collective-permute-start.6 = (bf16[32,2048]{1,0:T(8,128)(2,1)S(1)}, bf16[32,2048]{1,0:T(8,128)(2,1)S(1)}, u32[]{:S(2)}, u32[]{:S(2)}) collective-permute-start(bf16[32,2048]{1,0:T(8,128)(2,1)S(1)} %get-tuple-element.33.own_f), channel_id=1, source_target_pairs={{0,4},{1,5},{2,6},{3,7},{4,0},{5,1},{6,2},{7,3},{8,12},{9,13},{10,... | collective-permute-start | bytes 393224 | tf_op jit(solution)/shard_map/ppermute | solution.py:167
  16.4 5.9 %collective-permute-start.7 = (bf16[32,2048]{1,0:T(8,128)(2,1)S(1)}, bf16[32,2048]{1,0:T(8,128)(2,1)S(1)}, u32[]{:S(2)}, u32[]{:S(2)}) collective-permute-start(bf16[32,2048]{1,0:T(8,128)(2,1)S(1)} %collective-permute-done.4.other_f), channel_id=1, source_target_pairs={{0,4},{1,5},{2,6},{3,7},{4,0},{5,1},{6,2},{7,3},{8,12},{9,13},{10,... | collective-permute-start | bytes 393224 | tf_op jit(solution)/shard_map/ppermute | solution.py:167
  18.3 7.4 %collective-permute-start.15 = (bf16[32,2048]{1,0:T(8,128)(2,1)S(1)}, bf16[32,2048]{1,0:T(8,128)(2,1)S(1)}, u32[]{:S(2)}, u32[]{:S(2)}) collective-permute-start(bf16[32,2048]{1,0:T(8,128)(2,1)S(1)} %get-tuple-element.33.own_f), channel_id=1, source_target_pairs={{0,12},{1,13},{2,14},{3,15},{4,8},{5,9},{6,10},{7,11},{8,4},{9,5},... | collective-permute-start | bytes 393224 | tf_op jit(solution)/shard_map/ppermute | solution.py:167
  19.5 8.5 %collective-permute-start.12 = (bf16[32,2048]{1,0:T(8,128)(2,1)S(1)}, bf16[32,2048]{1,0:T(8,128)(2,1)S(1)}, u32[]{:S(2)}, u32[]{:S(2)}) collective-permute-start(bf16[32,2048]{1,0:T(8,128)(2,1)S(1)} %collective-permute-done.11.own_f), channel_id=1, source_target_pairs={{0,2},{1,3},{2,0},{3,1},{4,6},{5,7},{6,4},{7,5},{8,10},{9,11},{10,... | collective-permute-start | bytes 393224 | tf_op jit(solution)/shard_map/ppermute | solution.py:167
  23.4 6.5 %collective-permute-start.9 = (bf16[32,2048]{1,0:T(8,128)(2,1)S(1)}, bf16[32,2048]{1,0:T(8,128)(2,1)S(1)}, u32[]{:S(2)}, u32[]{:S(2)}) collective-permute-start(bf16[32,2048]{1,0:T(8,128)(2,1)S(1)} %get-tuple-element.40), channel_id=1, source_target_pairs={{0,4},{1,5},{2,6},{3,7},{4,0},{5,1},{6,2},{7,3},{8,12},{9,13},{10,... | collective-permute-start | bytes 393224 | tf_op jit(solution)/shard_map/ppermute | solution.py:167
  25.6 5.2 %collective-permute-start.16 = (bf16[32,2048]{1,0:T(8,128)(2,1)S(1)}, bf16[32,2048]{1,0:T(8,128)(2,1)S(1)}, u32[]{:S(2)}, u32[]{:S(2)}) collective-permute-start(bf16[32,2048]{1,0:T(8,128)(2,1)S(1)} %collective-permute-done.15.own_f), channel_id=1, source_target_pairs={{0,2},{1,3},{2,0},{3,1},{4,6},{5,7},{6,4},{7,5},{8,10},{9,11},{10,... | collective-permute-start | bytes 393224 | tf_op jit(solution)/shard_map/ppermute | solution.py:167
  26.8 11.5 %collective-permute-start.8 = (bf16[32,2048]{1,0:T(8,128)(2,1)S(1)}, bf16[32,2048]{1,0:T(8,128)(2,1)S(1)}, u32[]{:S(2)}, u32[]{:S(2)}) collective-permute-start(bf16[32,2048]{1,0:T(8,128)(2,1)S(1)} %get-tuple-element.38), channel_id=1, source_target_pairs={{0,4},{1,5},{2,6},{3,7},{4,0},{5,1},{6,2},{7,3},{8,12},{9,13},{10,... | collective-permute-start | bytes 393224 | tf_op jit(solution)/shard_map/ppermute | solution.py:167
  29.2 4.2 %collective-permute-start.13 = (bf16[32,2048]{1,0:T(8,128)(2,1)S(1)}, bf16[32,2048]{1,0:T(8,128)(2,1)S(1)}, u32[]{:S(2)}, u32[]{:S(2)}) collective-permute-start(bf16[32,2048]{1,0:T(8,128)(2,1)S(1)} %get-tuple-element.44), channel_id=1, source_target_pairs={{0,2},{1,3},{2,0},{3,1},{4,6},{5,7},{6,4},{7,5},{8,10},{9,11},{10,... | collective-permute-start | bytes 393224 | tf_op jit(solution)/shard_map/ppermute | solution.py:167
  30.0 8.3 %collective-permute-start.10 = (bf16[32,2048]{1,0:T(8,128)(2,1)S(1)}, bf16[32,2048]{1,0:T(8,128)(2,1)S(1)}, u32[]{:S(2)}, u32[]{:S(2)}) collective-permute-start(bf16[32,2048]{1,0:T(8,128)(2,1)S(1)} %add_convert_fusion.2), channel_id=1, source_target_pairs={{0,2},{1,3},{2,0},{3,1},{4,6},{5,7},{6,4},{7,5},{8,10},{9,11},{10,... | collective-permute-start | bytes 393224 | tf_op jit(solution)/shard_map/ppermute | solution.py:167
  32.0 6.0 %collective-permute-start.17 = (bf16[32,2048]{1,0:T(8,128)(2,1)S(1)}, bf16[32,2048]{1,0:T(8,128)(2,1)S(1)}, u32[]{:S(2)}, u32[]{:S(2)}) collective-permute-start(bf16[32,2048]{1,0:T(8,128)(2,1)S(1)} %get-tuple-element.47), channel_id=1, source_target_pairs={{0,2},{1,3},{2,0},{3,1},{4,6},{5,7},{6,4},{7,5},{8,10},{9,11},{10,... | collective-permute-start | bytes 393224 | tf_op jit(solution)/shard_map/ppermute | solution.py:167
  33.4 4.9 %collective-permute-start.14 = (bf16[32,2048]{1,0:T(8,128)(2,1)S(1)}, bf16[32,2048]{1,0:T(8,128)(2,1)S(1)}, u32[]{:S(2)}, u32[]{:S(2)}) collective-permute-start(bf16[32,2048]{1,0:T(8,128)(2,1)S(1)} %add_convert_fusion.1), channel_id=1, source_target_pairs={{0,8},{1,9},{2,10},{3,11},{4,12},{5,13},{6,14},{7,15},{8,0},{9,1},... | collective-permute-start | bytes 393224 | tf_op jit(solution)/shard_map/ppermute | solution.py:167
  38.1 9.4 %collective-permute-start.18 = (bf16[32,2048]{1,0:T(8,128)(2,1)S(1)}, bf16[32,2048]{1,0:T(8,128)(2,1)S(1)}, u32[]{:S(2)}, u32[]{:S(2)}) collective-permute-start(bf16[32,2048]{1,0:T(8,128)(2,1)S(1)} %add_convert_fusion), channel_id=1, source_target_pairs={{0,12},{1,13},{2,14},{3,15},{4,8},{5,9},{6,10},{7,11},{8,4},{9,5},... | collective-permute-start | bytes 393224 | tf_op jit(solution)/shard_map/ppermute | solution.py:167
  47.7 4.4 %collective-permute-start.19 = (f32[32,64]{1,0:T(8,128)S(1)}, f32[32,64]{1,0:T(8,128)S(1)}, u32[]{:S(2)}, u32[]{:S(2)}) collective-permute-start(f32[32,64]{1,0:T(8,128)S(1)} %slice.6), channel_id=1, source_target_pairs={{0,1},{1,0},{2,3},{3,2},{4,5},{5,4},{6,7},{7,6},{8,9},{9,8},{10,11... | collective-permute-start | bytes 24584 | tf_op jit(solution)/shard_map/ppermute | solution.py:167
  49.9 7.7 %collective-permute-start.21 = (bf16[32,2048]{1,0:T(8,128)(2,1)S(1)}, bf16[32,2048]{1,0:T(8,128)(2,1)S(1)}, u32[]{:S(2)}, u32[]{:S(2)}) collective-permute-start(bf16[32,2048]{1,0:T(8,128)(2,1)S(1)} %get-tuple-element.53), channel_id=1, source_target_pairs={{1,2},{2,1},{3,4},{4,3},{5,6},{6,5},{7,8},{8,7},{9,10},{10,9},{11,... | collective-permute-start | bytes 393224 | tf_op jit(solution)/shard_map/ppermute | solution.py:173
  52.1 1.6 %collective-permute-start.20 = (bf16[32,2048]{1,0:T(8,128)(2,1)S(1)}, bf16[32,2048]{1,0:T(8,128)(2,1)S(1)}, u32[]{:S(2)}, u32[]{:S(2)}) collective-permute-start(bf16[32,2048]{1,0:T(8,128)(2,1)S(1)} %get-tuple-element.53), channel_id=1, source_target_pairs={{0,1},{1,0},{2,3},{3,2},{4,5},{5,4},{6,7},{7,6},{8,9},{9,8},{10,11... | collective-permute-start | bytes 393224 | tf_op jit(solution)/shard_map/ppermute | solution.py:167
